TPU v7x, 512 devices: a whole 4x8x8 slice. The times are simulated.
512 devices in a mesh: branch: 128 (over y, z, core), level: 4 (over x).
Axes of the slice: x: 4, y: 8, z: 8, core: 2. Of those that a mesh axis runs over, the one named last changes fastest.
Arguments:
- basis: bfloat16 [512, 64, 4096], P('branch', None, 'level'), may hold values from -0.09375 to 0.09375
- bottom_transfer: bfloat16 [512, 4096], P('branch'), may hold values from -0.75 to 0.75
- bottom_rank: int32 [512], P('branch'), may hold values from 16 to 64
- upper_transfer: bfloat16 [254, 4096], replicated, may hold values from -0.75 to 0.75
- upper_rank: int32 [254], replicated, may hold values from 16 to 64
- couplings: bfloat16 [49152, 4096], P(('branch', 'level')), may hold values from -6 to 6
- row_cluster: int32 [49152], P(('branch', 'level')), may hold values from 0 to 3
- column_owner: int32 [49152, 1], P(('branch', 'level')), may hold values from 0 to 127; in each aligned block of 96 rows (0 to 95, 96 to 191, ...) at most 2 rows name the same one
- column_cluster: int32 [49152], P(('branch', 'level')), may hold values from 0 to 3
Outputs:
- upper_grams: float32 [128, 4096], P('branch')
- projected: float32 [49152, 4096], P(('branch', 'level'))
Inputs may be any that keep to these rules, and one draw needn't show every extreme that they name: Among the 96 blocks of one device at most 2 have the same column_owner, and in every draw some owner is named by exactly 2 of them.
All inputs are finite; a program needn't handle non-finite values.
Results may differ from a plain program's by a relative error of at most 0.0052.
Values may be sent and summed in bfloat16 or wider, within the bound.
No kernel may reach another device: no remote copies, remote signals or barrier semaphores. Data moves between devices by JAX's collectives and lax.ppermute only.
A program may use at most 64 MiB of HBM per device.

v0:
```python
import jax
import jax.numpy as jnp
from jax import lax
from jax.sharding import PartitionSpec as P

HIGH = lax.Precision.HIGHEST


def from_partner(block, axis, apart):
    count = lax.axis_size(axis)
    route = []
    for low in range(count):
        high = low | 1 << apart
        if high != low and high < count:
            route += [(low, high), (high, low)]
    return lax.ppermute(block, axis, route)


def rank_mask(ranks, width):
    index = jnp.arange(width, dtype=jnp.int32)
    keep = (index[None, :] < ranks[:, None]).astype(jnp.float32)
    return keep[:, :, None] * keep[:, None, :]


def lift(grams, transfer, ranks):
    width = grams.shape[1]
    masked = grams * rank_mask(ranks, width)
    mats = transfer.astype(jnp.float32).reshape(-1, width, width)
    inner = jnp.einsum("nij,njk->nik", masked, mats, precision=HIGH)
    return jnp.einsum("nji,njk->nik", mats, inner, precision=HIGH)


def on_device(
    basis,
    bottom_transfer,
    bottom_rank,
    upper_transfer,
    upper_rank,
    couplings,
    row_cluster,
    column_owner,
    column_cluster,
):
    width = basis.shape[1]
    nodes = basis.shape[0]
    branches = lax.axis_size("branch")
    levels = branches.bit_length() - 1
    me_branch = lax.axis_index("branch")
    partial_sum = jnp.einsum("nip,njp->nij", basis, basis, preferred_element_type=jnp.float32)
    grams = lax.psum(partial_sum.reshape(nodes, width * width), "level").reshape(
        nodes, width, width
    )
    terms = lift(grams, bottom_transfer, bottom_rank)
    device_gram = jnp.sum(terms, axis=0)
    neighbour = (me_branch + 1) % branches
    crossed = jnp.bitwise_xor(me_branch, neighbour)
    target = sum(
        [(jnp.right_shift(crossed, height) > 0).astype(jnp.int32) for height in range(levels)]
    )
    picked = jnp.zeros_like(device_gram)
    current = device_gram
    for height in range(levels):
        count = branches >> height
        slot = 2 * branches - 2 * count + jnp.right_shift(me_branch, height)
        mats = lax.dynamic_slice_in_dim(upper_transfer, slot, 1, 0)
        ranks = lax.dynamic_slice_in_dim(upper_rank, slot, 1, 0)
        term = lift(current[None], mats, ranks)[0]
        current = term + from_partner(term, "branch", height)
        picked = jnp.where(target == height + 1, current, picked)
    upper_grams = picked.reshape(1, width * width)
    masked = (grams * rank_mask(bottom_rank, width)).astype(jnp.bfloat16)
    owners = column_owner[:, 0]
    blk = couplings.shape[0]
    every_masked = lax.all_gather(
        masked.reshape(nodes, width * width), "branch", axis=0, tiled=True
    )
    right = jnp.take(
        every_masked.reshape(-1, width, width), owners * nodes + column_cluster, axis=0
    )
    carried = jnp.einsum(
        "bij,bjk->bik",
        couplings.reshape(blk, width, width),
        right,
        preferred_element_type=jnp.float32,
    ).astype(jnp.bfloat16)
    left = jnp.take(masked, row_cluster, axis=0)
    projected = jnp.einsum("bij,bjk->bik", left, carried, preferred_element_type=jnp.float32)
    return (upper_grams, projected.reshape(blk, width * width))


def solution(mesh):
    placed = (
        P("branch", None, "level"),
        P("branch", None),
        P("branch"),
        P(),
        P(),
        P(("branch", "level"), None),
        P(("branch", "level")),
        P(("branch", "level"), None),
        P(("branch", "level")),
    )
    return jax.shard_map(
        on_device,
        mesh=mesh,
        in_specs=placed,
        out_specs=(P("branch", None), P(("branch", "level"), None)),
        check_vma=False,
    )
```

profile of v0, /device:TPU:1, one launch (start us, length us, event | category | flops | bytes accessed | tf_op | source)
XLA Modules:
  0.0 192.8 jit_solution(5854907021708066578)
XLA Ops:
  7.3 0.9 copy-done
  8.2 0.3 fusion.53
  8.5 0.7 reshape.338
  9.3 0.7 fusion.49
  10.0 55.9 %all-reduce.2.cloned.1.call-done = f32[4,4096]{1,0:T(4,128)} async-done(((f32[4,4096]{1,0:T(4,128)}), f32[4,4096]{1,0:T(4,128)}) %all-reduce.2.cloned.1.call-update) | async-done | bytes 65552 | tf_op jit(solution)/shard_map/psum | solution.py:50
  66.0 1.0 reshape.339
  67.2 1.5 fusion.12
  68.8 1.4 dynamic-slice_reduce_fusion
  70.3 0.7 fusion.52
  71.0 0.6 compare_convert_fusion.6
  71.7 0.3 fusion.10
  72.1 0.2 fusion.7
  72.3 0.2 fusion.54
  72.7 4.6 %collective-permute-start = (f32[64,64]{1,0:T(8,128)S(1)}, f32[64,64]{1,0:T(8,128)S(1)}, u32[]{:S(2)}, u32[]{:S(2)}) collective-permute-start(f32[64,64]{1,0:T(8,128)S(1)} %fusion.55), channel_id=1, source_target_pairs={{0,4},{4,0},{8,12},{12,8},{16,20},{20,16},{24,28},{28,24},{32,36},... | collective-permute-start | bytes 49160 | tf_op jit(solution)/shard_map/ppermute | solution.py:16
  77.3 0.6 compare_convert_fusion.5
  78.4 0.2 fusion.56
  78.6 3.3 %collective-permute-start.1 = (f32[64,64]{1,0:T(8,128)S(1)}, f32[64,64]{1,0:T(8,128)S(1)}, u32[]{:S(2)}, u32[]{:S(2)}) collective-permute-start(f32[64,64]{1,0:T(8,128)S(1)} %fusion.56), channel_id=1, source_target_pairs={{0,8},{8,0},{4,12},{12,4},{16,24},{24,16},{20,28},{28,20},{32,40},... | collective-permute-start | bytes 49160 | tf_op jit(solution)/shard_map/ppermute | solution.py:16
  81.9 0.6 compare_convert_fusion.4
  82.6 0.7 collective-permute-done.1
  83.5 0.2 fusion.57
  83.7 4.4 %collective-permute-start.2 = (f32[64,64]{1,0:T(8,128)S(1)}, f32[64,64]{1,0:T(8,128)S(1)}, u32[]{:S(2)}, u32[]{:S(2)}) collective-permute-start(f32[64,64]{1,0:T(8,128)S(1)} %fusion.57), channel_id=1, source_target_pairs={{0,16},{16,0},{4,20},{20,4},{8,24},{24,8},{12,28},{28,12},{32,48},... | collective-permute-start | bytes 49160 | tf_op jit(solution)/shard_map/ppermute | solution.py:16
  88.1 0.6 compare_convert_fusion.3
  88.7 0.6 collective-permute-done.2
  89.6 0.2 fusion.58
  89.8 8.3 %collective-permute-start.3 = (f32[64,64]{1,0:T(8,128)S(1)}, f32[64,64]{1,0:T(8,128)S(1)}, u32[]{:S(2)}, u32[]{:S(2)}) collective-permute-start(f32[64,64]{1,0:T(8,128)S(1)} %fusion.58), channel_id=1, source_target_pairs={{0,32},{32,0},{4,36},{36,4},{8,40},{40,8},{12,44},{44,12},{16,48},... | collective-permute-start | bytes 49160 | tf_op jit(solution)/shard_map/ppermute | solution.py:16
  98.1 0.7 compare_convert_fusion.2
  98.9 0.6 collective-permute-done.3
  99.6 0.2 fusion.59
  99.9 3.1 %collective-permute-start.4 = (f32[64,64]{1,0:T(8,128)S(1)}, f32[64,64]{1,0:T(8,128)S(1)}, u32[]{:S(2)}, u32[]{:S(2)}) collective-permute-start(f32[64,64]{1,0:T(8,128)S(1)} %fusion.59), channel_id=1, source_target_pairs={{0,64},{64,0},{4,68},{68,4},{8,72},{72,8},{12,76},{76,12},{16,80},... | collective-permute-start | bytes 49160 | tf_op jit(solution)/shard_map/ppermute | solution.py:16
  103.0 0.6 compare_convert_fusion.1
  103.7 1.2 collective-permute-done.4
  104.9 0.6 copy-done.2
  106.0 3.7 %collective-permute-start.5 = (f32[64,64]{1,0:T(8,128)S(1)}, f32[64,64]{1,0:T(8,128)S(1)}, u32[]{:S(2)}, u32[]{:S(2)}) collective-permute-start(f32[64,64]{1,0:T(8,128)S(1)} %fusion.60), channel_id=1, source_target_pairs={{0,128},{128,0},{4,132},{132,4},{8,136},{136,8},{12,140},{140,12},... | collective-permute-start | bytes 49160 | tf_op jit(solution)/shard_map/ppermute | solution.py:16
  109.7 0.7 compare_convert_fusion
  110.5 1.5 collective-permute-done.5
  112.2 0.8 fusion.61
  113.0 6.8 %collective-permute-start.6 = (f32[64,64]{1,0:T(8,128)}, f32[64,64]{1,0:T(8,128)}, u32[]{:S(2)}, u32[]{:S(2)}) collective-permute-start(f32[64,64]{1,0:T(8,128)} %fusion.61), channel_id=1, source_target_pairs={{0,256},{256,0},{4,260},{260,4},{8,264},{264,8},{12,268},{268,12},... | collective-permute-start | bytes 49160 | tf_op jit(solution)/shard_map/ppermute | solution.py:16
  119.8 0.7 copy.15
  120.5 2.4 %copy.17 = bf16[96,64,64]{2,1,0:T(8,128)(2,1)S(1)} copy(bf16[96,64,64]{0,2,1:T(8,128)(2,1)S(1)} %bitcast.51) | data formatting | bytes 1572864 | tf_op jit(solution)/shard_map/reshape | solution.py:82
  122.9 1.9 %gather_fusion = bf16[96,64,64]{2,1,0:T(8,128)(2,1)} fusion(bf16[4,64,64]{2,1,0:T(8,128)(2,1)S(1)} %get-tuple-element.16, s32[1024]{0:T(1024)S(1)} %pad_clamp_fusion.1), kind=kCustom, calls=%fused_computation | custom fusion | bytes 1573248 | tf_op jit(solution)/shard_map/jit(_take)/gather | solution.py:86
  124.8 0.8 select_select_fusion
  125.6 0.7 reshape.341
  126.3 30.9 %all-gather.3.cloned.1.call-done = bf16[128,4,4096]{2,1,0:T(4,128)(2,1)} async-done(((bf16[1,4,4096]{2,1,0:T(4,128)(2,1)}), bf16[128,4,4096]{2,1,0:T(4,128)(2,1)}) %all-gather.3.cloned.1.call-update) | async-done | bytes 4194320 | tf_op jit(solution)/shard_map/all_gather | solution.py:74
  157.2 12.7 %reshape.342 = bf16[512,64,64]{2,1,0:T(8,128)(2,1)} reshape(bf16[128,4,4096]{2,1,0:T(4,128)(2,1)} %all-gather.3.cloned.1.call-done) | data formatting | bytes 8388608 | tf_op jit(solution)/shard_map/reshape | solution.py:78
  169.9 5.4 %gather_fusion.1 = bf16[96,64,64]{2,1,0:T(8,128)(2,1)} fusion(bf16[512,64,64]{2,1,0:T(8,128)(2,1)} %reshape.342, s32[1024]{0:T(1024)S(1)} %pad_clamp_fusion), kind=kCustom, calls=%fused_computation.1 | custom fusion | bytes 1573248 | tf_op jit(solution)/shard_map/jit(_take)/gather | solution.py:77
  175.3 5.9 %fusion.1 = f32[96,64,64]{2,1,0:T(8,128)} fusion(bf16[96,64,64]{2,1,0:T(8,128)(2,1)} %gather_fusion, bf16[96,64,64]{2,1,0:T(8,128)(2,1)S(1)} %copy.17, bf16[96,64,64]{2,1,0:T(8,128)(2,1)} %gather_fusion.1, pred[96]{0:T(512)(128)(4,1)S(1)} %get-tuple-element.13, pred[96]{0:T(512)(128)(4,1)S(1)} %get-tuple-element.24), kind=kOutput, calls=%fused_computation.4 | convolution fusion | flops 101842944 | bytes 3932352 | tf_op jit(solution)/shard_map/bij,bjk->bik/dot_general | solution.py:87
  181.2 3.1 %copy.18 = f32[96,64,64]{0,2,1:T(8,128)S(1)} copy(f32[96,64,64]{2,1,0:T(8,128)} %fusion.1) | data formatting | bytes 3145728 | tf_op jit(solution)/shard_map/bij,bjk->bik/dot_general | solution.py:87
  184.3 1.7 copy.19
  (48 shorter events, 2.9 us)
Async XLA Ops:
  7.2 1.0 copy-start
  7.2 61.5 %copy-start.6 = (bf16[4,4096]{1,0:T(4,128)(2,1)S(1)}, bf16[4,4096]{1,0:T(4,128)(2,1)}, u32[]{:S(2)}) copy-start(bf16[4,4096]{1,0:T(4,128)(2,1)} %param.10) | copy-start | bytes 98308
  7.2 63.1 %copy-start.7 = (s32[254]{0:T(256)S(1)}, s32[254]{0:T(256)}, u32[]{:S(2)}) copy-start(s32[254]{0:T(256)} %param.13) | copy-start | bytes 3052
  7.2 64.5 %copy-start.10 = (s32[96]{0:T(128)S(1)}, s32[96]{0:T(128)}, u32[]{:S(2)}) copy-start(s32[96]{0:T(128)} %param.15) | copy-start | bytes 1156
  7.2 64.5 %copy-start.9 = (s32[96,1]{0,1:T(1,128)S(1)}, s32[96,1]{0,1:T(1,128)}, u32[]{:S(2)}) copy-start(s32[96,1]{0,1:T(1,128)} %param.16) | copy-start | bytes 1156
  7.2 64.5 %copy-start.8 = (s32[96]{0:T(128)S(1)}, s32[96]{0:T(128)}, u32[]{:S(2)}) copy-start(s32[96]{0:T(128)} %param.17) | copy-start | bytes 1156
  7.2 58.7 %all-reduce.2.cloned.1.call-start = ((), (), s32[]{:S(2)}) async-start(), calls=%async_computation | async-start | bytes 131072 | tf_op jit(solution)/shard_map/psum | solution.py:50
  9.3 147.9 %all-gather.3.cloned.1.call-start = ((), (), s32[]{:S(2)}) async-start(), calls=%async_computation.1 | async-start | bytes 4227072 | tf_op jit(solution)/shard_map/all_gather | solution.py:74
  67.0 52.8 %copy-start.1 = (bf16[96,4096]{1,0:T(8,128)(2,1)S(1)}, bf16[96,4096]{1,0:T(8,128)(2,1)}, u32[]{:S(2)}) copy-start(bf16[96,4096]{1,0:T(8,128)(2,1)} %param.14) | copy-start | bytes 2359300
  72.7 5.4 %collective-permute-start = (f32[64,64]{1,0:T(8,128)S(1)}, f32[64,64]{1,0:T(8,128)S(1)}, u32[]{:S(2)}, u32[]{:S(2)}) collective-permute-start(f32[64,64]{1,0:T(8,128)S(1)} %fusion.55), channel_id=1, source_target_pairs={{0,4},{4,0},{8,12},{12,8},{16,20},{20,16},{24,28},{28,24},{32,36},... | collective-permute-start | bytes 49160 | tf_op jit(solution)/shard_map/ppermute | solution.py:16
  78.6 4.7 %collective-permute-start.1 = (f32[64,64]{1,0:T(8,128)S(1)}, f32[64,64]{1,0:T(8,128)S(1)}, u32[]{:S(2)}, u32[]{:S(2)}) collective-permute-start(f32[64,64]{1,0:T(8,128)S(1)} %fusion.56), channel_id=1, source_target_pairs={{0,8},{8,0},{4,12},{12,4},{16,24},{24,16},{20,28},{28,20},{32,40},... | collective-permute-start | bytes 49160 | tf_op jit(solution)/shard_map/ppermute | solution.py:16
  83.7 5.7 %collective-permute-start.2 = (f32[64,64]{1,0:T(8,128)S(1)}, f32[64,64]{1,0:T(8,128)S(1)}, u32[]{:S(2)}, u32[]{:S(2)}) collective-permute-start(f32[64,64]{1,0:T(8,128)S(1)} %fusion.57), channel_id=1, source_target_pairs={{0,16},{16,0},{4,20},{20,4},{8,24},{24,8},{12,28},{28,12},{32,48},... | collective-permute-start | bytes 49160 | tf_op jit(solution)/shard_map/ppermute | solution.py:16
  89.8 9.6 %collective-permute-start.3 = (f32[64,64]{1,0:T(8,128)S(1)}, f32[64,64]{1,0:T(8,128)S(1)}, u32[]{:S(2)}, u32[]{:S(2)}) collective-permute-start(f32[64,64]{1,0:T(8,128)S(1)} %fusion.58), channel_id=1, source_target_pairs={{0,32},{32,0},{4,36},{36,4},{8,40},{40,8},{12,44},{44,12},{16,48},... | collective-permute-start | bytes 49160 | tf_op jit(solution)/shard_map/ppermute | solution.py:16
  99.9 5.1 %collective-permute-start.4 = (f32[64,64]{1,0:T(8,128)S(1)}, f32[64,64]{1,0:T(8,128)S(1)}, u32[]{:S(2)}, u32[]{:S(2)}) collective-permute-start(f32[64,64]{1,0:T(8,128)S(1)} %fusion.59), channel_id=1, source_target_pairs={{0,64},{64,0},{4,68},{68,4},{8,72},{72,8},{12,76},{76,12},{16,80},... | collective-permute-start | bytes 49160 | tf_op jit(solution)/shard_map/ppermute | solution.py:16
  104.9 0.6 copy-start.2
  106.0 6.0 %collective-permute-start.5 = (f32[64,64]{1,0:T(8,128)S(1)}, f32[64,64]{1,0:T(8,128)S(1)}, u32[]{:S(2)}, u32[]{:S(2)}) collective-permute-start(f32[64,64]{1,0:T(8,128)S(1)} %fusion.60), channel_id=1, source_target_pairs={{0,128},{128,0},{4,132},{132,4},{8,136},{136,8},{12,140},{140,12},... | collective-permute-start | bytes 49160 | tf_op jit(solution)/shard_map/ppermute | solution.py:16
  111.9 8.6 %copy-start.4 = (f32[64,64]{1,0:T(8,128)}, f32[64,64]{1,0:T(8,128)S(1)}, u32[]{:S(2)}) copy-start(f32[64,64]{1,0:T(8,128)S(1)} %collective-permute-done.5) | copy-start | bytes 49156
  113.0 11.8 %collective-permute-start.6 = (f32[64,64]{1,0:T(8,128)}, f32[64,64]{1,0:T(8,128)}, u32[]{:S(2)}, u32[]{:S(2)}) collective-permute-start(f32[64,64]{1,0:T(8,128)} %fusion.61), channel_id=1, source_target_pairs={{0,256},{256,0},{4,260},{260,4},{8,264},{264,8},{12,268},{268,12},... | collective-permute-start | bytes 49160 | tf_op jit(solution)/shard_map/ppermute | solution.py:16
  122.9 2.0 %copy-start.3 = (f32[64,64]{1,0:T(8,128)S(1)}, f32[64,64]{1,0:T(8,128)}, u32[]{:S(2)}) copy-start(f32[64,64]{1,0:T(8,128)} %copy-done.2) | copy-start | bytes 49156
  122.9 2.0 %copy-start.5 = (f32[64,64]{1,0:T(8,128)S(1)}, f32[64,64]{1,0:T(8,128)}, u32[]{:S(2)}) copy-start(f32[64,64]{1,0:T(8,128)} %copy-done.4) | copy-start | bytes 49156
Sparse Core Ops, SparseCore 0:
  10.9 54.9 all-reduce.1
  69.6 87.5 all-gather.2
where the time goes:
time: 194 us; the launch traced here: 193 us
  waiting for transfers between devices  91.6 us (47%)
  local copies, waits for them, and re-layouts  34.7 us (18%)
  starting transfers between devices  34.2 us (18%)
  between operations  14.5 us (7%)
  matrix products  10.2 us (5%)
  other arithmetic  7.55 us (4%)
    psum x1, waiting for transfers between devices, on_device(): lax.psum(partial_sum.reshape(nodes, width * width), 'level')  55.9 us
    ppermute x7, starting transfers between devices, from_partner(): return lax.ppermute(block, axis, route)  34.1 us
    all_gather x1, waiting for transfers between devices, on_device(): lax.all_gather(masked.reshape(nodes, width * width), 'branch', axis=0, ti...  30.9 us
    reshape x1, local copies, waits for them, and re-layouts, on_device(): every_masked.reshape(-1, width, width)  12.7 us
    dot_general x1, matrix products, on_device(): jnp.einsum('bij,bjk->bik', left, carried, preferred_element_type=jnp.floa...  5.87 us
    gather x1, local copies, waits for them, and re-layouts, on_device(): jnp.take(every_masked.reshape(-1, width, width), owners * nodes + column_...  5.4 us
    convert_element_type x8, other arithmetic, rank_mask(): keep = (index[None, :] < ranks[:, None]).astype(jnp.float32)  5.09 us
    ppermute x7, waiting for transfers between devices, from_partner(): return lax.ppermute(block, axis, route)  4.76 us
  transfers between devices with their start and end apart: 9, of which 8 were waited for; matrix products, arithmetic and copies ran while one was open for 10% of the time, Pallas kernels for 0%

commit v1 on v0

v1 whole, which is shorter than its diff:
```python
import functools

import jax
import jax.numpy as jnp
from jax import lax
from jax.experimental import pallas as pl
from jax.experimental.pallas import tpu as pltpu
from jax.sharding import PartitionSpec as P

VMEM = pl.BlockSpec(memory_space=pltpu.VMEM)
SMEM = pl.BlockSpec(memory_space=pltpu.SMEM)
ROWS = 16
TOGETHER = 4
F32 = jnp.float32
BF16 = jnp.bfloat16


def iota(shape, axis):
    return lax.broadcasted_iota(jnp.int32, shape, axis)


def nn(a, b):
    return jnp.dot(a, b, preferred_element_type=F32)


def nt(a, b):
    return lax.dot_general(a, b, (((1,), (1,)), ((), ())), preferred_element_type=F32)


def tn(a, b):
    return lax.dot_general(a, b, (((0,), (0,)), ((), ())), preferred_element_type=F32)


def halves(x):
    high = x.astype(BF16)
    return high, (x - high.astype(F32)).astype(BF16)


def keep_rank(gram, rank):
    return jnp.where((iota(gram.shape, 0) < rank) & (iota(gram.shape, 1) < rank), gram, 0.0)


def lift(masked, transfer):
    inner = []
    for gram, mat in zip(masked, transfer):
        high, low = halves(gram)
        inner.append(nn(high, mat) + nn(low, mat))
    high, low = halves(jnp.concatenate(inner, axis=0))
    mats = jnp.concatenate(transfer, axis=0)
    return tn(mats, high) + tn(mats, low)


def pack(square):
    half = square.shape[0] // 2
    return jnp.concatenate([square[:half], square[half:]], axis=1)


def unpack(packed):
    half = packed.shape[1] // 2
    return jnp.concatenate([packed[:, :half], packed[:, half:]], axis=0)


def reach(index, count):
    return (index ^ ((index + 1) % count)).bit_length()


def gram_kernel(basis_ref, out_ref):
    copies = out_ref.shape[0]
    width = basis_ref.shape[1]
    wide = 2 * width
    row = iota((width, wide), 0)
    lane = iota((width, wide), 1)
    column = lane & (width - 1)
    sides = []
    for side in range(2):
        both = jnp.concatenate([basis_ref[side], basis_ref[side + 2]], axis=0)
        crossed = nt(both, both)
        sides.append(jnp.where(lane < width, crossed[:width], crossed[width:]))
    folded = jnp.where(row <= column, sides[0], sides[1])
    diagonal = jnp.sum(jnp.where(row == column, sides[1], 0.0), axis=0, keepdims=True)
    for copy in range(copies):
        out_ref[copy, :width] = folded
        out_ref[copy, width:] = jnp.broadcast_to(diagonal, (8, wide))


def share_kernel(rank_ref, level_ref, parts_ref, share_ref, total_ref, scratch):
    copies, share, wide = share_ref.shape
    width = wide // 2
    total = parts_ref[0]
    for part in range(1, parts_ref.shape[0]):
        total = total + parts_ref[part]
    total_ref[...] = total
    row = iota((width, wide), 0)
    lane = iota((width, wide), 1)
    column = lane & (width - 1)
    low = lane < width
    upper = jnp.where(low, rank_ref[0], rank_ref[2])
    lower = jnp.where(low, rank_ref[1], rank_ref[3])
    kept = jnp.maximum(row, column) < jnp.where(row <= column, upper, lower)
    scratch[...] = jnp.where(kept, total[:width], 0.0)
    mine = scratch[pl.ds(pl.multiple_of(level_ref[0] * share, share), share), :].astype(BF16)
    for copy in range(copies):
        share_ref[copy] = mine


def near_kernel(rank_ref, path_rank_ref, place_ref, total_ref, bottom_ref, path_ref, left_ref, sent_ref):
    nodes, width, _ = bottom_ref.shape
    wide = 2 * width
    group, rows, _ = sent_ref.shape
    heights = path_ref.shape[0]
    half = width // 2
    folded = total_ref[:width]
    diagonal = total_ref[width : width + 1]
    turned = folded.T
    row = iota((width, width), 0)
    column = iota((width, width), 1)
    even_first = jnp.where(row < half, 2 * row, 2 * row - width + 1)
    order = (column == even_first).astype(F32).astype(BF16)
    masked = []
    for node in range(nodes):
        pair, side = node // 2, node % 2
        here = folded[:, pair * width : (pair + 1) * width]
        there = turned[pair * width : (pair + 1) * width]
        if side == 0:
            gram = jnp.where(row <= column, here, there)
        else:
            centre = jnp.broadcast_to(diagonal[:, pair * width : (pair + 1) * width], (width, width))
            gram = jnp.where(row > column, here, jnp.where(row < column, there, centre))
        gram = keep_rank(gram, rank_ref[node])
        masked.append(gram)
        left_ref[node] = nt(nn(order, gram.astype(BF16)).astype(BF16), order).astype(BF16)
    current = lift(masked, [bottom_ref[node] for node in range(nodes)])
    terms = []
    for height in range(heights):
        current = lift([keep_rank(current, path_rank_ref[height])], [path_ref[height]])
        terms.append(pack(current).astype(BF16))
    place = place_ref[0]
    lane = iota((1, wide), 1)
    lower = jnp.where(lane < width, rank_ref[1], rank_ref[3])
    diagonal = jnp.where((lane & (width - 1)) < lower, diagonal, 0.0)
    diagonal = jnp.broadcast_to(diagonal, (rows - half, wide)).astype(BF16)
    none = jnp.zeros((half, wide), BF16)
    for target in range(group):
        height = min(reach(target, 2 * group), heights)
        inside = jnp.right_shift(place, height) == target >> height

        @pl.when(inside)
        def _():
            sent_ref[target, :half] = terms[height - 1]

        @pl.when(jnp.logical_not(inside))
        def _():
            sent_ref[target, :half] = none

        sent_ref[target, half:] = diagonal


def far_kernel(path_rank_ref, place_ref, received_ref, path_ref, near_ref, sent_ref):
    group, rows, wide = received_ref.shape
    targets = sent_ref.shape[0]
    width = wide // 2
    half = width // 2
    heights = path_ref.shape[0]
    total = received_ref[0, :half].astype(F32)
    for member in range(1, group):
        total = total + received_ref[member, :half].astype(F32)
    near_ref[...] = total
    diagonals = [received_ref[member, half:].astype(F32)[:1] for member in range(group)]
    diagonals += [jnp.zeros((rows - half - group, wide), F32)] if group < rows - half else []
    diagonals = jnp.concatenate(diagonals, axis=0).astype(BF16)
    current = unpack(total)
    terms = []
    for height in range(heights):
        current = lift([keep_rank(current, path_rank_ref[height])], [path_ref[height]])
        terms.append(pack(current).astype(BF16))
    place = place_ref[0]
    none = jnp.zeros((half, wide), BF16)
    for target in range(targets):
        height = reach(target, targets)
        inside = jnp.right_shift(place, height) == target >> height

        @pl.when(inside)
        def _():
            sent_ref[target, :half] = terms[height - 1]

        @pl.when(jnp.logical_not(inside))
        def _():
            sent_ref[target, :half] = none

        sent_ref[target, half:] = diagonals


def top_kernel(last_ref, near_ref, received_ref, out_ref, diagonal_ref, scratch):
    targets, rows, wide = received_ref.shape
    half = wide // 4
    total = received_ref[0, :half].astype(F32)
    for member in range(1, targets):
        total = total + received_ref[member, :half].astype(F32)
    total = jnp.where(last_ref[0] == 1, total, near_ref[...])
    scratch[...] = unpack(total)
    natural = jnp.concatenate([scratch[pl.ds(side, half, stride=2), :] for side in range(2)], axis=1)
    for tile in range(half):
        out_ref[:, tile * wide : (tile + 1) * wide] = natural[tile : tile + 1]
    group = diagonal_ref.shape[0] // targets
    for member in range(targets):
        diagonal_ref[member * group : (member + 1) * group] = received_ref[member, half:].astype(F32)[:group]


def project_kernel(
    owner_ref,
    column_ref,
    row_ref,
    core_ref,
    blocks_ref,
    own_ref,
    other_ref,
    diagonal_ref,
    left_ref,
    out_ref,
    spread,
    result,
    triangles,
):
    step = pl.program_id(0)
    count, flat = blocks_ref.shape
    depth = own_ref.shape[2]
    width = left_ref.shape[1]
    wide = 2 * width
    tiles = flat // wide
    row = iota((width, wide), 0)
    lane = iota((width, wide), 1)
    column = lane & (width - 1)
    low = lane < width

    @pl.when(step == 0)
    def _():
        triangles[0, 0] = (row <= column).astype(F32)
        triangles[0, 1] = (row < column).astype(F32)
        triangles[0, 2] = jnp.zeros((width, wide), F32)
        triangles[1, 0] = (row > column).astype(F32)
        triangles[1, 1] = (row > column).astype(F32)
        triangles[1, 2] = (row == column).astype(F32)

    for tile in range(tiles):
        spread[tile * count : (tile + 1) * count, :] = blocks_ref[:, tile * wide : (tile + 1) * wide].astype(F32)

    def right_product(index):
        block = step * count + index
        owner = owner_ref[block]
        cluster = column_ref[block]
        pair = jnp.right_shift(cluster, 1)
        side = cluster & 1
        across = jnp.right_shift(owner, 1) & (depth - 1)
        along = owner // (2 * depth)
        near = own_ref[along, :, across].reshape(width, wide)
        far = other_ref[along, :, across].reshape(width, wide)
        folded = jnp.where((owner & 1) == core_ref[0], near, far).astype(F32)
        centre = jnp.broadcast_to(diagonal_ref[pl.ds(owner, 1), :], (width, wide))
        direct = folded * triangles[side, 0] + centre * triangles[side, 2]
        mirrored = folded * triangles[side, 1]
        wanted = low == (pair == 0)
        direct = jnp.where(wanted, direct, pltpu.roll(direct, width, 1)).astype(BF16)
        mirrored = jnp.where(wanted, mirrored, pltpu.roll(mirrored, width, 1)).astype(BF16)[:, :width]
        here = spread[pl.ds(index, tiles, stride=count), :]
        rows = jnp.concatenate([here, pltpu.roll(here, width, 1)], axis=0).astype(BF16)[:, :width]
        return nn(rows, direct) + nt(rows, jnp.concatenate([mirrored, mirrored], axis=0))

    for first in range(0, count, TOGETHER):
        group = range(first, first + TOGETHER)
        carried = [right_product(index).astype(BF16) for index in group]
        for index, value in zip(group, carried):
            full = nn(left_ref[row_ref[step * count + index]], value)
            result[pl.ds(index, tiles, stride=count), :] = jnp.where(low[:tiles], full[:tiles], full[tiles:])
    for tile in range(tiles):
        out_ref[:, tile * wide : (tile + 1) * wide] = result[tile * count : (tile + 1) * count, :]


def copies_of(block, count):
    return jnp.broadcast_to(block[None], (count,) + block.shape)


def shape(dims, dtype):
    return jax.ShapeDtypeStruct(dims, dtype)


def on_device(
    depth,
    basis,
    bottom_transfer,
    bottom_rank,
    upper_transfer,
    upper_rank,
    couplings,
    row_cluster,
    column_owner,
    column_cluster,
):
    nodes, width, _ = basis.shape
    wide = 2 * width
    half = width // 2
    branches = lax.axis_size("branch")
    parts = lax.axis_size("level")
    levels = branches.bit_length() - 1
    group = 2 * depth
    spans = branches // group
    near_levels = group.bit_length() - 1
    share = width // parts
    me_branch = lax.axis_index("branch")
    me_level = lax.axis_index("level")
    core = me_branch & 1
    me_near = me_branch & (group - 1)
    me_far = me_branch // group
    blk = couplings.shape[0]

    along_z = [[y * group + z * 2 + c for z in range(depth)] for y in range(spans) for c in range(2)]
    along_y = [[y * group + near for y in range(spans)] for near in range(group)]
    same_y = [[y * group + near for near in range(group)] for y in range(spans)]
    along_yx = [[(y * group + near) * parts + x for y in range(spans) for x in range(parts)] for near in range(group)]

    partial_sums = pl.pallas_call(
        gram_kernel,
        out_shape=shape((parts, width + 8, wide), F32),
        in_specs=[VMEM],
        out_specs=VMEM,
        name="gram",
    )(basis)
    gathered = lax.all_to_all(partial_sums, "level", 0, 0)
    shares, total = pl.pallas_call(
        share_kernel,
        out_shape=[shape((depth, share, wide), BF16), shape((width + 8, wide), F32)],
        in_specs=[SMEM, SMEM, VMEM],
        out_specs=[VMEM, VMEM],
        scratch_shapes=[pltpu.VMEM((width, wide), F32)],
        name="share",
    )(bottom_rank, me_level[None], gathered)

    column = lax.all_to_all(shares, "branch", 0, 0, axis_index_groups=along_z)
    own = lax.all_to_all(
        copies_of(column, spans * parts), ("branch", "level"), 0, 0, axis_index_groups=along_yx
    ).reshape(spans, parts, depth, share, wide)
    other = lax.ppermute(own, "branch", [(i, i ^ 1) for i in range(branches)])

    heights = jnp.arange(levels, dtype=jnp.int32)
    slots = 2 * branches - jnp.right_shift(2 * branches, heights) + jnp.right_shift(me_branch, heights)
    path = jnp.take(upper_transfer, slots, axis=0).reshape(levels, width, width)
    path_rank = jnp.take(upper_rank, slots, axis=0)
    left, near_sent = pl.pallas_call(
        near_kernel,
        out_shape=[shape((nodes, width, width), BF16), shape((group, half + 16, wide), BF16)],
        in_specs=[SMEM, SMEM, SMEM, VMEM, VMEM, VMEM],
        out_specs=[VMEM, VMEM],
        name="near",
    )(
        bottom_rank,
        path_rank[:near_levels],
        me_near[None],
        total,
        bottom_transfer.reshape(nodes, width, width),
        path[:near_levels],
    )
    near_received = lax.all_to_all(near_sent, "branch", 0, 0, axis_index_groups=same_y)
    near_gram, far_sent = pl.pallas_call(
        far_kernel,
        out_shape=[shape((half, wide), F32), shape((spans, half + 16, wide), BF16)],
        in_specs=[SMEM, SMEM, VMEM, VMEM],
        out_specs=[VMEM, VMEM],
        name="far",
    )(path_rank[near_levels:], me_far[None], near_received, path[near_levels:])
    far_received = lax.all_to_all(far_sent, "branch", 0, 0, axis_index_groups=along_y)
    upper_grams, diagonals = pl.pallas_call(
        top_kernel,
        out_shape=[shape((1, width * width), F32), shape((branches, wide), F32)],
        in_specs=[SMEM, VMEM, VMEM],
        out_specs=[VMEM, VMEM],
        scratch_shapes=[pltpu.VMEM((width, width), F32)],
        name="top",
    )((me_near == group - 1).astype(jnp.int32)[None], near_gram, far_received)

    whole = pl.BlockSpec(own.shape, lambda i, *_: (0, 0, 0, 0, 0))
    projected = pl.pallas_call(
        project_kernel,
        out_shape=shape((blk, width * width), F32),
        grid_spec=pltpu.PrefetchScalarGridSpec(
            num_scalar_prefetch=4,
            grid=(blk // ROWS,),
            in_specs=[
                pl.BlockSpec((ROWS, width * width), lambda i, *_: (i, 0)),
                whole,
                whole,
                pl.BlockSpec((branches, wide), lambda i, *_: (0, 0)),
                pl.BlockSpec((nodes, width, width), lambda i, *_: (0, 0, 0)),
            ],
            out_specs=pl.BlockSpec((ROWS, width * width), lambda i, *_: (i, 0)),
            scratch_shapes=[
                pltpu.VMEM((ROWS * half, wide), F32),
                pltpu.VMEM((ROWS * half, wide), F32),
                pltpu.VMEM((2, 3, width, wide), F32),
            ],
        ),
        compiler_params=pltpu.CompilerParams(vmem_limit_bytes=24 * 1024 * 1024),
        name="project",
    )(column_owner[:, 0], column_cluster, row_cluster, core[None], couplings, own, other, diagonals, left)
    return (upper_grams, projected)


def solution(mesh):
    placed = (
        P("branch", None, "level"),
        P("branch", None),
        P("branch"),
        P(),
        P(),
        P(("branch", "level"), None),
        P(("branch", "level")),
        P(("branch", "level"), None),
        P(("branch", "level")),
    )
    depth = min(8, mesh.shape["branch"] // 4)
    return jax.shard_map(
        functools.partial(on_device, depth),
        mesh=mesh,
        in_specs=placed,
        out_specs=(P("branch", None), P(("branch", "level"), None)),
        check_vma=False,
    )
```

time: 194 us -> 123 us (0.63)
  waiting for transfers between devices: 91.6 us -> 44.8 us
  local copies, waits for them, and re-layouts: 34.7 us -> 10.7 us
  Pallas kernels: 0 us -> 21.4 us
  blocking collectives: 0 us -> 16.9 us
  between operations: 14.5 us -> 0.77 us
  matrix products: 10.2 us -> 0 us
  starting transfers between devices: 34.2 us -> 27.2 us
  other arithmetic: 7.55 us -> 0.65 us
    psum x1 -> x0, waiting for transfers between devices: 55.9 us -> none  [on_device(): lax.psum(partial_sum.reshape(nodes, width * width), 'level')]
    all_to_all x0 -> x4, waiting for transfers between devices: none -> 44.8 us  [the longest x1 23.1 us: on_device(): lax.all_to_all(copies_of(column, spans * parts), ('branch', 'level'), 0,...]
    all_gather x1 -> x0, waiting for transfers between devices: 30.9 us -> none  [on_device(): lax.all_gather(masked.reshape(nodes, width * width), 'branch', axis=0, ti...]
    ppermute x7 -> x1, starting transfers between devices: 34.1 us -> 7.31 us  [on_device(): other = lax.ppermute(own, 'branch', [(i, i ^ 1) for i in range(branches)])]
    pallas_call x0 -> x6, Pallas kernels: none -> 21.4 us  [the longest x1 9.98 us: on_device(): pl.pallas_call(project_kernel, out_shape=shape((blk, width * width), F32)...]
    all_to_all x0 -> x4, starting transfers between devices: none -> 19.9 us  [the longest x1 7.95 us: on_device(): lax.all_to_all(copies_of(column, spans * parts), ('branch', 'level'), 0,...]
    all_to_all x0 -> x1, blocking collectives: none -> 16.9 us  [on_device(): column = lax.all_to_all(shares, 'branch', 0, 0, axis_index_groups=along_z)]
    reshape x6 -> x1, local copies, waits for them, and re-layouts: 17.6 us -> 0.75 us  [on_device(): bottom_transfer.reshape(nodes, width, width)]
  transfers between devices with their start and end apart: 9 -> 5, of which waited for: 8 -> 4; matrix products, arithmetic and copies ran while one was open for 10% -> 4% of each run, Pallas kernels for 0% -> 6%
where the time goes in v1:
time: 123 us; the launch traced here: 122 us
  waiting for transfers between devices  44.8 us (36%)
  starting transfers between devices  27.2 us (22%)
  Pallas kernels  21.4 us (17%)
  blocking collectives  16.9 us (14%)
  local copies, waits for them, and re-layouts  10.7 us (9%)
    all_to_all x1, waiting for transfers between devices, on_device(): lax.all_to_all(copies_of(column, spans * parts), ('branch', 'level'), 0,...  23.1 us
    all_to_all x1, blocking collectives, on_device(): column = lax.all_to_all(shares, 'branch', 0, 0, axis_index_groups=along_z)  16.9 us
    pallas_call x1, Pallas kernels, on_device(): pl.pallas_call(project_kernel, out_shape=shape((blk, width * width), F32)...  9.98 us
    all_to_all x1, waiting for transfers between devices, on_device(): lax.all_to_all(far_sent, 'branch', 0, 0, axis_index_groups=along_y)  8.45 us
    all_to_all x1, waiting for transfers between devices, on_device(): lax.all_to_all(near_sent, 'branch', 0, 0, axis_index_groups=same_y)  8.27 us
    all_to_all x1, starting transfers between devices, on_device(): lax.all_to_all(copies_of(column, spans * parts), ('branch', 'level'), 0,...  7.95 us
    ppermute x1, starting transfers between devices, on_device(): other = lax.ppermute(own, 'branch', [(i, i ^ 1) for i in range(branches)])  7.31 us
    all_to_all x1, waiting for transfers between devices, on_device(): gathered = lax.all_to_all(partial_sums, 'level', 0, 0)  4.91 us
  transfers between devices with their start and end apart: 5, of which 4 were waited for; matrix products, arithmetic and copies ran while one was open for 4% of the time, Pallas kernels for 6%

profile of v1, /device:TPU:1, one launch (start us, length us, event | category | flops | bytes accessed | tf_op | source)
XLA Modules:
  0.0 122.4 jit_solution(13940396257950542598)
XLA Ops:
  0.6 0.0 copy-start
  0.6 2.2 %gram.1 = f32[4,72,128]{2,1,0:T(8,128)} custom-call(bf16[4,64,1024]{2,1,0:T(8,128)(2,1)} %basis_ref.1), custom_call_target="tpu_custom_call" | custom-call | tf_op jit(solution)/shard_map/gram/pallas_call | solution.py:320
  2.8 4.8 %all-to-all-start = ((f32[4,72,128]{2,1,0:T(8,128)}), f32[4,72,128]{2,1,0:T(8,128)S(1)}, u32[]{:S(2)}, u32[]{:S(2)}) async-start(f32[4,72,128]{2,1,0:T(8,128)} %gram.1), calls=%async_computation | async-start | bytes 294912 | tf_op jit(solution)/shard_map/all_to_all | solution.py:327
  7.6 0.0 copy-start.7
  7.6 4.9 %all-to-all-done.parts_ref = f32[4,72,128]{2,1,0:T(8,128)S(1)} async-done(((f32[4,72,128]{2,1,0:T(8,128)}), f32[4,72,128]{2,1,0:T(8,128)S(1)}, u32[]{:S(2)}, u32[]{:S(2)}) %all-to-all-start) | async-done | bytes 147488 | tf_op jit(solution)/shard_map/all_to_all | solution.py:327
  12.6 0.0 copy-start.9
  12.6 0.7 copy-done.9
  13.2 1.6 %share.1 = (bf16[8,16,128]{2,1,0:T(8,128)(2,1)}, f32[72,128]{1,0:T(8,128)}) custom-call(s32[4]{0:T(128)} %rank_ref.3, s32[1]{0:T(128)} %bitcast.4.level_ref, f32[4,72,128]{2,1,0:T(8,128)} %copy-done.9), custom_call_target="tpu_custom_call" | custom-call | tf_op jit(solution)/shard_map/share/pallas_call | solution.py:328
  14.8 16.9 %all_to_all.25 = bf16[8,16,128]{2,1,0:T(8,128)(2,1)S(1)} all-to-all(bf16[8,16,128]{2,1,0:T(8,128)(2,1)} %get-tuple-element.15), channel_id=1, replica_groups={{0,8,16,24,32,40,48,56},{4,12,20,28,36,44,52,60},{64,72,80,88,96,104,11..., dimensions={0} | all-to-all | bytes 65536 | tf_op jit(solution)/shard_map/all_to_all | solution.py:337
  31.7 0.0 copy-start.11
  31.7 1.2 broadcast_in_dim.43
  32.9 0.0 copy-start.4
  32.9 0.0 copy-start.5
  32.9 0.0 copy-start.6
  32.9 7.9 %all-to-all-start.4 = ((bf16[32,8,16,128]{3,2,1,0:T(8,128)(2,1)}), bf16[32,8,16,128]{3,2,1,0:T(8,128)(2,1)S(1)}, u32[]{:S(2)}, u32[]{:S(2)}) async-start(bf16[32,8,16,128]{3,2,1,0:T(8,128)(2,1)} %broadcast_in_dim.43), calls=%async_computation.4 | async-start | bytes 2097152 | tf_op jit(solution)/shard_map/all_to_all | solution.py:338
  40.9 0.0 copy-done
  40.9 0.6 gather_fusion.1
  41.5 23.1 %all-to-all-done.4 = bf16[32,8,16,128]{3,2,1,0:T(8,128)(2,1)S(1)} async-done(((bf16[32,8,16,128]{3,2,1,0:T(8,128)(2,1)}), bf16[32,8,16,128]{3,2,1,0:T(8,128)(2,1)S(1)}, u32[]{:S(2)}, u32[]{:S(2)}) %all-to-all-start.4) | async-done | bytes 1048608 | tf_op jit(solution)/shard_map/all_to_all | solution.py:338
  64.6 7.3 %collective-permute-start = (bf16[8,4,8,16,128]{4,3,2,1,0:T(8,128)(2,1)S(1)}, bf16[8,4,8,16,128]{4,3,2,1,0:T(8,128)(2,1)}, u32[]{:S(2)}, u32[]{:S(2)}) collective-permute-start(bf16[8,4,8,16,128]{4,3,2,1,0:T(8,128)(2,1)S(1)} %bitcast.10), channel_id=1, source_target_pairs={{0,4},{4,0},{8,12},{12,8},{16,20},{20,16},{24,28},{28,24},{32,36},... | collective-permute-start | bytes 3145736 | tf_op jit(solution)/shard_map/ppermute | solution.py:341
  72.0 0.1 broadcast_select_fusion
  72.0 0.0 copy-done.7
  72.1 0.6 gather_fusion
  72.7 0.7 slice.21.path_ref
  73.5 0.0 copy-done.11
  73.5 0.7 reshape.47.bottom_ref
  74.2 0.5 broadcast_select_fusion.1
  74.8 3.5 %near.1 = (bf16[4,64,64]{2,1,0:T(8,128)(2,1)}, bf16[16,48,128]{2,1,0:T(8,128)(2,1)}) custom-call(s32[4]{0:T(128)} %rank_ref.3, s32[4]{0:T(128)} %bitcast.13, s32[1]{0:T(128)} %bitcast.3.place_ref, f32[72,128]{1,0:T(8,128)} %get-tuple-element.10.total_ref, bf16[4,64,64]{2,1,0:T(8,128)(2,1)} %reshape.47.bottom_ref, bf16[4,64,64]{2,1,0:T(8,128)(2,1)} %slice.21.path_ref), custom_call_target="tpu_custom_call" | custom-call | tf_op jit(solution)/shard_map/near/pallas_call | solution.py:347
  78.2 3.4 %all-to-all-start.1 = ((bf16[16,48,128]{2,1,0:T(8,128)(2,1)}), bf16[16,48,128]{2,1,0:T(8,128)(2,1)S(1)}, u32[]{:S(2)}, u32[]{:S(2)}) async-start(bf16[16,48,128]{2,1,0:T(8,128)(2,1)} %get-tuple-element.11), calls=%async_computation.1 | async-start | bytes 393216 | tf_op jit(solution)/shard_map/all_to_all | solution.py:361
  81.7 1.2 %slice.18.path_rank_ref = s32[3]{0:T(128)} slice(s32[7]{0:T(128)} %broadcast_select_fusion.1), slice={[4:7]} | slice | bytes 24 | tf_op jit(solution)/shard_map/slice | solution.py:368
  83.0 0.7 slice.23.path_ref
  83.7 8.3 %all-to-all-done.1.received_ref = bf16[16,48,128]{2,1,0:T(8,128)(2,1)S(1)} async-done(((bf16[16,48,128]{2,1,0:T(8,128)(2,1)}), bf16[16,48,128]{2,1,0:T(8,128)(2,1)S(1)}, u32[]{:S(2)}, u32[]{:S(2)}) %all-to-all-start.1) | async-done | bytes 196640 | tf_op jit(solution)/shard_map/all_to_all | solution.py:361
  91.9 0.0 copy-start.8
  91.9 0.7 copy-done.8
  92.6 2.6 %far.1 = (f32[32,128]{1,0:T(8,128)}, bf16[8,48,128]{2,1,0:T(8,128)(2,1)}) custom-call(s32[3]{0:T(128)} %slice.18.path_rank_ref, s32[1]{0:T(128)} %bitcast.2.place_ref, bf16[16,48,128]{2,1,0:T(8,128)(2,1)} %copy-done.8, bf16[3,64,64]{2,1,0:T(8,128)(2,1)} %slice.23.path_ref), custom_call_target="tpu_custom_call" | custom-call | tf_op jit(solution)/shard_map/far/pallas_call | solution.py:362
  95.2 3.6 %all-to-all-start.2 = ((bf16[8,48,128]{2,1,0:T(8,128)(2,1)}), bf16[8,48,128]{2,1,0:T(8,128)(2,1)S(1)}, u32[]{:S(2)}, u32[]{:S(2)}) async-start(bf16[8,48,128]{2,1,0:T(8,128)(2,1)} %get-tuple-element.13), calls=%async_computation.2 | async-start | bytes 196608 | tf_op jit(solution)/shard_map/all_to_all | solution.py:369
  98.8 8.4 %all-to-all-done.2.received_ref = bf16[8,48,128]{2,1,0:T(8,128)(2,1)S(1)} async-done(((bf16[8,48,128]{2,1,0:T(8,128)(2,1)}), bf16[8,48,128]{2,1,0:T(8,128)(2,1)S(1)}, u32[]{:S(2)}, u32[]{:S(2)}) %all-to-all-start.2) | async-done | bytes 98336 | tf_op jit(solution)/shard_map/all_to_all | solution.py:369
  107.3 0.6 copy-done.10
  107.9 1.7 %top.1 = (f32[1,4096]{1,0:T(1,128)}, f32[128,128]{1,0:T(8,128)}) custom-call(s32[1]{0:T(128)} %bitcast.last_ref, f32[32,128]{1,0:T(8,128)} %get-tuple-element.12.near_ref, bf16[8,48,128]{2,1,0:T(8,128)(2,1)} %copy-done.10), custom_call_target="tpu_custom_call" | custom-call | tf_op jit(solution)/shard_map/top/pallas_call | solution.py:370
  109.6 0.0 collective-permute-done.other_ref
  109.6 0.0 copy-done.4
  109.6 0.0 copy-done.5
  109.6 0.0 copy-done.6
  109.6 0.0 copy-start.1
  109.7 1.1 copy-done.1
  110.8 0.0 copy-start.2
  110.8 0.8 copy-done.2
  111.6 0.8 copy-done.3
  112.5 10.0 %project.1 = f32[96,4096]{1,0:T(8,128)} custom-call(s32[96]{0:T(128)S(1)} %bitcast.12, s32[96]{0:T(128)S(1)} %copy-done.5, s32[96]{0:T(128)S(1)} %copy-done.6, s32[1]{0:T(128)} %bitcast.6.core_ref, bf16[96,4096]{1,0:T(8,128)(2,1)S(1)} %copy-done.1, bf16[8,4,8,16,128]{4,3,2,1,0:T(8,128)(2,1)S(1)} %bitcast.11, ...), custom_call_target="tpu_custom_call" | custom-call | tf_op jit(solution)/shard_map/project/pallas_call | solution.py:380
  (7 shorter events, 0.1 us)
Async XLA Ops:
  0.6 40.3 %copy-start = (bf16[254,4096]{1,0:T(8,128)(2,1)S(1)}, bf16[254,4096]{1,0:T(8,128)(2,1)}, u32[]{:S(2)}) copy-start(bf16[254,4096]{1,0:T(8,128)(2,1)} %param.12) | copy-start | bytes 6242308
  2.8 9.8 %all-to-all-start = ((f32[4,72,128]{2,1,0:T(8,128)}), f32[4,72,128]{2,1,0:T(8,128)S(1)}, u32[]{:S(2)}, u32[]{:S(2)}) async-start(f32[4,72,128]{2,1,0:T(8,128)} %gram.1), calls=%async_computation | async-start | bytes 294912 | tf_op jit(solution)/shard_map/all_to_all | solution.py:327
  7.6 64.4 %copy-start.7 = (s32[254]{0:T(256)S(1)}, s32[254]{0:T(256)}, u32[]{:S(2)}) copy-start(s32[254]{0:T(256)} %param.13) | copy-start | bytes 3052
  12.6 0.7 copy-start.9
  31.7 41.8 %copy-start.11 = (bf16[4,4096]{1,0:T(4,128)(2,1)S(1)}, bf16[4,4096]{1,0:T(4,128)(2,1)}, u32[]{:S(2)}) copy-start(bf16[4,4096]{1,0:T(4,128)(2,1)} %param.10) | copy-start | bytes 98308
  32.9 76.7 %copy-start.4 = (s32[96,1]{0,1:T(1,128)S(1)}, s32[96,1]{0,1:T(1,128)}, u32[]{:S(2)}) copy-start(s32[96,1]{0,1:T(1,128)} %param.16) | copy-start | bytes 1156
  32.9 76.7 %copy-start.5 = (s32[96]{0:T(128)S(1)}, s32[96]{0:T(128)}, u32[]{:S(2)}) copy-start(s32[96]{0:T(128)} %column_ref.1) | copy-start | bytes 1156
  32.9 76.7 %copy-start.6 = (s32[96]{0:T(128)S(1)}, s32[96]{0:T(128)}, u32[]{:S(2)}) copy-start(s32[96]{0:T(128)} %row_ref.1) | copy-start | bytes 1156
  32.9 31.7 %all-to-all-start.4 = ((bf16[32,8,16,128]{3,2,1,0:T(8,128)(2,1)}), bf16[32,8,16,128]{3,2,1,0:T(8,128)(2,1)S(1)}, u32[]{:S(2)}, u32[]{:S(2)}) async-start(bf16[32,8,16,128]{3,2,1,0:T(8,128)(2,1)} %broadcast_in_dim.43), calls=%async_computation.4 | async-start | bytes 2097152 | tf_op jit(solution)/shard_map/all_to_all | solution.py:338
  64.6 45.0 %collective-permute-start = (bf16[8,4,8,16,128]{4,3,2,1,0:T(8,128)(2,1)S(1)}, bf16[8,4,8,16,128]{4,3,2,1,0:T(8,128)(2,1)}, u32[]{:S(2)}, u32[]{:S(2)}) collective-permute-start(bf16[8,4,8,16,128]{4,3,2,1,0:T(8,128)(2,1)S(1)} %bitcast.10), channel_id=1, source_target_pairs={{0,4},{4,0},{8,12},{12,8},{16,20},{20,16},{24,28},{28,24},{32,36},... | collective-permute-start | bytes 3145736 | tf_op jit(solution)/shard_map/ppermute | solution.py:341
  78.2 13.7 %all-to-all-start.1 = ((bf16[16,48,128]{2,1,0:T(8,128)(2,1)}), bf16[16,48,128]{2,1,0:T(8,128)(2,1)S(1)}, u32[]{:S(2)}, u32[]{:S(2)}) async-start(bf16[16,48,128]{2,1,0:T(8,128)(2,1)} %get-tuple-element.11), calls=%async_computation.1 | async-start | bytes 393216 | tf_op jit(solution)/shard_map/all_to_all | solution.py:361
  91.9 0.7 copy-start.8
  95.2 12.1 %all-to-all-start.2 = ((bf16[8,48,128]{2,1,0:T(8,128)(2,1)}), bf16[8,48,128]{2,1,0:T(8,128)(2,1)S(1)}, u32[]{:S(2)}, u32[]{:S(2)}) async-start(bf16[8,48,128]{2,1,0:T(8,128)(2,1)} %get-tuple-element.13), calls=%async_computation.2 | async-start | bytes 196608 | tf_op jit(solution)/shard_map/all_to_all | solution.py:369
  107.3 0.6 copy-start.10
  109.6 1.1 copy-start.1
  110.8 0.8 copy-start.2
  111.6 0.8 copy-start.3

commit v2 on v1

v2 whole, which is shorter than its diff:
```python
import jax
import jax.numpy as jnp
from jax import lax
from jax.experimental import pallas as pl
from jax.experimental.pallas import tpu as pltpu
from jax.sharding import PartitionSpec as P

VMEM = pl.BlockSpec(memory_space=pltpu.VMEM)
SMEM = pl.BlockSpec(memory_space=pltpu.SMEM)
SMALL = pltpu.CompilerParams(vmem_limit_bytes=8 * 1024 * 1024)
ROWS = 16
TOGETHER = 4
F32 = jnp.float32
BF16 = jnp.bfloat16


def iota(shape, axis):
    return lax.broadcasted_iota(jnp.int32, shape, axis)


def nn(a, b):
    return jnp.dot(a, b, preferred_element_type=F32)


def nt(a, b):
    return lax.dot_general(a, b, (((1,), (1,)), ((), ())), preferred_element_type=F32)


def tn(a, b):
    return lax.dot_general(a, b, (((0,), (0,)), ((), ())), preferred_element_type=F32)


def halves(x):
    high = x.astype(BF16)
    return high, (x - high.astype(F32)).astype(BF16)


def keep_rank(gram, rank):
    return jnp.where((iota(gram.shape, 0) < rank) & (iota(gram.shape, 1) < rank), gram, 0.0)


def lift(masked, transfer):
    inner = []
    for gram, mat in zip(masked, transfer):
        high, low = halves(gram)
        inner.append(nn(high, mat) + nn(low, mat))
    high, low = halves(jnp.concatenate(inner, axis=0))
    mats = jnp.concatenate(transfer, axis=0)
    return tn(mats, high) + tn(mats, low)


def product(multiply, a, b):
    return multiply(a[0], b[0]) + (multiply(a[0], b[1]) + multiply(a[1], b[0]))


def fold(square):
    half = square.shape[0] // 2
    row, column = iota((half, half), 0), iota((half, half), 1)
    first = square[:half, :half]
    mixed = jnp.where(row < column, first, square[half:, half:])
    centre = jnp.sum(jnp.where(row == column, first, 0.0), axis=0, keepdims=True)
    return jnp.concatenate([mixed, square[:half, half:]], axis=1), centre


def unfold(folded, centre):
    half = folded.shape[0]
    row, column = iota((half, half), 0), iota((half, half), 1)
    turned = folded.T
    mixed, mixed_turned = folded[:, :half], turned[:half]
    first = jnp.where(row < column, mixed, jnp.where(row > column, mixed_turned, centre))
    last = jnp.where(row >= column, mixed, mixed_turned)
    top = jnp.concatenate([first, folded[:, half:]], axis=1)
    return jnp.concatenate([top, jnp.concatenate([turned[half:], last], axis=1)], axis=0)


def pack(square):
    half = square.shape[0] // 2
    return jnp.concatenate([square[:half], square[half:]], axis=1)


def unpack(packed):
    half = packed.shape[1] // 2
    return jnp.concatenate([packed[:, :half], packed[:, half:]], axis=0)


def reach(index, count):
    return (index ^ ((index + 1) % count)).bit_length()


def gram_kernel(basis_ref, out_ref):
    copies = out_ref.shape[0]
    width = basis_ref.shape[1]
    wide = 2 * width
    row = iota((width, wide), 0)
    lane = iota((width, wide), 1)
    column = lane & (width - 1)
    sides = []
    for side in range(2):
        both = jnp.concatenate([basis_ref[side], basis_ref[side + 2]], axis=0)
        crossed = nt(both, both)
        sides.append(jnp.where(lane < width, crossed[:width], crossed[width:]))
    folded = jnp.where(row <= column, sides[0], sides[1])
    diagonal = jnp.sum(jnp.where(row == column, sides[1], 0.0), axis=0, keepdims=True)
    for copy in range(copies):
        out_ref[copy, :width] = folded
        out_ref[copy, width:] = jnp.broadcast_to(diagonal, (8, wide))


def path_kernel(rank_ref, path_ref, high_ref, low_ref):
    heights = path_ref.shape[0]
    row = iota(path_ref.shape[1:], 0)
    for height in range(heights):
        step = jnp.where(row < rank_ref[height], path_ref[height].astype(F32), 0.0)
        if height == 0:
            whole = step
        else:
            step = step.astype(BF16)
            whole = nn(high, step) + nn(low, step)
        high, low = halves(whole)
        high_ref[height] = high
        low_ref[height] = low


def near_kernel(
    rank_ref, place_ref, level_ref, parts_ref, bottom_ref, high_ref, low_ref, left_ref, sent_ref, first_ref, tiles
):
    nodes, width, _ = bottom_ref.shape
    wide = 2 * width
    half = width // 2
    targets = sent_ref.shape[0]
    heights = high_ref.shape[0]
    total = parts_ref[0]
    for part in range(1, parts_ref.shape[0]):
        total = total + parts_ref[part]
    folded = total[:width]
    diagonal = total[width : width + 1]
    turned = folded.T
    row = iota((width, width), 0)
    column = iota((width, width), 1)
    masked = []
    for node in range(nodes):
        pair, side = node // 2, node % 2
        here = folded[:, pair * width : (pair + 1) * width]
        there = turned[pair * width : (pair + 1) * width]
        if side == 0:
            gram = jnp.where(row <= column, here, there)
        else:
            centre = jnp.broadcast_to(diagonal[:, pair * width : (pair + 1) * width], (width, width))
            gram = jnp.where(row > column, here, jnp.where(row < column, there, centre))
        masked.append(keep_rank(gram, rank_ref[node]))
    bottom = halves(lift(masked, [bottom_ref[node] for node in range(nodes)]))
    lane = iota((1, wide), 1)
    lower = jnp.where(lane < width, rank_ref[1], rank_ref[3])
    diagonal = jnp.where((lane & (width - 1)) < lower, diagonal, 0.0)
    tiles[0] = jnp.concatenate([diagonal, jnp.zeros((7, wide), F32)], axis=0)
    parts = parts_ref.shape[0]
    share = half // (2 * parts)
    for height in range(heights):
        path = (high_ref[height], low_ref[height])
        term = product(tn, path, halves(product(nn, bottom, path)))
        if height == 0:
            first_ref[...] = pack(term)
            continue
        square, centre = fold(term)
        packed = pack(square)
        mine = packed[:share]
        for part in range(1, parts):
            mine = jnp.where(level_ref[0] == part, packed[part * share : (part + 1) * share], mine)
        centre = jnp.concatenate([centre, jnp.zeros((1, wide - half), F32)], axis=1)
        tiles[height] = jnp.concatenate([diagonal, mine, centre, jnp.zeros((6 - share, wide), F32)], axis=0)

    row = iota((width, wide), 0)
    lane = iota((width, wide), 1)
    column = lane & (width - 1)
    low = lane < width
    upper = jnp.where(low, rank_ref[0], rank_ref[2])
    lower = jnp.where(low, rank_ref[1], rank_ref[3])
    kept = jnp.maximum(row, column) < jnp.where(row <= column, upper, lower)
    share_rows = jnp.where(kept, folded, 0.0).astype(BF16)
    place = place_ref[0]
    for target in range(targets):
        device = 2 * target + 1
        height = reach(device, 2 * targets)
        inside = jnp.right_shift(place, height) == device >> height
        sent_ref[target, :width] = share_rows
        sent_ref[target, width:] = tiles[jnp.where(inside, height - 1, 0)].astype(BF16)

    row = iota((width, width), 0)
    even_first = jnp.where(row < half, 2 * row, 2 * row - width + 1)
    order = (iota((width, width), 1) == even_first).astype(F32).astype(BF16)
    for node in range(nodes):
        left_ref[node] = nt(nn(order, masked[node].astype(BF16)).astype(BF16), order).astype(BF16)


def sum_kernel(received_ref, out_ref):
    sources, rows, _ = received_ref.shape
    total = received_ref[0, rows - 8 :].astype(F32)
    for source in range(1, sources):
        total = total + received_ref[source, rows - 8 :].astype(F32)
    out_ref[...] = total


def top_kernel(core_ref, received_ref, first_ref, other_ref, out_ref, scratch):
    parts, _, wide = received_ref.shape
    width = wide // 2
    half = width // 2
    share = half // (2 * parts)
    packed = jnp.concatenate([received_ref[part, 1 : 1 + share] for part in range(parts)], axis=0)
    high = unfold(unpack(packed), received_ref[0, 1 + share : 2 + share, :half])
    scratch[...] = jnp.where(core_ref[0] == 1, high, unpack(first_ref[...] + other_ref[...]))
    natural = jnp.concatenate([scratch[pl.ds(side, half, stride=2), :] for side in range(2)], axis=1)
    for tile in range(half):
        out_ref[:, tile * wide : (tile + 1) * wide] = natural[tile : tile + 1]


def project_kernel(
    owner_ref,
    column_ref,
    row_ref,
    core_ref,
    blocks_ref,
    own_ref,
    other_ref,
    left_ref,
    out_ref,
    spread,
    result,
    triangles,
):
    step = pl.program_id(0)
    count, flat = blocks_ref.shape
    width = left_ref.shape[1]
    wide = 2 * width
    tiles = flat // wide
    row = iota((width, wide), 0)
    lane = iota((width, wide), 1)
    column = lane & (width - 1)
    low = lane < width

    @pl.when(step == 0)
    def _():
        triangles[0, 0] = (row <= column).astype(F32)
        triangles[0, 1] = (row < column).astype(F32)
        triangles[0, 2] = jnp.zeros((width, wide), F32)
        triangles[1, 0] = (row > column).astype(F32)
        triangles[1, 1] = (row > column).astype(F32)
        triangles[1, 2] = (row == column).astype(F32)

    for tile in range(tiles):
        spread[tile * count : (tile + 1) * count, :] = blocks_ref[:, tile * wide : (tile + 1) * wide].astype(F32)

    def right_product(index):
        block = step * count + index
        owner = owner_ref[block]
        cluster = column_ref[block]
        pair = jnp.right_shift(cluster, 1)
        side = cluster & 1
        source = jnp.right_shift(owner, 1)
        at_home = (owner & 1) == core_ref[0]
        folded = jnp.where(at_home, own_ref[source, :width], other_ref[source, :width]).astype(F32)
        centre = jnp.where(at_home, own_ref[source, width:], other_ref[source, width:]).astype(F32)[:1]
        wanted = low == (pair == 0)
        folded = jnp.where(wanted, folded, pltpu.roll(folded, width, 1))
        centre = jnp.where(wanted[:1], centre, pltpu.roll(centre, width, 1))
        direct = (folded * triangles[side, 0] + centre * triangles[side, 2]).astype(BF16)
        mirrored = (folded * triangles[side, 1]).astype(BF16)[:, :width]
        here = spread[pl.ds(index, tiles, stride=count), :]
        rows = jnp.concatenate([here, pltpu.roll(here, width, 1)], axis=0).astype(BF16)[:, :width]
        return nn(rows, direct) + nt(rows, jnp.concatenate([mirrored, mirrored], axis=0))

    for first in range(0, count, TOGETHER):
        group = range(first, first + TOGETHER)
        carried = [right_product(index).astype(BF16) for index in group]
        for index, value in zip(group, carried):
            full = nn(left_ref[row_ref[step * count + index]], value)
            result[pl.ds(index, tiles, stride=count), :] = jnp.where(low[:tiles], full[:tiles], full[tiles:])
    for tile in range(tiles):
        out_ref[:, tile * wide : (tile + 1) * wide] = result[tile * count : (tile + 1) * count, :]


def shape(dims, dtype):
    return jax.ShapeDtypeStruct(dims, dtype)


def on_device(
    basis,
    bottom_transfer,
    bottom_rank,
    upper_transfer,
    upper_rank,
    couplings,
    row_cluster,
    column_owner,
    column_cluster,
):
    nodes, width, _ = basis.shape
    wide = 2 * width
    half = width // 2
    branches = lax.axis_size("branch")
    parts = lax.axis_size("level")
    levels = branches.bit_length() - 1
    me_branch = lax.axis_index("branch")
    me_level = lax.axis_index("level")
    core = me_branch & 1
    blk = couplings.shape[0]
    same_core = [list(range(c, branches, 2)) for c in range(2)]
    partners = [(i, i ^ 1) for i in range(branches)]

    partial_sums = pl.pallas_call(
        gram_kernel,
        out_shape=shape((parts, width + 8, wide), F32),
        in_specs=[VMEM],
        out_specs=VMEM,
        compiler_params=SMALL,
        name="gram",
    )(basis)
    partial_sums, upper_transfer, upper_rank, bottom_transfer = lax.optimization_barrier(
        (partial_sums, upper_transfer, upper_rank, bottom_transfer)
    )
    gathered = lax.all_to_all(partial_sums, "level", 0, 0)
    heights = jnp.arange(levels, dtype=jnp.int32)
    slots = 2 * branches - jnp.right_shift(2 * branches, heights) + jnp.right_shift(me_branch, heights)
    path = jnp.take(upper_transfer, slots, axis=0).reshape(levels, width, width)
    path_high, path_low = pl.pallas_call(
        path_kernel,
        out_shape=[shape((levels, width, width), BF16)] * 2,
        in_specs=[SMEM, VMEM],
        out_specs=[VMEM, VMEM],
        compiler_params=SMALL,
        name="path",
    )(jnp.take(upper_rank, slots, axis=0), path)
    left, sent, first = pl.pallas_call(
        near_kernel,
        out_shape=[
            shape((nodes, width, width), BF16),
            shape((branches // 2, width + 8, wide), BF16),
            shape((half, wide), F32),
        ],
        in_specs=[SMEM, SMEM, SMEM, VMEM, VMEM, VMEM, VMEM],
        out_specs=[VMEM, VMEM, VMEM],
        scratch_shapes=[pltpu.VMEM((levels, 8, wide), F32)],
        compiler_params=SMALL,
        name="near",
    )(
        bottom_rank,
        me_branch[None],
        me_level[None],
        gathered,
        bottom_transfer.reshape(nodes, width, width),
        path_high,
        path_low,
    )
    own = lax.all_to_all(sent, "branch", 0, 0, axis_index_groups=same_core)
    first_other = lax.ppermute(first, "branch", partners)
    own, first_other = lax.optimization_barrier((own, first_other))
    summed = pl.pallas_call(
        sum_kernel,
        out_shape=shape((8, wide), F32),
        in_specs=[VMEM],
        out_specs=VMEM,
        compiler_params=SMALL,
        name="sum",
    )(own)
    summed_other = lax.ppermute(summed, "branch", partners)
    other = lax.ppermute(own, "branch", partners)
    quarters = lax.all_to_all(
        jnp.broadcast_to((summed + summed_other)[None], (parts, 8, wide)), "level", 0, 0
    )
    upper_grams = pl.pallas_call(
        top_kernel,
        out_shape=shape((1, width * width), F32),
        in_specs=[SMEM, VMEM, VMEM, VMEM],
        out_specs=VMEM,
        scratch_shapes=[pltpu.VMEM((width, width), F32)],
        compiler_params=SMALL,
        name="top",
    )(core[None], quarters, first, first_other)

    whole = pl.BlockSpec(own.shape, lambda i, *_: (0, 0, 0))
    projected = pl.pallas_call(
        project_kernel,
        out_shape=shape((blk, width * width), F32),
        grid_spec=pltpu.PrefetchScalarGridSpec(
            num_scalar_prefetch=4,
            grid=(blk // ROWS,),
            in_specs=[
                pl.BlockSpec((ROWS, width * width), lambda i, *_: (i, 0)),
                whole,
                whole,
                pl.BlockSpec((nodes, width, width), lambda i, *_: (0, 0, 0)),
            ],
            out_specs=pl.BlockSpec((ROWS, width * width), lambda i, *_: (i, 0)),
            scratch_shapes=[
                pltpu.VMEM((ROWS * half, wide), F32),
                pltpu.VMEM((ROWS * half, wide), F32),
                pltpu.VMEM((2, 3, width, wide), F32),
            ],
        ),
        compiler_params=pltpu.CompilerParams(vmem_limit_bytes=12 * 1024 * 1024),
        name="project",
    )(column_owner[:, 0], column_cluster, row_cluster, core[None], couplings, own, other, left)
    return (upper_grams, projected)


def solution(mesh):
    placed = (
        P("branch", None, "level"),
        P("branch", None),
        P("branch"),
        P(),
        P(),
        P(("branch", "level"), None),
        P(("branch", "level")),
        P(("branch", "level"), None),
        P(("branch", "level")),
    )
    return jax.shard_map(
        on_device,
        mesh=mesh,
        in_specs=placed,
        out_specs=(P("branch", None), P(("branch", "level"), None)),
        check_vma=False,
    )
```

time: 123 us -> 91.1 us (0.74)
  blocking collectives: 16.9 us -> 0 us
  waiting for transfers between devices: 44.8 us -> 30.9 us
  starting transfers between devices: 27.2 us -> 37.3 us
  Pallas kernels: 21.4 us -> 14.9 us
  local copies, waits for them, and re-layouts: 10.7 us -> 6.1 us
    all_to_all x1 -> x0, blocking collectives: 16.9 us -> none  [on_device(): column = lax.all_to_all(shares, 'branch', 0, 0, axis_index_groups=along_z)]
    all_to_all x3 -> x2, waiting for transfers between devices: 39.9 us -> 27.7 us  [the longest x1 23.5 us: on_device(): own = lax.all_to_all(sent, 'branch', 0, 0, axis_index_groups=same_core)]
    ppermute x1 -> x3, starting transfers between devices: 7.31 us -> 12.8 us  [the longest x1 6.56 us: on_device(): other = lax.ppermute(own, 'branch', partners)]
    all_to_all x3 -> x2, starting transfers between devices: 15 us -> 19.7 us  [the longest x1 16.4 us: on_device(): own = lax.all_to_all(sent, 'branch', 0, 0, axis_index_groups=same_core)]
    all_to_all x1, waiting for transfers between devices: 4.91 us -> 1.26 us  [on_device(): gathered = lax.all_to_all(partial_sums, 'level', 0, 0)]
    pallas_call x3, Pallas kernels: 5.82 us -> 2.31 us  [the longest x1 1.33 us: on_device(): pl.pallas_call(path_kernel, out_shape=[shape((levels, width, width), BF16...]
    slice x5 -> x0, local copies, waits for them, and re-layouts: 2.74 us -> none  [the longest x1 1.24 us: on_device(): path_rank[near_levels:]]
    ppermute x1 -> x3, waiting for transfers between devices: 0.01 us -> 1.95 us  [the longest x1 1.13 us: on_device(): summed_other = lax.ppermute(summed, 'branch', partners)]
  transfers between devices with their start and end apart: 5 -> 6, of which waited for: 4 -> 5; matrix products, arithmetic and copies ran while one was open for 4% -> 3% of each run, Pallas kernels for 6% -> 3%
where the time goes in v2:
time: 91.1 us; the launch traced here: 90.1 us
  starting transfers between devices  37.3 us (41%)
  waiting for transfers between devices  30.9 us (34%)
  Pallas kernels  14.9 us (16%)
  local copies, waits for them, and re-layouts  6.1 us (7%)
    all_to_all x1, waiting for transfers between devices, on_device(): own = lax.all_to_all(sent, 'branch', 0, 0, axis_index_groups=same_core)  23.5 us
    all_to_all x1, starting transfers between devices, on_device(): own = lax.all_to_all(sent, 'branch', 0, 0, axis_index_groups=same_core)  16.4 us
    pallas_call x1, Pallas kernels, on_device(): pl.pallas_call(project_kernel, out_shape=shape((blk, width * width), F32)...  10 us
    ppermute x1, starting transfers between devices, on_device(): other = lax.ppermute(own, 'branch', partners)  6.56 us
    all_to_all x1, starting transfers between devices, on_device(): gathered = lax.all_to_all(partial_sums, 'level', 0, 0)  4.84 us
    ppermute x1, starting transfers between devices, on_device(): first_other = lax.ppermute(first, 'branch', partners)  4.29 us
    all_to_all x1, waiting for transfers between devices, on_device(): lax.all_to_all(jnp.broadcast_to((summed + summed_other)[None], (parts, 8,...  4.18 us
    unnamed x18, local copies, waits for them, and re-layouts  3.35 us
  transfers between devices with their start and end apart: 6, of which 5 were waited for; matrix products, arithmetic and copies ran while one was open for 3% of the time, Pallas kernels for 3%

profile of v2, /device:TPU:1, one launch (start us, length us, event | category | flops | bytes accessed | tf_op | source)
XLA Modules:
  0.0 90.1 jit_solution(6839958584551912215)
XLA Ops:
  0.6 0.0 copy-start
  0.6 0.0 copy-start.3
  0.7 1.2 %copy-done.3 = bf16[4,64,1024]{2,1,0:T(8,128)(2,1)S(1)} copy-done((bf16[4,64,1024]{2,1,0:T(8,128)(2,1)S(1)}, bf16[4,64,1024]{2,1,0:T(8,128)(2,1)}, u32[]{:S(2)}) %copy-start.3) | copy-done | bytes 524312
  1.8 0.0 copy-start.8
  1.8 0.0 copy-start.7
  1.8 1.0 %gram.1 = f32[4,72,128]{2,1,0:T(8,128)} custom-call(bf16[4,64,1024]{2,1,0:T(8,128)(2,1)S(1)} %copy-done.3), custom_call_target="tpu_custom_call" | custom-call | tf_op jit(solution)/shard_map/gram/pallas_call | solution.py:309
  2.8 4.8 %all-to-all-start = ((f32[4,72,128]{2,1,0:T(8,128)}), f32[4,72,128]{2,1,0:T(8,128)S(1)}, u32[]{:S(2)}, u32[]{:S(2)}) async-start(f32[4,72,128]{2,1,0:T(8,128)} %gram.1), calls=%async_computation | async-start | bytes 294912 | tf_op jit(solution)/shard_map/all_to_all | solution.py:320
  7.7 1.3 %gather_fusion = s32[7]{0:T(128)S(1)} fusion(s32[254]{0:T(256)} %param.13, s32[1024]{0:T(1024)S(1)} %pad_clamp_fusion), kind=kCustom, calls=%fused_computation | custom fusion | bytes 84 | tf_op jit(solution)/shard_map/jit(_take)/gather | solution.py:331
  9.0 0.0 copy-done
  9.0 0.6 gather_fusion.1
  9.6 0.1 gather.12
  9.7 0.1 broadcast_select_fusion.path_ref
  9.8 0.0 copy-done.8
  9.8 0.1 reshape.47.bottom_ref
  10.0 1.3 %path.1 = (bf16[7,64,64]{2,1,0:T(8,128)(2,1)S(1)}, bf16[7,64,64]{2,1,0:T(8,128)(2,1)S(1)}) custom-call(s32[7]{0:T(128)S(1)} %broadcast_select_fusion.1.rank_ref, bf16[7,64,64]{2,1,0:T(8,128)(2,1)S(1)} %broadcast_select_fusion.path_ref), custom_call_target="tpu_custom_call" | custom-call | tf_op jit(solution)/shard_map/path/pallas_call | solution.py:324
  11.3 1.3 %all-to-all-done.parts_ref = f32[4,72,128]{2,1,0:T(8,128)S(1)} async-done(((f32[4,72,128]{2,1,0:T(8,128)}), f32[4,72,128]{2,1,0:T(8,128)S(1)}, u32[]{:S(2)}, u32[]{:S(2)}) %all-to-all-start) | async-done | bytes 147488 | tf_op jit(solution)/shard_map/all_to_all | solution.py:320
  12.6 0.0 copy-done.7
  12.6 1.6 %near.1 = (bf16[4,64,64]{2,1,0:T(8,128)(2,1)S(1)}, bf16[64,72,128]{2,1,0:T(8,128)(2,1)S(1)}, f32[32,128]{1,0:T(8,128)S(1)}) custom-call(s32[4]{0:T(128)S(1)} %copy-done.7, s32[1]{0:T(128)} %bitcast.1.place_ref, s32[1]{0:T(128)} %bitcast.2.level_ref, f32[4,72,128]{2,1,0:T(8,128)S(1)} %all-to-all-done.parts_ref, bf16[4,64,64]{2,1,0:T(8,128)(2,1)S(1)} %reshape.47.bottom_ref, ...), custom_call_target="tpu_custom_call" | custom-call | tf_op jit(solution)/shard_map/near/pallas_call | solution.py:332
  14.1 0.0 copy-start.1
  14.2 1.0 %copy-done.1 = bf16[64,72,128]{2,1,0:T(8,128)(2,1)} copy-done((bf16[64,72,128]{2,1,0:T(8,128)(2,1)}, bf16[64,72,128]{2,1,0:T(8,128)(2,1)S(1)}, u32[]{:S(2)}) %copy-start.1) | copy-done | bytes 1179672
  15.2 0.0 copy-start.4
  15.2 0.0 copy-start.5
  15.2 0.0 copy-start.6
  15.2 16.4 %all-to-all-start.1 = ((bf16[64,72,128]{2,1,0:T(8,128)(2,1)}), bf16[64,72,128]{2,1,0:T(8,128)(2,1)S(1)}, u32[]{:S(2)}, u32[]{:S(2)}) async-start(bf16[64,72,128]{2,1,0:T(8,128)(2,1)} %copy-done.1), calls=%async_computation.1 | async-start | bytes 2359296 | tf_op jit(solution)/shard_map/all_to_all | solution.py:353
  31.6 4.3 %collective-permute-start = (f32[32,128]{1,0:T(8,128)S(1)}, f32[32,128]{1,0:T(8,128)S(1)}, u32[]{:S(2)}, u32[]{:S(2)}) collective-permute-start(f32[32,128]{1,0:T(8,128)S(1)} %get-tuple-element.20.first_ref), channel_id=1, source_target_pairs={{0,4},{4,0},{8,12},{12,8},{16,20},{20,16},{24,28},{28,24},{32,36},... | collective-permute-start | bytes 49160 | tf_op jit(solution)/shard_map/ppermute | solution.py:354
  35.9 0.8 collective-permute-done.other_ref
  36.7 23.5 %all-to-all-done.1.received_ref.own_ref = bf16[64,72,128]{2,1,0:T(8,128)(2,1)S(1)} async-done(((bf16[64,72,128]{2,1,0:T(8,128)(2,1)}), bf16[64,72,128]{2,1,0:T(8,128)(2,1)S(1)}, u32[]{:S(2)}, u32[]{:S(2)}) %all-to-all-start.1) | async-done | bytes 1179680 | tf_op jit(solution)/shard_map/all_to_all | solution.py:353
  60.2 6.6 %collective-permute-start.2 = (bf16[64,72,128]{2,1,0:T(8,128)(2,1)S(1)}, bf16[64,72,128]{2,1,0:T(8,128)(2,1)}, u32[]{:S(2)}, u32[]{:S(2)}) collective-permute-start(bf16[64,72,128]{2,1,0:T(8,128)(2,1)S(1)} %all-to-all-done.1.received_ref.own_ref), channel_id=1, source_target_pairs={{0,4},{4,0},{8,12},{12,8},{16,20},{20,16},{24,28},{28,24},{32,36},... | collective-permute-start | bytes 3538952 | tf_op jit(solution)/shard_map/ppermute | solution.py:365
  66.8 0.1 sum.1
  66.9 1.9 %collective-permute-start.1 = (f32[8,128]{1,0:T(8,128)S(1)}, f32[8,128]{1,0:T(8,128)S(1)}, u32[]{:S(2)}, u32[]{:S(2)}) collective-permute-start(f32[8,128]{1,0:T(8,128)S(1)} %sum.1), channel_id=1, source_target_pairs={{0,4},{4,0},{8,12},{12,8},{16,20},{20,16},{24,28},{28,24},{32,36},... | collective-permute-start | bytes 12296 | tf_op jit(solution)/shard_map/ppermute | solution.py:364
  68.8 1.1 %collective-permute-done.1 = f32[8,128]{1,0:T(8,128)S(1)} collective-permute-done((f32[8,128]{1,0:T(8,128)S(1)}, f32[8,128]{1,0:T(8,128)S(1)}, u32[]{:S(2)}, u32[]{:S(2)}) %collective-permute-start.1) | collective-permute-done | bytes 4128 | tf_op jit(solution)/shard_map/ppermute | solution.py:364
  69.9 0.6 broadcast_in_dim.33
  70.6 3.3 %all-to-all-start.2 = ((f32[4,8,128]{2,1,0:T(8,128)}), f32[4,8,128]{2,1,0:T(8,128)S(1)}, u32[]{:S(2)}, u32[]{:S(2)}) async-start(f32[4,8,128]{2,1,0:T(8,128)} %broadcast_in_dim.33), calls=%async_computation.2 | async-start | bytes 32768 | tf_op jit(solution)/shard_map/all_to_all | solution.py:366
  73.8 4.2 %all-to-all-done.2.received_ref = f32[4,8,128]{2,1,0:T(8,128)S(1)} async-done(((f32[4,8,128]{2,1,0:T(8,128)}), f32[4,8,128]{2,1,0:T(8,128)S(1)}, u32[]{:S(2)}, u32[]{:S(2)}) %all-to-all-start.2) | async-done | bytes 16416 | tf_op jit(solution)/shard_map/all_to_all | solution.py:366
  78.0 0.9 %top.1 = f32[1,4096]{1,0:T(1,128)} custom-call(s32[1]{0:T(128)} %bitcast.core_ref, f32[4,8,128]{2,1,0:T(8,128)S(1)} %all-to-all-done.2.received_ref, f32[32,128]{1,0:T(8,128)S(1)} %get-tuple-element.20.first_ref, f32[32,128]{1,0:T(8,128)S(1)} %collective-permute-done.other_ref), custom_call_target="tpu_custom_call" | custom-call | tf_op jit(solution)/shard_map/top/pallas_call | solution.py:369
  78.9 0.0 collective-permute-done.2.other_ref
  78.9 0.0 copy-done.4
  78.9 0.0 copy-done.5
  78.9 0.0 copy-done.6
  78.9 0.0 copy-start.2
  78.9 1.1 %copy-done.2 = bf16[96,4096]{1,0:T(8,128)(2,1)S(1)} copy-done((bf16[96,4096]{1,0:T(8,128)(2,1)S(1)}, bf16[96,4096]{1,0:T(8,128)(2,1)}, u32[]{:S(2)}) %copy-start.2) | copy-done | bytes 786456
  80.1 10.0 %project.1 = f32[96,4096]{1,0:T(8,128)} custom-call(s32[96]{0:T(128)S(1)} %bitcast.6, s32[96]{0:T(128)S(1)} %copy-done.5, s32[96]{0:T(128)S(1)} %copy-done.6, s32[1]{0:T(128)} %bitcast.core_ref, bf16[96,4096]{1,0:T(8,128)(2,1)S(1)} %copy-done.2, bf16[64,72,128]{2,1,0:T(8,128)(2,1)S(1)} %all-to-all-done.1.received_ref.own_ref, ...), custom_call_target="tpu_custom_call" | custom-call | tf_op jit(solution)/shard_map/project/pallas_call | solution.py:380
  (5 shorter events, 0.0 us)
Async XLA Ops:
  0.6 8.4 %copy-start = (bf16[254,4096]{1,0:T(8,128)(2,1)S(1)}, bf16[254,4096]{1,0:T(8,128)(2,1)}, u32[]{:S(2)}) copy-start(bf16[254,4096]{1,0:T(8,128)(2,1)} %param.12) | copy-start | bytes 6242308
  0.6 1.2 %copy-start.3 = (bf16[4,64,1024]{2,1,0:T(8,128)(2,1)S(1)}, bf16[4,64,1024]{2,1,0:T(8,128)(2,1)}, u32[]{:S(2)}) copy-start(bf16[4,64,1024]{2,1,0:T(8,128)(2,1)} %basis_ref.1) | copy-start | bytes 1572868
  1.8 8.0 %copy-start.8 = (bf16[4,4096]{1,0:T(4,128)(2,1)S(1)}, bf16[4,4096]{1,0:T(4,128)(2,1)}, u32[]{:S(2)}) copy-start(bf16[4,4096]{1,0:T(4,128)(2,1)} %param.10) | copy-start | bytes 98308
  1.8 10.7 %copy-start.7 = (s32[4]{0:T(128)S(1)}, s32[4]{0:T(128)}, u32[]{:S(2)}) copy-start(s32[4]{0:T(128)} %rank_ref.1) | copy-start | bytes 52
  2.8 9.8 %all-to-all-start = ((f32[4,72,128]{2,1,0:T(8,128)}), f32[4,72,128]{2,1,0:T(8,128)S(1)}, u32[]{:S(2)}, u32[]{:S(2)}) async-start(f32[4,72,128]{2,1,0:T(8,128)} %gram.1), calls=%async_computation | async-start | bytes 294912 | tf_op jit(solution)/shard_map/all_to_all | solution.py:320
  14.1 1.0 %copy-start.1 = (bf16[64,72,128]{2,1,0:T(8,128)(2,1)}, bf16[64,72,128]{2,1,0:T(8,128)(2,1)S(1)}, u32[]{:S(2)}) copy-start(bf16[64,72,128]{2,1,0:T(8,128)(2,1)S(1)} %get-tuple-element.19) | copy-start | bytes 3538948
  15.2 63.7 %copy-start.4 = (s32[96,1]{0,1:T(1,128)S(1)}, s32[96,1]{0,1:T(1,128)}, u32[]{:S(2)}) copy-start(s32[96,1]{0,1:T(1,128)} %param.16) | copy-start | bytes 1156
  15.2 63.7 %copy-start.5 = (s32[96]{0:T(128)S(1)}, s32[96]{0:T(128)}, u32[]{:S(2)}) copy-start(s32[96]{0:T(128)} %column_ref.1) | copy-start | bytes 1156
  15.2 63.7 %copy-start.6 = (s32[96]{0:T(128)S(1)}, s32[96]{0:T(128)}, u32[]{:S(2)}) copy-start(s32[96]{0:T(128)} %row_ref.1) | copy-start | bytes 1156
  15.2 45.1 %all-to-all-start.1 = ((bf16[64,72,128]{2,1,0:T(8,128)(2,1)}), bf16[64,72,128]{2,1,0:T(8,128)(2,1)S(1)}, u32[]{:S(2)}, u32[]{:S(2)}) async-start(bf16[64,72,128]{2,1,0:T(8,128)(2,1)} %copy-done.1), calls=%async_computation.1 | async-start | bytes 2359296 | tf_op jit(solution)/shard_map/all_to_all | solution.py:353
  31.6 5.1 %collective-permute-start = (f32[32,128]{1,0:T(8,128)S(1)}, f32[32,128]{1,0:T(8,128)S(1)}, u32[]{:S(2)}, u32[]{:S(2)}) collective-permute-start(f32[32,128]{1,0:T(8,128)S(1)} %get-tuple-element.20.first_ref), channel_id=1, source_target_pairs={{0,4},{4,0},{8,12},{12,8},{16,20},{20,16},{24,28},{28,24},{32,36},... | collective-permute-start | bytes 49160 | tf_op jit(solution)/shard_map/ppermute | solution.py:354
  60.2 18.7 %collective-permute-start.2 = (bf16[64,72,128]{2,1,0:T(8,128)(2,1)S(1)}, bf16[64,72,128]{2,1,0:T(8,128)(2,1)}, u32[]{:S(2)}, u32[]{:S(2)}) collective-permute-start(bf16[64,72,128]{2,1,0:T(8,128)(2,1)S(1)} %all-to-all-done.1.received_ref.own_ref), channel_id=1, source_target_pairs={{0,4},{4,0},{8,12},{12,8},{16,20},{20,16},{24,28},{28,24},{32,36},... | collective-permute-start | bytes 3538952 | tf_op jit(solution)/shard_map/ppermute | solution.py:365
  66.9 3.1 %collective-permute-start.1 = (f32[8,128]{1,0:T(8,128)S(1)}, f32[8,128]{1,0:T(8,128)S(1)}, u32[]{:S(2)}, u32[]{:S(2)}) collective-permute-start(f32[8,128]{1,0:T(8,128)S(1)} %sum.1), channel_id=1, source_target_pairs={{0,4},{4,0},{8,12},{12,8},{16,20},{20,16},{24,28},{28,24},{32,36},... | collective-permute-start | bytes 12296 | tf_op jit(solution)/shard_map/ppermute | solution.py:364
  70.6 7.4 %all-to-all-start.2 = ((f32[4,8,128]{2,1,0:T(8,128)}), f32[4,8,128]{2,1,0:T(8,128)S(1)}, u32[]{:S(2)}, u32[]{:S(2)}) async-start(f32[4,8,128]{2,1,0:T(8,128)} %broadcast_in_dim.33), calls=%async_computation.2 | async-start | bytes 32768 | tf_op jit(solution)/shard_map/all_to_all | solution.py:366
  78.9 1.1 %copy-start.2 = (bf16[96,4096]{1,0:T(8,128)(2,1)S(1)}, bf16[96,4096]{1,0:T(8,128)(2,1)}, u32[]{:S(2)}) copy-start(bf16[96,4096]{1,0:T(8,128)(2,1)} %blocks_ref.1) | copy-start | bytes 2359300

commit v3 on v2

--- a/solution.py
+++ b/solution.py
@@ -9,7 +9,6 @@
 SMEM = pl.BlockSpec(memory_space=pltpu.SMEM)
 SMALL = pltpu.CompilerParams(vmem_limit_bytes=8 * 1024 * 1024)
 ROWS = 16
-TOGETHER = 4
 F32 = jnp.float32
 BF16 = jnp.bfloat16
 
@@ -197,83 +196,83 @@
     total = received_ref[0, rows - 8 :].astype(F32)
     for source in range(1, sources):
         total = total + received_ref[source, rows - 8 :].astype(F32)
-    out_ref[...] = total
+    for copy in range(out_ref.shape[0]):
+        out_ref[copy] = total
 
 
 def top_kernel(core_ref, received_ref, first_ref, other_ref, out_ref, scratch):
-    parts, _, wide = received_ref.shape
+    parts = received_ref.shape[0] // 2
+    wide = received_ref.shape[2]
     width = wide // 2
     half = width // 2
     share = half // (2 * parts)
-    packed = jnp.concatenate([received_ref[part, 1 : 1 + share] for part in range(parts)], axis=0)
-    high = unfold(unpack(packed), received_ref[0, 1 + share : 2 + share, :half])
+    sums = [received_ref[part] + received_ref[parts + part] for part in range(parts)]
+    packed = jnp.concatenate([value[1 : 1 + share] for value in sums], axis=0)
+    high = unfold(unpack(packed), sums[0][1 + share : 2 + share, :half])
     scratch[...] = jnp.where(core_ref[0] == 1, high, unpack(first_ref[...] + other_ref[...]))
     natural = jnp.concatenate([scratch[pl.ds(side, half, stride=2), :] for side in range(2)], axis=1)
     for tile in range(half):
         out_ref[:, tile * wide : (tile + 1) * wide] = natural[tile : tile + 1]
 
 
-def project_kernel(
-    owner_ref,
-    column_ref,
-    row_ref,
-    core_ref,
-    blocks_ref,
-    own_ref,
-    other_ref,
-    left_ref,
-    out_ref,
-    spread,
-    result,
-    triangles,
-):
+def left_kernel(row_ref, column_ref, blocks_ref, left_ref, out_ref, spread):
     step = pl.program_id(0)
     count, flat = blocks_ref.shape
     width = left_ref.shape[1]
     wide = 2 * width
     tiles = flat // wide
-    row = iota((width, wide), 0)
-    lane = iota((width, wide), 1)
-    column = lane & (width - 1)
-    low = lane < width
+    low = iota((width, wide), 1) < width
+    for tile in range(tiles):
+        spread[tile * count : (tile + 1) * count, :] = blocks_ref[:, tile * wide : (tile + 1) * wide].astype(F32)
+    for index in range(count):
+        block = step * count + index
+        here = spread[pl.ds(index, tiles, stride=count), :]
+        turned = pltpu.roll(here, width, 1)
+        rows = jnp.where(
+            low, jnp.concatenate([here, turned], axis=0), jnp.concatenate([turned, here], axis=0)
+        ).astype(BF16)
+        product = nn(left_ref[row_ref[block]], rows)
+        out_ref[index] = jnp.where(low == (column_ref[block] < 2), product, 0.0).astype(BF16)
+
+
+def project_kernel(
+    owner_ref, column_ref, core_ref, rows_ref, own_ref, other_ref, out_ref, result, triangles
+):
+    step = pl.program_id(0)
+    count, width, wide = rows_ref.shape
+    tiles = width // 2
+    low = iota((tiles, wide), 1) < width
 
     @pl.when(step == 0)
     def _():
-        triangles[0, 0] = (row <= column).astype(F32)
-        triangles[0, 1] = (row < column).astype(F32)
-        triangles[0, 2] = jnp.zeros((width, wide), F32)
-        triangles[1, 0] = (row > column).astype(F32)
-        triangles[1, 1] = (row > column).astype(F32)
-        triangles[1, 2] = (row == column).astype(F32)
-
-    for tile in range(tiles):
-        spread[tile * count : (tile + 1) * count, :] = blocks_ref[:, tile * wide : (tile + 1) * wide].astype(F32)
-
-    def right_product(index):
+        row = iota((width, wide), 0)
+        column = iota((width, wide), 1) & (width - 1)
+        triangles[0, 0] = (row <= column).astype(F32).astype(BF16)
+        triangles[0, 1] = (row < column).astype(F32).astype(BF16)
+        triangles[0, 2] = jnp.zeros((width, wide), BF16)
+        triangles[1, 0] = (row > column).astype(F32).astype(BF16)
+        triangles[1, 1] = (row > column).astype(F32).astype(BF16)
+        triangles[1, 2] = (row == column).astype(F32).astype(BF16)
+
+    for index in range(count):
         block = step * count + index
         owner = owner_ref[block]
         cluster = column_ref[block]
-        pair = jnp.right_shift(cluster, 1)
+        first = cluster < 2
         side = cluster & 1
         source = jnp.right_shift(owner, 1)
         at_home = (owner & 1) == core_ref[0]
-        folded = jnp.where(at_home, own_ref[source, :width], other_ref[source, :width]).astype(F32)
-        centre = jnp.where(at_home, own_ref[source, width:], other_ref[source, width:]).astype(F32)[:1]
-        wanted = low == (pair == 0)
-        folded = jnp.where(wanted, folded, pltpu.roll(folded, width, 1))
-        centre = jnp.where(wanted[:1], centre, pltpu.roll(centre, width, 1))
-        direct = (folded * triangles[side, 0] + centre * triangles[side, 2]).astype(BF16)
-        mirrored = (folded * triangles[side, 1]).astype(BF16)[:, :width]
-        here = spread[pl.ds(index, tiles, stride=count), :]
-        rows = jnp.concatenate([here, pltpu.roll(here, width, 1)], axis=0).astype(BF16)[:, :width]
-        return nn(rows, direct) + nt(rows, jnp.concatenate([mirrored, mirrored], axis=0))
-
-    for first in range(0, count, TOGETHER):
-        group = range(first, first + TOGETHER)
-        carried = [right_product(index).astype(BF16) for index in group]
-        for index, value in zip(group, carried):
-            full = nn(left_ref[row_ref[step * count + index]], value)
-            result[pl.ds(index, tiles, stride=count), :] = jnp.where(low[:tiles], full[:tiles], full[tiles:])
+        folded = jnp.where(at_home, own_ref[source, :width], other_ref[source, :width])
+        centre = jnp.where(at_home, own_ref[source, width:], other_ref[source, width:])[:1]
+        direct = folded * triangles[side, 0] + centre * triangles[side, 2]
+        mirrored = folded * triangles[side, 1]
+        rows = rows_ref[index]
+        full = nn(rows, jnp.concatenate([direct, direct], axis=0))
+        full = full + nt(rows, jnp.concatenate([mirrored, mirrored], axis=0))
+        top, bottom = full[:tiles], full[tiles:]
+        stay = jnp.where(first, top, bottom)
+        move = pltpu.roll(jnp.where(first, bottom, top), width, 1)
+        result[pl.ds(index, tiles, stride=count), :] = jnp.where(low == first, stay, move)
     for tile in range(tiles):
         out_ref[:, tile * wide : (tile + 1) * wide] = result[tile * count : (tile + 1) * count, :]
 
@@ -304,6 +303,7 @@
     core = me_branch & 1
     blk = couplings.shape[0]
     same_core = [list(range(c, branches, 2)) for c in range(2)]
+    same_chip = [list(range(2 * parts * chip, 2 * parts * (chip + 1))) for chip in range(branches // 2)]
     partners = [(i, i ^ 1) for i in range(branches)]
 
     partial_sums = pl.pallas_call(
@@ -352,20 +352,59 @@
     )
     own = lax.all_to_all(sent, "branch", 0, 0, axis_index_groups=same_core)
     first_other = lax.ppermute(first, "branch", partners)
-    own, first_other = lax.optimization_barrier((own, first_other))
+    square = pl.BlockSpec((ROWS, width, wide), lambda i, *_: (i, 0, 0))
+    rows = pl.pallas_call(
+        left_kernel,
+        out_shape=shape((blk, width, wide), BF16),
+        grid_spec=pltpu.PrefetchScalarGridSpec(
+            num_scalar_prefetch=2,
+            grid=(blk // ROWS,),
+            in_specs=[
+                pl.BlockSpec((ROWS, width * width), lambda i, *_: (i, 0)),
+                pl.BlockSpec((nodes, width, width), lambda i, *_: (0, 0, 0)),
+            ],
+            out_specs=square,
+            scratch_shapes=[pltpu.VMEM((ROWS * half, wide), F32)],
+        ),
+        compiler_params=SMALL,
+        cost_estimate=pl.CostEstimate(
+            flops=4 * blk * width**3, bytes_accessed=4 * blk * width * width, transcendentals=0
+        ),
+        name="left",
+    )(row_cluster, column_cluster, couplings, left)
+    own, first_other, rows = lax.optimization_barrier((own, first_other, rows))
     summed = pl.pallas_call(
         sum_kernel,
-        out_shape=shape((8, wide), F32),
+        out_shape=shape((2 * parts, 8, wide), F32),
         in_specs=[VMEM],
         out_specs=VMEM,
         compiler_params=SMALL,
         name="sum",
     )(own)
-    summed_other = lax.ppermute(summed, "branch", partners)
     other = lax.ppermute(own, "branch", partners)
-    quarters = lax.all_to_all(
-        jnp.broadcast_to((summed + summed_other)[None], (parts, 8, wide)), "level", 0, 0
-    )
+    quarters = lax.all_to_all(summed, ("branch", "level"), 0, 0, axis_index_groups=same_chip)
+
+    whole = pl.BlockSpec(own.shape, lambda i, *_: (0, 0, 0))
+    projected = pl.pallas_call(
+        project_kernel,
+        out_shape=shape((blk, width * width), F32),
+        grid_spec=pltpu.PrefetchScalarGridSpec(
+            num_scalar_prefetch=3,
+            grid=(blk // ROWS,),
+            in_specs=[square, whole, whole],
+            out_specs=pl.BlockSpec((ROWS, width * width), lambda i, *_: (i, 0)),
+            scratch_shapes=[
+                pltpu.VMEM((ROWS * half, wide), F32),
+                pltpu.VMEM((2, 3, width, wide), BF16),
+            ],
+        ),
+        compiler_params=pltpu.CompilerParams(vmem_limit_bytes=56 * 1024 * 1024),
+        cost_estimate=pl.CostEstimate(
+            flops=8 * blk * width**3, bytes_accessed=6 * blk * width * width, transcendentals=0
+        ),
+        name="project",
+    )(column_owner[:, 0], column_cluster, core[None], rows, own, other)
+    projected, quarters = lax.optimization_barrier((projected, quarters))
     upper_grams = pl.pallas_call(
         top_kernel,
         out_shape=shape((1, width * width), F32),
@@ -375,30 +414,6 @@
         compiler_params=SMALL,
         name="top",
     )(core[None], quarters, first, first_other)
-
-    whole = pl.BlockSpec(own.shape, lambda i, *_: (0, 0, 0))
-    projected = pl.pallas_call(
-        project_kernel,
-        out_shape=shape((blk, width * width), F32),
-        grid_spec=pltpu.PrefetchScalarGridSpec(
-            num_scalar_prefetch=4,
-            grid=(blk // ROWS,),
-            in_specs=[
-                pl.BlockSpec((ROWS, width * width), lambda i, *_: (i, 0)),
-                whole,
-                whole,
-                pl.BlockSpec((nodes, width, width), lambda i, *_: (0, 0, 0)),
-            ],
-            out_specs=pl.BlockSpec((ROWS, width * width), lambda i, *_: (i, 0)),
-            scratch_shapes=[
-                pltpu.VMEM((ROWS * half, wide), F32),
-                pltpu.VMEM((ROWS * half, wide), F32),
-                pltpu.VMEM((2, 3, width, wide), F32),
-            ],
-        ),
-        compiler_params=pltpu.CompilerParams(vmem_limit_bytes=12 * 1024 * 1024),
-        name="project",
-    )(column_owner[:, 0], column_cluster, row_cluster, core[None], couplings, own, other, left)
     return (upper_grams, projected)
 
 

time: 91.1 us -> 80.5 us (0.88)
  waiting for transfers between devices: 30.9 us -> 21.5 us
  starting transfers between devices: 37.3 us -> 35.3 us
  Pallas kernels: 14.9 us -> 16.2 us
    all_to_all x1, waiting for transfers between devices: 4.18 us -> 0.01 us  [on_device(): lax.all_to_all(summed, ('branch', 'level'), 0, 0, axis_index_groups=same_...]
    all_to_all x1, waiting for transfers between devices: 23.5 us -> 19.6 us  [on_device(): own = lax.all_to_all(sent, 'branch', 0, 0, axis_index_groups=same_core)]
    pallas_call x1 -> x2, Pallas kernels: 0.07 us -> 3.11 us  [the longest x1 2.43 us: on_device(): pl.pallas_call(left_kernel, out_shape=shape((blk, width, wide), BF16), gr...]
    ppermute x1 -> x0, starting transfers between devices: 1.91 us -> none  [on_device(): summed_other = lax.ppermute(summed, 'branch', partners)]
    pallas_call x1, Pallas kernels: 10 us -> 8.28 us  [on_device(): pl.pallas_call(project_kernel, out_shape=shape((blk, width * width), F32)...]
    unnamed x18 -> x22, local copies, waits for them, and re-layouts: 3.35 us -> 4.52 us
    ppermute x1 -> x0, waiting for transfers between devices: 1.13 us -> none  [on_device(): summed_other = lax.ppermute(summed, 'branch', partners)]
  transfers between devices with their start and end apart: 6 -> 5, of which waited for: 5 -> 2; matrix products, arithmetic and copies ran while one was open for 3% -> 2% of each run, Pallas kernels for 3% -> 16%
where the time goes in v3:
time: 80.5 us; the launch traced here: 79.8 us
  starting transfers between devices  35.3 us (44%)
  waiting for transfers between devices  21.5 us (27%)
  Pallas kernels  16.2 us (20%)
  local copies, waits for them, and re-layouts  5.98 us (7%)
  between operations  0.84 us (1%)
    all_to_all x1, waiting for transfers between devices, on_device(): own = lax.all_to_all(sent, 'branch', 0, 0, axis_index_groups=same_core)  19.6 us
    all_to_all x1, starting transfers between devices, on_device(): own = lax.all_to_all(sent, 'branch', 0, 0, axis_index_groups=same_core)  16.3 us
    pallas_call x1, Pallas kernels, on_device(): pl.pallas_call(project_kernel, out_shape=shape((blk, width * width), F32)...  8.28 us
    ppermute x1, starting transfers between devices, on_device(): other = lax.ppermute(own, 'branch', partners)  6.56 us
    all_to_all x1, starting transfers between devices, on_device(): gathered = lax.all_to_all(partial_sums, 'level', 0, 0)  4.84 us
    unnamed x22, local copies, waits for them, and re-layouts  4.52 us
    ppermute x1, starting transfers between devices, on_device(): first_other = lax.ppermute(first, 'branch', partners)  4.29 us
    all_to_all x1, starting transfers between devices, on_device(): lax.all_to_all(summed, ('branch', 'level'), 0, 0, axis_index_groups=same_...  3.28 us
  transfers between devices with their start and end apart: 5, of which 2 were waited for; matrix products, arithmetic and copies ran while one was open for 2% of the time, Pallas kernels for 16%

profile of v3, /device:TPU:1, one launch (start us, length us, event | category | flops | bytes accessed | tf_op | source)
XLA Modules:
  0.0 79.8 jit_solution(10729148307795665442)
XLA Ops:
  0.6 0.0 copy-start
  0.6 0.0 copy-start.5
  0.7 1.2 %copy-done.5 = bf16[4,64,1024]{2,1,0:T(8,128)(2,1)S(1)} copy-done((bf16[4,64,1024]{2,1,0:T(8,128)(2,1)S(1)}, bf16[4,64,1024]{2,1,0:T(8,128)(2,1)}, u32[]{:S(2)}) %copy-start.5) | copy-done | bytes 524312
  1.8 0.0 copy-start.9
  1.8 0.0 copy-start.10
  1.8 0.0 copy-start.8
  1.8 1.0 %gram.1 = f32[4,72,128]{2,1,0:T(8,128)} custom-call(bf16[4,64,1024]{2,1,0:T(8,128)(2,1)S(1)} %copy-done.5), custom_call_target="tpu_custom_call" | custom-call | tf_op jit(solution)/shard_map/gram/pallas_call | solution.py:309
  2.8 4.8 %all-to-all-start = ((f32[4,72,128]{2,1,0:T(8,128)}), f32[4,72,128]{2,1,0:T(8,128)S(1)}, u32[]{:S(2)}, u32[]{:S(2)}) async-start(f32[4,72,128]{2,1,0:T(8,128)} %gram.1), calls=%async_computation | async-start | bytes 294912 | tf_op jit(solution)/shard_map/all_to_all | solution.py:320
  7.7 0.0 copy-done
  7.7 0.6 gather_fusion.1
  8.3 0.1 gather.12
  8.4 0.0 copy-done.9
  8.4 0.6 gather_fusion
  9.1 0.1 broadcast_select_fusion.path_ref
  9.2 0.0 copy-start.6
  9.2 0.0 copy-start.7
  9.2 0.0 copy-done.10
  9.2 0.1 reshape.46.bottom_ref
  9.3 1.3 %path.1 = (bf16[7,64,64]{2,1,0:T(8,128)(2,1)S(1)}, bf16[7,64,64]{2,1,0:T(8,128)(2,1)S(1)}) custom-call(s32[7]{0:T(128)S(1)} %broadcast_select_fusion.1.rank_ref, bf16[7,64,64]{2,1,0:T(8,128)(2,1)S(1)} %broadcast_select_fusion.path_ref), custom_call_target="tpu_custom_call" | custom-call | tf_op jit(solution)/shard_map/path/pallas_call | solution.py:324
  10.7 1.9 %all-to-all-done.parts_ref = f32[4,72,128]{2,1,0:T(8,128)S(1)} async-done(((f32[4,72,128]{2,1,0:T(8,128)}), f32[4,72,128]{2,1,0:T(8,128)S(1)}, u32[]{:S(2)}, u32[]{:S(2)}) %all-to-all-start) | async-done | bytes 147488 | tf_op jit(solution)/shard_map/all_to_all | solution.py:320
  12.6 0.0 copy-done.8
  12.6 1.6 %near.1 = (bf16[4,64,64]{2,1,0:T(8,128)(2,1)S(1)}, bf16[64,72,128]{2,1,0:T(8,128)(2,1)S(1)}, f32[32,128]{1,0:T(8,128)S(1)}) custom-call(s32[4]{0:T(128)S(1)} %copy-done.8, s32[1]{0:T(128)} %bitcast.2.place_ref, s32[1]{0:T(128)} %bitcast.3.level_ref, f32[4,72,128]{2,1,0:T(8,128)S(1)} %all-to-all-done.parts_ref, bf16[4,64,64]{2,1,0:T(8,128)(2,1)S(1)} %reshape.46.bottom_ref, ...), custom_call_target="tpu_custom_call" | custom-call | tf_op jit(solution)/shard_map/near/pallas_call | solution.py:332
  14.1 0.0 copy-start.3
  14.2 1.0 %copy-done.3 = bf16[64,72,128]{2,1,0:T(8,128)(2,1)} copy-done((bf16[64,72,128]{2,1,0:T(8,128)(2,1)}, bf16[64,72,128]{2,1,0:T(8,128)(2,1)S(1)}, u32[]{:S(2)}) %copy-start.3) | copy-done | bytes 1179672
  15.2 16.3 %all-to-all-start.1 = ((bf16[64,72,128]{2,1,0:T(8,128)(2,1)}), bf16[64,72,128]{2,1,0:T(8,128)(2,1)S(1)}, u32[]{:S(2)}, u32[]{:S(2)}) async-start(bf16[64,72,128]{2,1,0:T(8,128)(2,1)} %copy-done.3), calls=%async_computation.1 | async-start | bytes 2359296 | tf_op jit(solution)/shard_map/all_to_all | solution.py:353
  31.5 4.3 %collective-permute-start = (f32[32,128]{1,0:T(8,128)S(1)}, f32[32,128]{1,0:T(8,128)S(1)}, u32[]{:S(2)}, u32[]{:S(2)}) collective-permute-start(f32[32,128]{1,0:T(8,128)S(1)} %get-tuple-element.23.first_ref), channel_id=1, source_target_pairs={{0,4},{4,0},{8,12},{12,8},{16,20},{20,16},{24,28},{28,24},{32,36},... | collective-permute-start | bytes 49160 | tf_op jit(solution)/shard_map/ppermute | solution.py:354
  35.8 0.0 copy-done.6
  35.8 0.0 copy-done.7
  35.8 0.0 copy-start.4
  35.8 1.1 %copy-done.4 = bf16[96,4096]{1,0:T(8,128)(2,1)S(1)} copy-done((bf16[96,4096]{1,0:T(8,128)(2,1)S(1)}, bf16[96,4096]{1,0:T(8,128)(2,1)}, u32[]{:S(2)}) %copy-start.4) | copy-done | bytes 786456
  36.9 2.4 %left.1.rows_ref = bf16[96,64,128]{2,1,0:T(8,128)(2,1)S(1)} custom-call(s32[96]{0:T(128)S(1)} %copy-done.7, s32[96]{0:T(128)S(1)} %copy-done.6, bf16[96,4096]{1,0:T(8,128)(2,1)S(1)} %copy-done.4, bf16[4,64,64]{2,1,0:T(8,128)(2,1)S(1)} %get-tuple-element.24.left_ref), custom_call_target="tpu_custom_call" | custom-call | flops 100663296 | bytes 1572864 | tf_op jit(solution)/shard_map/left/pallas_call | solution.py:356
  39.4 0.0 copy-start.2
  39.4 1.2 %copy-done.2 = bf16[96,64,128]{2,1,0:T(8,128)(2,1)} copy-done((bf16[96,64,128]{2,1,0:T(8,128)(2,1)}, bf16[96,64,128]{2,1,0:T(8,128)(2,1)S(1)}, u32[]{:S(2)}) %copy-start.2) | copy-done | bytes 1572888
  40.6 0.0 collective-permute-done.other_ref
  40.6 19.6 %all-to-all-done.1.own_ref.received_ref = bf16[64,72,128]{2,1,0:T(8,128)(2,1)S(1)} async-done(((bf16[64,72,128]{2,1,0:T(8,128)(2,1)}), bf16[64,72,128]{2,1,0:T(8,128)(2,1)S(1)}, u32[]{:S(2)}, u32[]{:S(2)}) %all-to-all-start.1) | async-done | bytes 1179680 | tf_op jit(solution)/shard_map/all_to_all | solution.py:353
  60.1 0.0 copy-start.1
  60.1 6.6 %collective-permute-start.1 = (bf16[64,72,128]{2,1,0:T(8,128)(2,1)S(1)}, bf16[64,72,128]{2,1,0:T(8,128)(2,1)}, u32[]{:S(2)}, u32[]{:S(2)}) collective-permute-start(bf16[64,72,128]{2,1,0:T(8,128)(2,1)S(1)} %all-to-all-done.1.own_ref.received_ref), channel_id=1, source_target_pairs={{0,4},{4,0},{8,12},{12,8},{16,20},{20,16},{24,28},{28,24},{32,36},... | collective-permute-start | bytes 3538952 | tf_op jit(solution)/shard_map/ppermute | solution.py:384
  66.7 0.7 sum.1
  67.4 3.3 %all-to-all-start.2 = ((f32[8,8,128]{2,1,0:T(8,128)}), f32[8,8,128]{2,1,0:T(8,128)S(1)}, u32[]{:S(2)}, u32[]{:S(2)}) async-start(f32[8,8,128]{2,1,0:T(8,128)} %sum.1), calls=%async_computation.2 | async-start | bytes 65536 | tf_op jit(solution)/shard_map/all_to_all | solution.py:385
  70.6 0.0 collective-permute-done.1.other_ref
  70.7 0.0 copy-done.1
  70.7 8.3 %project.1 = f32[96,4096]{1,0:T(8,128)} custom-call(s32[96]{0:T(128)} %bitcast.6, s32[96]{0:T(128)} %column_ref.3, s32[1]{0:T(128)} %bitcast.core_ref, bf16[96,64,128]{2,1,0:T(8,128)(2,1)} %copy-done.2, bf16[64,72,128]{2,1,0:T(8,128)(2,1)} %copy-done.1, bf16[64,72,128]{2,1,0:T(8,128)(2,1)} %collective-permute-done.1.other_ref), custom_call_target="tpu_custom_call" | custom-call | flops 201326592 | bytes 2359296 | tf_op jit(solution)/shard_map/project/pallas_call | solution.py:388
  78.9 0.0 all-to-all-done.2.received_ref
  78.9 0.9 %top.1 = f32[1,4096]{1,0:T(1,128)} custom-call(s32[1]{0:T(128)} %bitcast.core_ref, f32[8,8,128]{2,1,0:T(8,128)S(1)} %all-to-all-done.2.received_ref, f32[32,128]{1,0:T(8,128)S(1)} %get-tuple-element.23.first_ref, f32[32,128]{1,0:T(8,128)S(1)} %collective-permute-done.other_ref), custom_call_target="tpu_custom_call" | custom-call | tf_op jit(solution)/shard_map/top/pallas_call | solution.py:408
  (4 shorter events, 0.0 us)
Async XLA Ops:
  0.6 7.1 %copy-start = (bf16[254,4096]{1,0:T(8,128)(2,1)S(1)}, bf16[254,4096]{1,0:T(8,128)(2,1)}, u32[]{:S(2)}) copy-start(bf16[254,4096]{1,0:T(8,128)(2,1)} %param.12) | copy-start | bytes 6242308
  0.6 1.2 %copy-start.5 = (bf16[4,64,1024]{2,1,0:T(8,128)(2,1)S(1)}, bf16[4,64,1024]{2,1,0:T(8,128)(2,1)}, u32[]{:S(2)}) copy-start(bf16[4,64,1024]{2,1,0:T(8,128)(2,1)} %basis_ref.1) | copy-start | bytes 1572868
  1.8 6.6 %copy-start.9 = (s32[254]{0:T(256)S(1)}, s32[254]{0:T(256)}, u32[]{:S(2)}) copy-start(s32[254]{0:T(256)} %param.13) | copy-start | bytes 3052
  1.8 7.4 %copy-start.10 = (bf16[4,4096]{1,0:T(4,128)(2,1)S(1)}, bf16[4,4096]{1,0:T(4,128)(2,1)}, u32[]{:S(2)}) copy-start(bf16[4,4096]{1,0:T(4,128)(2,1)} %param.10) | copy-start | bytes 98308
  1.8 10.7 %copy-start.8 = (s32[4]{0:T(128)S(1)}, s32[4]{0:T(128)}, u32[]{:S(2)}) copy-start(s32[4]{0:T(128)} %rank_ref.1) | copy-start | bytes 52
  2.8 9.8 %all-to-all-start = ((f32[4,72,128]{2,1,0:T(8,128)}), f32[4,72,128]{2,1,0:T(8,128)S(1)}, u32[]{:S(2)}, u32[]{:S(2)}) async-start(f32[4,72,128]{2,1,0:T(8,128)} %gram.1), calls=%async_computation | async-start | bytes 294912 | tf_op jit(solution)/shard_map/all_to_all | solution.py:320
  9.2 26.6 %copy-start.6 = (s32[96]{0:T(128)S(1)}, s32[96]{0:T(128)}, u32[]{:S(2)}) copy-start(s32[96]{0:T(128)} %column_ref.3) | copy-start | bytes 1156
  9.2 26.6 %copy-start.7 = (s32[96]{0:T(128)S(1)}, s32[96]{0:T(128)}, u32[]{:S(2)}) copy-start(s32[96]{0:T(128)} %row_ref.1) | copy-start | bytes 1156
  14.1 1.0 %copy-start.3 = (bf16[64,72,128]{2,1,0:T(8,128)(2,1)}, bf16[64,72,128]{2,1,0:T(8,128)(2,1)S(1)}, u32[]{:S(2)}) copy-start(bf16[64,72,128]{2,1,0:T(8,128)(2,1)S(1)} %get-tuple-element.22) | copy-start | bytes 3538948
  15.2 44.9 %all-to-all-start.1 = ((bf16[64,72,128]{2,1,0:T(8,128)(2,1)}), bf16[64,72,128]{2,1,0:T(8,128)(2,1)S(1)}, u32[]{:S(2)}, u32[]{:S(2)}) async-start(bf16[64,72,128]{2,1,0:T(8,128)(2,1)} %copy-done.3), calls=%async_computation.1 | async-start | bytes 2359296 | tf_op jit(solution)/shard_map/all_to_all | solution.py:353
  31.5 9.1 %collective-permute-start = (f32[32,128]{1,0:T(8,128)S(1)}, f32[32,128]{1,0:T(8,128)S(1)}, u32[]{:S(2)}, u32[]{:S(2)}) collective-permute-start(f32[32,128]{1,0:T(8,128)S(1)} %get-tuple-element.23.first_ref), channel_id=1, source_target_pairs={{0,4},{4,0},{8,12},{12,8},{16,20},{20,16},{24,28},{28,24},{32,36},... | collective-permute-start | bytes 49160 | tf_op jit(solution)/shard_map/ppermute | solution.py:354
  35.8 1.1 %copy-start.4 = (bf16[96,4096]{1,0:T(8,128)(2,1)S(1)}, bf16[96,4096]{1,0:T(8,128)(2,1)}, u32[]{:S(2)}) copy-start(bf16[96,4096]{1,0:T(8,128)(2,1)} %blocks_ref.1) | copy-start | bytes 2359300
  39.4 1.2 %copy-start.2 = (bf16[96,64,128]{2,1,0:T(8,128)(2,1)}, bf16[96,64,128]{2,1,0:T(8,128)(2,1)S(1)}, u32[]{:S(2)}) copy-start(bf16[96,64,128]{2,1,0:T(8,128)(2,1)S(1)} %left.1.rows_ref) | copy-start | bytes 4718596
  60.1 10.6 %copy-start.1 = (bf16[64,72,128]{2,1,0:T(8,128)(2,1)}, bf16[64,72,128]{2,1,0:T(8,128)(2,1)S(1)}, u32[]{:S(2)}) copy-start(bf16[64,72,128]{2,1,0:T(8,128)(2,1)S(1)} %all-to-all-done.1.own_ref.received_ref) | copy-start | bytes 3538948
  60.1 10.5 %collective-permute-start.1 = (bf16[64,72,128]{2,1,0:T(8,128)(2,1)S(1)}, bf16[64,72,128]{2,1,0:T(8,128)(2,1)}, u32[]{:S(2)}, u32[]{:S(2)}) collective-permute-start(bf16[64,72,128]{2,1,0:T(8,128)(2,1)S(1)} %all-to-all-done.1.own_ref.received_ref), channel_id=1, source_target_pairs={{0,4},{4,0},{8,12},{12,8},{16,20},{20,16},{24,28},{28,24},{32,36},... | collective-permute-start | bytes 3538952 | tf_op jit(solution)/shard_map/ppermute | solution.py:384
  67.4 11.6 %all-to-all-start.2 = ((f32[8,8,128]{2,1,0:T(8,128)}), f32[8,8,128]{2,1,0:T(8,128)S(1)}, u32[]{:S(2)}, u32[]{:S(2)}) async-start(f32[8,8,128]{2,1,0:T(8,128)} %sum.1), calls=%async_computation.2 | async-start | bytes 65536 | tf_op jit(solution)/shard_map/all_to_all | solution.py:385

commit v4 on v3

--- a/solution.py
+++ b/solution.py
@@ -215,7 +215,7 @@
         out_ref[:, tile * wide : (tile + 1) * wide] = natural[tile : tile + 1]
 
 
-def left_kernel(row_ref, column_ref, blocks_ref, left_ref, out_ref, spread):
+def left_kernel(row_ref, blocks_ref, left_ref, out_ref, spread):
     step = pl.program_id(0)
     count, flat = blocks_ref.shape
     width = left_ref.shape[1]
@@ -231,8 +231,7 @@
         rows = jnp.where(
             low, jnp.concatenate([here, turned], axis=0), jnp.concatenate([turned, here], axis=0)
         ).astype(BF16)
-        product = nn(left_ref[row_ref[block]], rows)
-        out_ref[index] = jnp.where(low == (column_ref[block] < 2), product, 0.0).astype(BF16)
+        out_ref[index] = nn(left_ref[row_ref[block]], rows).astype(BF16)
 
 
 def project_kernel(
@@ -241,38 +240,38 @@
     step = pl.program_id(0)
     count, width, wide = rows_ref.shape
     tiles = width // 2
-    low = iota((tiles, wide), 1) < width
 
     @pl.when(step == 0)
     def _():
         row = iota((width, wide), 0)
-        column = iota((width, wide), 1) & (width - 1)
-        triangles[0, 0] = (row <= column).astype(F32).astype(BF16)
-        triangles[0, 1] = (row < column).astype(F32).astype(BF16)
-        triangles[0, 2] = jnp.zeros((width, wide), BF16)
-        triangles[1, 0] = (row > column).astype(F32).astype(BF16)
-        triangles[1, 1] = (row > column).astype(F32).astype(BF16)
-        triangles[1, 2] = (row == column).astype(F32).astype(BF16)
+        lane = iota((width, wide), 1)
+        column = lane & (width - 1)
+        for cluster in range(triangles.shape[0]):
+            mine = (lane < width) == (cluster < 2)
+            if cluster % 2 == 0:
+                parts = (row <= column, row < column, row < 0)
+            else:
+                parts = (row > column, row > column, row == column)
+            for index, part in enumerate(parts):
+                triangles[cluster, index] = (mine & part).astype(F32).astype(BF16)
 
     for index in range(count):
         block = step * count + index
         owner = owner_ref[block]
         cluster = column_ref[block]
         first = cluster < 2
-        side = cluster & 1
         source = jnp.right_shift(owner, 1)
         at_home = (owner & 1) == core_ref[0]
         folded = jnp.where(at_home, own_ref[source, :width], other_ref[source, :width])
         centre = jnp.where(at_home, own_ref[source, width:], other_ref[source, width:])[:1]
-        direct = folded * triangles[side, 0] + centre * triangles[side, 2]
-        mirrored = folded * triangles[side, 1]
+        direct = folded * triangles[cluster, 0] + centre * triangles[cluster, 2]
+        mirrored = folded * triangles[cluster, 1]
         rows = rows_ref[index]
-        full = nn(rows, jnp.concatenate([direct, direct], axis=0))
-        full = full + nt(rows, jnp.concatenate([mirrored, mirrored], axis=0))
-        top, bottom = full[:tiles], full[tiles:]
-        stay = jnp.where(first, top, bottom)
-        move = pltpu.roll(jnp.where(first, bottom, top), width, 1)
-        result[pl.ds(index, tiles, stride=count), :] = jnp.where(low == first, stay, move)
+        one = nn(rows[:, :width], direct)
+        two = jnp.concatenate([nt(rows, mirrored), jnp.zeros((width, width), F32)], axis=1)
+        stay = jnp.where(first, one[:tiles], one[tiles:]) + two[:tiles]
+        move = jnp.where(first, one[tiles:], one[:tiles]) + two[tiles:]
+        result[pl.ds(index, tiles, stride=count), :] = stay + pltpu.roll(move, width, 1)
     for tile in range(tiles):
         out_ref[:, tile * wide : (tile + 1) * wide] = result[tile * count : (tile + 1) * count, :]
 
@@ -357,7 +356,7 @@
         left_kernel,
         out_shape=shape((blk, width, wide), BF16),
         grid_spec=pltpu.PrefetchScalarGridSpec(
-            num_scalar_prefetch=2,
+            num_scalar_prefetch=1,
             grid=(blk // ROWS,),
             in_specs=[
                 pl.BlockSpec((ROWS, width * width), lambda i, *_: (i, 0)),
@@ -371,7 +370,7 @@
             flops=4 * blk * width**3, bytes_accessed=4 * blk * width * width, transcendentals=0
         ),
         name="left",
-    )(row_cluster, column_cluster, couplings, left)
+    )(row_cluster, couplings, left)
     own, first_other, rows = lax.optimization_barrier((own, first_other, rows))
     summed = pl.pallas_call(
         sum_kernel,
@@ -395,7 +394,7 @@
             out_specs=pl.BlockSpec((ROWS, width * width), lambda i, *_: (i, 0)),
             scratch_shapes=[
                 pltpu.VMEM((ROWS * half, wide), F32),
-                pltpu.VMEM((2, 3, width, wide), BF16),
+                pltpu.VMEM((nodes, 3, width, wide), BF16),
             ],
         ),
         compiler_params=pltpu.CompilerParams(vmem_limit_bytes=56 * 1024 * 1024),

time: 80.5 us -> 79.8 us (level)
    unnamed x22 -> x20, local copies, waits for them, and re-layouts: 4.52 us -> 4.52 us
  transfers between devices with their start and end apart: 5 -> 5, of which waited for: 2 -> 2; matrix products, arithmetic and copies ran while one was open for 2% -> 2% of each run, Pallas kernels for 16% -> 15%
where the time goes in v4:
time: 79.8 us; the launch traced here: 79.2 us
  starting transfers between devices  35.3 us (44%)
  waiting for transfers between devices  21.5 us (27%)
  Pallas kernels  15.4 us (19%)
  local copies, waits for them, and re-layouts  5.98 us (7%)
  between operations  0.82 us (1%)
    all_to_all x1, waiting for transfers between devices, on_device(): own = lax.all_to_all(sent, 'branch', 0, 0, axis_index_groups=same_core)  19.6 us
    all_to_all x1, starting transfers between devices, on_device(): own = lax.all_to_all(sent, 'branch', 0, 0, axis_index_groups=same_core)  16.3 us
    pallas_call x1, Pallas kernels, on_device(): pl.pallas_call(project_kernel, out_shape=shape((blk, width * width), F32)...  7.58 us
    ppermute x1, starting transfers between devices, on_device(): other = lax.ppermute(own, 'branch', partners)  6.56 us
    all_to_all x1, starting transfers between devices, on_device(): gathered = lax.all_to_all(partial_sums, 'level', 0, 0)  4.84 us
    unnamed x20, local copies, waits for them, and re-layouts  4.52 us
    ppermute x1, starting transfers between devices, on_device(): first_other = lax.ppermute(first, 'branch', partners)  4.29 us
    all_to_all x1, starting transfers between devices, on_device(): lax.all_to_all(summed, ('branch', 'level'), 0, 0, axis_index_groups=same_...  3.28 us
  transfers between devices with their start and end apart: 5, of which 2 were waited for; matrix products, arithmetic and copies ran while one was open for 2% of the time, Pallas kernels for 15%

profile of v4, /device:TPU:1, one launch (start us, length us, event | category | flops | bytes accessed | tf_op | source)
XLA Modules:
  0.0 79.2 jit_solution(11356455459928671030)
XLA Ops:
  0.6 0.0 copy-start
  0.6 0.0 copy-start.5
  0.7 1.2 %copy-done.5 = bf16[4,64,1024]{2,1,0:T(8,128)(2,1)S(1)} copy-done((bf16[4,64,1024]{2,1,0:T(8,128)(2,1)S(1)}, bf16[4,64,1024]{2,1,0:T(8,128)(2,1)}, u32[]{:S(2)}) %copy-start.5) | copy-done | bytes 524312
  1.8 0.0 copy-start.8
  1.8 0.0 copy-start.9
  1.8 0.0 copy-start.6
  1.8 1.0 %gram.1 = f32[4,72,128]{2,1,0:T(8,128)} custom-call(bf16[4,64,1024]{2,1,0:T(8,128)(2,1)S(1)} %copy-done.5), custom_call_target="tpu_custom_call" | custom-call | tf_op jit(solution)/shard_map/gram/pallas_call | solution.py:308
  2.8 4.8 %all-to-all-start = ((f32[4,72,128]{2,1,0:T(8,128)}), f32[4,72,128]{2,1,0:T(8,128)S(1)}, u32[]{:S(2)}, u32[]{:S(2)}) async-start(f32[4,72,128]{2,1,0:T(8,128)} %gram.1), calls=%async_computation | async-start | bytes 294912 | tf_op jit(solution)/shard_map/all_to_all | solution.py:319
  7.7 0.0 copy-done
  7.7 0.6 gather_fusion.1
  8.3 0.1 gather.12
  8.4 0.0 copy-done.8
  8.4 0.6 gather_fusion
  9.1 0.1 broadcast_select_fusion.path_ref
  9.2 0.0 copy-start.7
  9.2 0.0 copy-done.9
  9.2 0.1 reshape.46.bottom_ref
  9.3 1.3 %path.1 = (bf16[7,64,64]{2,1,0:T(8,128)(2,1)S(1)}, bf16[7,64,64]{2,1,0:T(8,128)(2,1)S(1)}) custom-call(s32[7]{0:T(128)S(1)} %broadcast_select_fusion.1.rank_ref, bf16[7,64,64]{2,1,0:T(8,128)(2,1)S(1)} %broadcast_select_fusion.path_ref), custom_call_target="tpu_custom_call" | custom-call | tf_op jit(solution)/shard_map/path/pallas_call | solution.py:323
  10.7 1.9 %all-to-all-done.parts_ref = f32[4,72,128]{2,1,0:T(8,128)S(1)} async-done(((f32[4,72,128]{2,1,0:T(8,128)}), f32[4,72,128]{2,1,0:T(8,128)S(1)}, u32[]{:S(2)}, u32[]{:S(2)}) %all-to-all-start) | async-done | bytes 147488 | tf_op jit(solution)/shard_map/all_to_all | solution.py:319
  12.6 0.0 copy-done.6
  12.6 1.6 %near.1 = (bf16[4,64,64]{2,1,0:T(8,128)(2,1)S(1)}, bf16[64,72,128]{2,1,0:T(8,128)(2,1)S(1)}, f32[32,128]{1,0:T(8,128)S(1)}) custom-call(s32[4]{0:T(128)S(1)} %copy-done.6, s32[1]{0:T(128)} %bitcast.2.place_ref, s32[1]{0:T(128)} %bitcast.3.level_ref, f32[4,72,128]{2,1,0:T(8,128)S(1)} %all-to-all-done.parts_ref, bf16[4,64,64]{2,1,0:T(8,128)(2,1)S(1)} %reshape.46.bottom_ref, ...), custom_call_target="tpu_custom_call" | custom-call | tf_op jit(solution)/shard_map/near/pallas_call | solution.py:331
  14.1 0.0 copy-start.3
  14.2 1.0 %copy-done.3 = bf16[64,72,128]{2,1,0:T(8,128)(2,1)} copy-done((bf16[64,72,128]{2,1,0:T(8,128)(2,1)}, bf16[64,72,128]{2,1,0:T(8,128)(2,1)S(1)}, u32[]{:S(2)}) %copy-start.3) | copy-done | bytes 1179672
  15.2 16.3 %all-to-all-start.1 = ((bf16[64,72,128]{2,1,0:T(8,128)(2,1)}), bf16[64,72,128]{2,1,0:T(8,128)(2,1)S(1)}, u32[]{:S(2)}, u32[]{:S(2)}) async-start(bf16[64,72,128]{2,1,0:T(8,128)(2,1)} %copy-done.3), calls=%async_computation.1 | async-start | bytes 2359296 | tf_op jit(solution)/shard_map/all_to_all | solution.py:352
  31.5 4.3 %collective-permute-start = (f32[32,128]{1,0:T(8,128)S(1)}, f32[32,128]{1,0:T(8,128)S(1)}, u32[]{:S(2)}, u32[]{:S(2)}) collective-permute-start(f32[32,128]{1,0:T(8,128)S(1)} %get-tuple-element.23.first_ref), channel_id=1, source_target_pairs={{0,4},{4,0},{8,12},{12,8},{16,20},{20,16},{24,28},{28,24},{32,36},... | collective-permute-start | bytes 49160 | tf_op jit(solution)/shard_map/ppermute | solution.py:353
  35.8 0.0 copy-done.7
  35.8 0.0 copy-start.4
  35.8 1.1 %copy-done.4 = bf16[96,4096]{1,0:T(8,128)(2,1)S(1)} copy-done((bf16[96,4096]{1,0:T(8,128)(2,1)S(1)}, bf16[96,4096]{1,0:T(8,128)(2,1)}, u32[]{:S(2)}) %copy-start.4) | copy-done | bytes 786456
  36.9 2.4 %left.1.rows_ref = bf16[96,64,128]{2,1,0:T(8,128)(2,1)S(1)} custom-call(s32[96]{0:T(128)S(1)} %copy-done.7, bf16[96,4096]{1,0:T(8,128)(2,1)S(1)} %copy-done.4, bf16[4,64,64]{2,1,0:T(8,128)(2,1)S(1)} %get-tuple-element.24.left_ref), custom_call_target="tpu_custom_call" | custom-call | flops 100663296 | bytes 1572864 | tf_op jit(solution)/shard_map/left/pallas_call | solution.py:355
  39.4 0.0 copy-start.2
  39.4 1.2 %copy-done.2 = bf16[96,64,128]{2,1,0:T(8,128)(2,1)} copy-done((bf16[96,64,128]{2,1,0:T(8,128)(2,1)}, bf16[96,64,128]{2,1,0:T(8,128)(2,1)S(1)}, u32[]{:S(2)}) %copy-start.2) | copy-done | bytes 1572888
  40.5 0.0 collective-permute-done.other_ref
  40.5 19.6 %all-to-all-done.1.own_ref.received_ref = bf16[64,72,128]{2,1,0:T(8,128)(2,1)S(1)} async-done(((bf16[64,72,128]{2,1,0:T(8,128)(2,1)}), bf16[64,72,128]{2,1,0:T(8,128)(2,1)S(1)}, u32[]{:S(2)}, u32[]{:S(2)}) %all-to-all-start.1) | async-done | bytes 1179680 | tf_op jit(solution)/shard_map/all_to_all | solution.py:352
  60.1 0.0 copy-start.1
  60.1 6.6 %collective-permute-start.1 = (bf16[64,72,128]{2,1,0:T(8,128)(2,1)S(1)}, bf16[64,72,128]{2,1,0:T(8,128)(2,1)}, u32[]{:S(2)}, u32[]{:S(2)}) collective-permute-start(bf16[64,72,128]{2,1,0:T(8,128)(2,1)S(1)} %all-to-all-done.1.own_ref.received_ref), channel_id=1, source_target_pairs={{0,4},{4,0},{8,12},{12,8},{16,20},{20,16},{24,28},{28,24},{32,36},... | collective-permute-start | bytes 3538952 | tf_op jit(solution)/shard_map/ppermute | solution.py:383
  66.7 0.7 sum.1
  67.4 3.3 %all-to-all-start.2 = ((f32[8,8,128]{2,1,0:T(8,128)}), f32[8,8,128]{2,1,0:T(8,128)S(1)}, u32[]{:S(2)}, u32[]{:S(2)}) async-start(f32[8,8,128]{2,1,0:T(8,128)} %sum.1), calls=%async_computation.2 | async-start | bytes 65536 | tf_op jit(solution)/shard_map/all_to_all | solution.py:384
  70.6 0.0 collective-permute-done.1.other_ref
  70.7 0.0 copy-done.1
  70.7 7.6 %project.1 = f32[96,4096]{1,0:T(8,128)} custom-call(s32[96]{0:T(128)} %bitcast.6, s32[96]{0:T(128)} %column_ref.1, s32[1]{0:T(128)} %bitcast.core_ref, bf16[96,64,128]{2,1,0:T(8,128)(2,1)} %copy-done.2, bf16[64,72,128]{2,1,0:T(8,128)(2,1)} %copy-done.1, bf16[64,72,128]{2,1,0:T(8,128)(2,1)} %collective-permute-done.1.other_ref), custom_call_target="tpu_custom_call" | custom-call | flops 201326592 | bytes 2359296 | tf_op jit(solution)/shard_map/project/pallas_call | solution.py:387
  78.2 0.0 all-to-all-done.2.received_ref
  78.2 0.9 %top.1 = f32[1,4096]{1,0:T(1,128)} custom-call(s32[1]{0:T(128)} %bitcast.core_ref, f32[8,8,128]{2,1,0:T(8,128)S(1)} %all-to-all-done.2.received_ref, f32[32,128]{1,0:T(8,128)S(1)} %get-tuple-element.23.first_ref, f32[32,128]{1,0:T(8,128)S(1)} %collective-permute-done.other_ref), custom_call_target="tpu_custom_call" | custom-call | tf_op jit(solution)/shard_map/top/pallas_call | solution.py:407
  (4 shorter events, 0.0 us)
Async XLA Ops:
  0.6 7.1 %copy-start = (bf16[254,4096]{1,0:T(8,128)(2,1)S(1)}, bf16[254,4096]{1,0:T(8,128)(2,1)}, u32[]{:S(2)}) copy-start(bf16[254,4096]{1,0:T(8,128)(2,1)} %param.12) | copy-start | bytes 6242308
  0.6 1.2 %copy-start.5 = (bf16[4,64,1024]{2,1,0:T(8,128)(2,1)S(1)}, bf16[4,64,1024]{2,1,0:T(8,128)(2,1)}, u32[]{:S(2)}) copy-start(bf16[4,64,1024]{2,1,0:T(8,128)(2,1)} %basis_ref.1) | copy-start | bytes 1572868
  1.8 6.6 %copy-start.8 = (s32[254]{0:T(256)S(1)}, s32[254]{0:T(256)}, u32[]{:S(2)}) copy-start(s32[254]{0:T(256)} %param.13) | copy-start | bytes 3052
  1.8 7.3 %copy-start.9 = (bf16[4,4096]{1,0:T(4,128)(2,1)S(1)}, bf16[4,4096]{1,0:T(4,128)(2,1)}, u32[]{:S(2)}) copy-start(bf16[4,4096]{1,0:T(4,128)(2,1)} %param.10) | copy-start | bytes 98308
  1.8 10.7 %copy-start.6 = (s32[4]{0:T(128)S(1)}, s32[4]{0:T(128)}, u32[]{:S(2)}) copy-start(s32[4]{0:T(128)} %rank_ref.1) | copy-start | bytes 52
  2.8 9.8 %all-to-all-start = ((f32[4,72,128]{2,1,0:T(8,128)}), f32[4,72,128]{2,1,0:T(8,128)S(1)}, u32[]{:S(2)}, u32[]{:S(2)}) async-start(f32[4,72,128]{2,1,0:T(8,128)} %gram.1), calls=%async_computation | async-start | bytes 294912 | tf_op jit(solution)/shard_map/all_to_all | solution.py:319
  9.2 26.6 %copy-start.7 = (s32[96]{0:T(128)S(1)}, s32[96]{0:T(128)}, u32[]{:S(2)}) copy-start(s32[96]{0:T(128)} %row_ref.1) | copy-start | bytes 1156
  14.1 1.0 %copy-start.3 = (bf16[64,72,128]{2,1,0:T(8,128)(2,1)}, bf16[64,72,128]{2,1,0:T(8,128)(2,1)S(1)}, u32[]{:S(2)}) copy-start(bf16[64,72,128]{2,1,0:T(8,128)(2,1)S(1)} %get-tuple-element.22) | copy-start | bytes 3538948
  15.2 44.9 %all-to-all-start.1 = ((bf16[64,72,128]{2,1,0:T(8,128)(2,1)}), bf16[64,72,128]{2,1,0:T(8,128)(2,1)S(1)}, u32[]{:S(2)}, u32[]{:S(2)}) async-start(bf16[64,72,128]{2,1,0:T(8,128)(2,1)} %copy-done.3), calls=%async_computation.1 | async-start | bytes 2359296 | tf_op jit(solution)/shard_map/all_to_all | solution.py:352
  31.5 9.1 %collective-permute-start = (f32[32,128]{1,0:T(8,128)S(1)}, f32[32,128]{1,0:T(8,128)S(1)}, u32[]{:S(2)}, u32[]{:S(2)}) collective-permute-start(f32[32,128]{1,0:T(8,128)S(1)} %get-tuple-element.23.first_ref), channel_id=1, source_target_pairs={{0,4},{4,0},{8,12},{12,8},{16,20},{20,16},{24,28},{28,24},{32,36},... | collective-permute-start | bytes 49160 | tf_op jit(solution)/shard_map/ppermute | solution.py:353
  35.8 1.1 %copy-start.4 = (bf16[96,4096]{1,0:T(8,128)(2,1)S(1)}, bf16[96,4096]{1,0:T(8,128)(2,1)}, u32[]{:S(2)}) copy-start(bf16[96,4096]{1,0:T(8,128)(2,1)} %blocks_ref.1) | copy-start | bytes 2359300
  39.4 1.2 %copy-start.2 = (bf16[96,64,128]{2,1,0:T(8,128)(2,1)}, bf16[96,64,128]{2,1,0:T(8,128)(2,1)S(1)}, u32[]{:S(2)}) copy-start(bf16[96,64,128]{2,1,0:T(8,128)(2,1)S(1)} %left.1.rows_ref) | copy-start | bytes 4718596
  60.1 10.5 %copy-start.1 = (bf16[64,72,128]{2,1,0:T(8,128)(2,1)}, bf16[64,72,128]{2,1,0:T(8,128)(2,1)S(1)}, u32[]{:S(2)}) copy-start(bf16[64,72,128]{2,1,0:T(8,128)(2,1)S(1)} %all-to-all-done.1.own_ref.received_ref) | copy-start | bytes 3538948
  60.1 10.5 %collective-permute-start.1 = (bf16[64,72,128]{2,1,0:T(8,128)(2,1)S(1)}, bf16[64,72,128]{2,1,0:T(8,128)(2,1)}, u32[]{:S(2)}, u32[]{:S(2)}) collective-permute-start(bf16[64,72,128]{2,1,0:T(8,128)(2,1)S(1)} %all-to-all-done.1.own_ref.received_ref), channel_id=1, source_target_pairs={{0,4},{4,0},{8,12},{12,8},{16,20},{20,16},{24,28},{28,24},{32,36},... | collective-permute-start | bytes 3538952 | tf_op jit(solution)/shard_map/ppermute | solution.py:383
  67.4 10.9 %all-to-all-start.2 = ((f32[8,8,128]{2,1,0:T(8,128)}), f32[8,8,128]{2,1,0:T(8,128)S(1)}, u32[]{:S(2)}, u32[]{:S(2)}) async-start(f32[8,8,128]{2,1,0:T(8,128)} %sum.1), calls=%async_computation.2 | async-start | bytes 65536 | tf_op jit(solution)/shard_map/all_to_all | solution.py:384

commit v5 on v4

--- a/solution.py
+++ b/solution.py
@@ -241,37 +241,49 @@
     count, width, wide = rows_ref.shape
     tiles = width // 2
 
+    low = iota((tiles, wide), 1) < width
+
     @pl.when(step == 0)
     def _():
         row = iota((width, wide), 0)
         lane = iota((width, wide), 1)
         column = lane & (width - 1)
-        for cluster in range(triangles.shape[0]):
+        for cluster in range(4):
             mine = (lane < width) == (cluster < 2)
-            if cluster % 2 == 0:
-                parts = (row <= column, row < column, row < 0)
-            else:
-                parts = (row > column, row > column, row == column)
+            parts = (row <= column, row < 0) if cluster % 2 == 0 else (row > column, row == column)
             for index, part in enumerate(parts):
                 triangles[cluster, index] = (mine & part).astype(F32).astype(BF16)
-
-    for index in range(count):
-        block = step * count + index
-        owner = owner_ref[block]
-        cluster = column_ref[block]
-        first = cluster < 2
-        source = jnp.right_shift(owner, 1)
-        at_home = (owner & 1) == core_ref[0]
-        folded = jnp.where(at_home, own_ref[source, :width], other_ref[source, :width])
-        centre = jnp.where(at_home, own_ref[source, width:], other_ref[source, width:])[:1]
-        direct = folded * triangles[cluster, 0] + centre * triangles[cluster, 2]
-        mirrored = folded * triangles[cluster, 1]
-        rows = rows_ref[index]
-        one = nn(rows[:, :width], direct)
-        two = jnp.concatenate([nt(rows, mirrored), jnp.zeros((width, width), F32)], axis=1)
-        stay = jnp.where(first, one[:tiles], one[tiles:]) + two[:tiles]
-        move = jnp.where(first, one[tiles:], one[:tiles]) + two[tiles:]
-        result[pl.ds(index, tiles, stride=count), :] = stay + pltpu.roll(move, width, 1)
+        for place in range(2):
+            mine = (lane < width) == (place == 0)
+            triangles[4 + place, 0] = (mine & (row > column)).astype(F32).astype(BF16)
+            triangles[4 + place, 1] = (mine & (row < column)).astype(F32).astype(BF16)
+
+    for index in range(0, count, 2):
+        folded = []
+        for place in range(2):
+            owner = owner_ref[step * count + index + place]
+            source = jnp.right_shift(owner, 1)
+            at_home = (owner & 1) == core_ref[0]
+            folded.append(
+                (
+                    jnp.where(at_home, own_ref[source, :width], other_ref[source, :width]),
+                    jnp.where(at_home, own_ref[source, width:], other_ref[source, width:])[:1],
+                )
+            )
+        turned = jnp.concatenate([folded[0][0], folded[1][0]], axis=0).T
+        for place in range(2):
+            cluster = column_ref[step * count + index + place]
+            here, centre = folded[place]
+            mirrored = jnp.where(cluster < 2, turned[:width], turned[width:])
+            right = (
+                here * triangles[cluster, 0]
+                + centre * triangles[cluster, 1]
+                + mirrored * triangles[4 + place, cluster & 1]
+            )
+            full = nn(rows_ref[index + place][:, :width], right)
+            top, bottom = full[:tiles], full[tiles:]
+            out = jnp.where(low, top, bottom) + pltpu.roll(jnp.where(low, bottom, top), width, 1)
+            result[pl.ds(index + place, tiles, stride=count), :] = out
     for tile in range(tiles):
         out_ref[:, tile * wide : (tile + 1) * wide] = result[tile * count : (tile + 1) * count, :]
 
@@ -349,6 +361,7 @@
         path_high,
         path_low,
     )
+    sent, first = lax.optimization_barrier((sent, first))
     own = lax.all_to_all(sent, "branch", 0, 0, axis_index_groups=same_core)
     first_other = lax.ppermute(first, "branch", partners)
     square = pl.BlockSpec((ROWS, width, wide), lambda i, *_: (i, 0, 0))
@@ -394,7 +407,7 @@
             out_specs=pl.BlockSpec((ROWS, width * width), lambda i, *_: (i, 0)),
             scratch_shapes=[
                 pltpu.VMEM((ROWS * half, wide), F32),
-                pltpu.VMEM((nodes, 3, width, wide), BF16),
+                pltpu.VMEM((6, 2, width, wide), BF16),
             ],
         ),
         compiler_params=pltpu.CompilerParams(vmem_limit_bytes=56 * 1024 * 1024),

time: 79.8 us -> 79.5 us (level)
  no operation moved by 1% of the time
where the time goes in v5:
time: 79.5 us; the launch traced here: 78.9 us
  starting transfers between devices  35.3 us (44%)
  waiting for transfers between devices  21.5 us (27%)
  Pallas kernels  15.2 us (19%)
  local copies, waits for them, and re-layouts  5.98 us (8%)
  between operations  0.82 us (1%)
    all_to_all x1, waiting for transfers between devices, on_device(): own = lax.all_to_all(sent, 'branch', 0, 0, axis_index_groups=same_core)  19.6 us
    all_to_all x1, starting transfers between devices, on_device(): own = lax.all_to_all(sent, 'branch', 0, 0, axis_index_groups=same_core)  16.3 us
    pallas_call x1, Pallas kernels, on_device(): pl.pallas_call(project_kernel, out_shape=shape((blk, width * width), F32)...  7.28 us
    ppermute x1, starting transfers between devices, on_device(): other = lax.ppermute(own, 'branch', partners)  6.56 us
    all_to_all x1, starting transfers between devices, on_device(): gathered = lax.all_to_all(partial_sums, 'level', 0, 0)  4.84 us
    unnamed x20, local copies, waits for them, and re-layouts  4.52 us
    ppermute x1, starting transfers between devices, on_device(): first_other = lax.ppermute(first, 'branch', partners)  4.29 us
    all_to_all x1, starting transfers between devices, on_device(): lax.all_to_all(summed, ('branch', 'level'), 0, 0, axis_index_groups=same_...  3.28 us
  transfers between devices with their start and end apart: 5, of which 2 were waited for; matrix products, arithmetic and copies ran while one was open for 2% of the time, Pallas kernels for 15%

profile of v5, /device:TPU:1, one launch (start us, length us, event | category | flops | bytes accessed | tf_op | source)
XLA Modules:
  0.0 78.9 jit_solution(12692435765206000016)
XLA Ops:
  0.6 0.0 copy-start
  0.6 0.0 copy-start.5
  0.7 1.2 %copy-done.5 = bf16[4,64,1024]{2,1,0:T(8,128)(2,1)S(1)} copy-done((bf16[4,64,1024]{2,1,0:T(8,128)(2,1)S(1)}, bf16[4,64,1024]{2,1,0:T(8,128)(2,1)}, u32[]{:S(2)}) %copy-start.5) | copy-done | bytes 524312
  1.8 0.0 copy-start.8
  1.8 0.0 copy-start.9
  1.8 0.0 copy-start.6
  1.8 1.0 %gram.1 = f32[4,72,128]{2,1,0:T(8,128)} custom-call(bf16[4,64,1024]{2,1,0:T(8,128)(2,1)S(1)} %copy-done.5), custom_call_target="tpu_custom_call" | custom-call | tf_op jit(solution)/shard_map/gram/pallas_call | solution.py:320
  2.8 4.8 %all-to-all-start = ((f32[4,72,128]{2,1,0:T(8,128)}), f32[4,72,128]{2,1,0:T(8,128)S(1)}, u32[]{:S(2)}, u32[]{:S(2)}) async-start(f32[4,72,128]{2,1,0:T(8,128)} %gram.1), calls=%async_computation | async-start | bytes 294912 | tf_op jit(solution)/shard_map/all_to_all | solution.py:331
  7.7 0.0 copy-done
  7.7 0.6 gather_fusion.1
  8.3 0.1 gather.12
  8.4 0.0 copy-done.8
  8.4 0.6 gather_fusion
  9.1 0.1 broadcast_select_fusion.path_ref
  9.2 0.0 copy-start.7
  9.2 0.0 copy-done.9
  9.2 0.1 reshape.46.bottom_ref
  9.3 1.3 %path.1 = (bf16[7,64,64]{2,1,0:T(8,128)(2,1)S(1)}, bf16[7,64,64]{2,1,0:T(8,128)(2,1)S(1)}) custom-call(s32[7]{0:T(128)S(1)} %broadcast_select_fusion.1.rank_ref, bf16[7,64,64]{2,1,0:T(8,128)(2,1)S(1)} %broadcast_select_fusion.path_ref), custom_call_target="tpu_custom_call" | custom-call | tf_op jit(solution)/shard_map/path/pallas_call | solution.py:335
  10.7 1.9 %all-to-all-done.parts_ref = f32[4,72,128]{2,1,0:T(8,128)S(1)} async-done(((f32[4,72,128]{2,1,0:T(8,128)}), f32[4,72,128]{2,1,0:T(8,128)S(1)}, u32[]{:S(2)}, u32[]{:S(2)}) %all-to-all-start) | async-done | bytes 147488 | tf_op jit(solution)/shard_map/all_to_all | solution.py:331
  12.6 0.0 copy-done.6
  12.6 1.6 %near.1 = (bf16[4,64,64]{2,1,0:T(8,128)(2,1)S(1)}, bf16[64,72,128]{2,1,0:T(8,128)(2,1)S(1)}, f32[32,128]{1,0:T(8,128)S(1)}) custom-call(s32[4]{0:T(128)S(1)} %copy-done.6, s32[1]{0:T(128)} %bitcast.2.place_ref, s32[1]{0:T(128)} %bitcast.3.level_ref, f32[4,72,128]{2,1,0:T(8,128)S(1)} %all-to-all-done.parts_ref, bf16[4,64,64]{2,1,0:T(8,128)(2,1)S(1)} %reshape.46.bottom_ref, ...), custom_call_target="tpu_custom_call" | custom-call | tf_op jit(solution)/shard_map/near/pallas_call | solution.py:343
  14.1 0.0 copy-start.3
  14.2 1.0 %copy-done.3 = bf16[64,72,128]{2,1,0:T(8,128)(2,1)} copy-done((bf16[64,72,128]{2,1,0:T(8,128)(2,1)}, bf16[64,72,128]{2,1,0:T(8,128)(2,1)S(1)}, u32[]{:S(2)}) %copy-start.3) | copy-done | bytes 1179672
  15.2 16.3 %all-to-all-start.1 = ((bf16[64,72,128]{2,1,0:T(8,128)(2,1)}), bf16[64,72,128]{2,1,0:T(8,128)(2,1)S(1)}, u32[]{:S(2)}, u32[]{:S(2)}) async-start(bf16[64,72,128]{2,1,0:T(8,128)(2,1)} %copy-done.3), calls=%async_computation.1 | async-start | bytes 2359296 | tf_op jit(solution)/shard_map/all_to_all | solution.py:365
  31.5 4.3 %collective-permute-start = (f32[32,128]{1,0:T(8,128)S(1)}, f32[32,128]{1,0:T(8,128)S(1)}, u32[]{:S(2)}, u32[]{:S(2)}) collective-permute-start(f32[32,128]{1,0:T(8,128)S(1)} %get-tuple-element.27.first_ref), channel_id=1, source_target_pairs={{0,4},{4,0},{8,12},{12,8},{16,20},{20,16},{24,28},{28,24},{32,36},... | collective-permute-start | bytes 49160 | tf_op jit(solution)/shard_map/ppermute | solution.py:366
  35.8 0.0 copy-done.7
  35.8 0.0 copy-start.4
  35.8 1.1 %copy-done.4 = bf16[96,4096]{1,0:T(8,128)(2,1)S(1)} copy-done((bf16[96,4096]{1,0:T(8,128)(2,1)S(1)}, bf16[96,4096]{1,0:T(8,128)(2,1)}, u32[]{:S(2)}) %copy-start.4) | copy-done | bytes 786456
  36.9 2.4 %left.1.rows_ref = bf16[96,64,128]{2,1,0:T(8,128)(2,1)S(1)} custom-call(s32[96]{0:T(128)S(1)} %copy-done.7, bf16[96,4096]{1,0:T(8,128)(2,1)S(1)} %copy-done.4, bf16[4,64,64]{2,1,0:T(8,128)(2,1)S(1)} %get-tuple-element.28.left_ref), custom_call_target="tpu_custom_call" | custom-call | flops 100663296 | bytes 1572864 | tf_op jit(solution)/shard_map/left/pallas_call | solution.py:368
  39.4 0.0 copy-start.2
  39.4 1.2 %copy-done.2 = bf16[96,64,128]{2,1,0:T(8,128)(2,1)} copy-done((bf16[96,64,128]{2,1,0:T(8,128)(2,1)}, bf16[96,64,128]{2,1,0:T(8,128)(2,1)S(1)}, u32[]{:S(2)}) %copy-start.2) | copy-done | bytes 1572888
  40.5 0.0 collective-permute-done.other_ref
  40.5 19.6 %all-to-all-done.1.own_ref.received_ref = bf16[64,72,128]{2,1,0:T(8,128)(2,1)S(1)} async-done(((bf16[64,72,128]{2,1,0:T(8,128)(2,1)}), bf16[64,72,128]{2,1,0:T(8,128)(2,1)S(1)}, u32[]{:S(2)}, u32[]{:S(2)}) %all-to-all-start.1) | async-done | bytes 1179680 | tf_op jit(solution)/shard_map/all_to_all | solution.py:365
  60.1 0.0 copy-start.1
  60.1 6.6 %collective-permute-start.1 = (bf16[64,72,128]{2,1,0:T(8,128)(2,1)S(1)}, bf16[64,72,128]{2,1,0:T(8,128)(2,1)}, u32[]{:S(2)}, u32[]{:S(2)}) collective-permute-start(bf16[64,72,128]{2,1,0:T(8,128)(2,1)S(1)} %all-to-all-done.1.own_ref.received_ref), channel_id=1, source_target_pairs={{0,4},{4,0},{8,12},{12,8},{16,20},{20,16},{24,28},{28,24},{32,36},... | collective-permute-start | bytes 3538952 | tf_op jit(solution)/shard_map/ppermute | solution.py:396
  66.7 0.7 sum.1
  67.4 3.3 %all-to-all-start.2 = ((f32[8,8,128]{2,1,0:T(8,128)}), f32[8,8,128]{2,1,0:T(8,128)S(1)}, u32[]{:S(2)}, u32[]{:S(2)}) async-start(f32[8,8,128]{2,1,0:T(8,128)} %sum.1), calls=%async_computation.2 | async-start | bytes 65536 | tf_op jit(solution)/shard_map/all_to_all | solution.py:397
  70.6 0.0 collective-permute-done.1.other_ref
  70.7 0.0 copy-done.1
  70.7 7.3 %project.1 = f32[96,4096]{1,0:T(8,128)} custom-call(s32[96]{0:T(128)} %bitcast.6, s32[96]{0:T(128)} %column_ref.1, s32[1]{0:T(128)} %bitcast.core_ref, bf16[96,64,128]{2,1,0:T(8,128)(2,1)} %copy-done.2, bf16[64,72,128]{2,1,0:T(8,128)(2,1)} %copy-done.1, bf16[64,72,128]{2,1,0:T(8,128)(2,1)} %collective-permute-done.1.other_ref), custom_call_target="tpu_custom_call" | custom-call | flops 201326592 | bytes 2359296 | tf_op jit(solution)/shard_map/project/pallas_call | solution.py:400
  77.9 0.0 all-to-all-done.2.received_ref
  78.0 0.9 %top.1 = f32[1,4096]{1,0:T(1,128)} custom-call(s32[1]{0:T(128)} %bitcast.core_ref, f32[8,8,128]{2,1,0:T(8,128)S(1)} %all-to-all-done.2.received_ref, f32[32,128]{1,0:T(8,128)S(1)} %get-tuple-element.27.first_ref, f32[32,128]{1,0:T(8,128)S(1)} %collective-permute-done.other_ref), custom_call_target="tpu_custom_call" | custom-call | tf_op jit(solution)/shard_map/top/pallas_call | solution.py:420
  (4 shorter events, 0.0 us)
Async XLA Ops:
  0.6 7.1 %copy-start = (bf16[254,4096]{1,0:T(8,128)(2,1)S(1)}, bf16[254,4096]{1,0:T(8,128)(2,1)}, u32[]{:S(2)}) copy-start(bf16[254,4096]{1,0:T(8,128)(2,1)} %param.12) | copy-start | bytes 6242308
  0.6 1.2 %copy-start.5 = (bf16[4,64,1024]{2,1,0:T(8,128)(2,1)S(1)}, bf16[4,64,1024]{2,1,0:T(8,128)(2,1)}, u32[]{:S(2)}) copy-start(bf16[4,64,1024]{2,1,0:T(8,128)(2,1)} %basis_ref.1) | copy-start | bytes 1572868
  1.8 6.6 %copy-start.8 = (s32[254]{0:T(256)S(1)}, s32[254]{0:T(256)}, u32[]{:S(2)}) copy-start(s32[254]{0:T(256)} %param.13) | copy-start | bytes 3052
  1.8 7.3 %copy-start.9 = (bf16[4,4096]{1,0:T(4,128)(2,1)S(1)}, bf16[4,4096]{1,0:T(4,128)(2,1)}, u32[]{:S(2)}) copy-start(bf16[4,4096]{1,0:T(4,128)(2,1)} %param.10) | copy-start | bytes 98308
  1.8 10.7 %copy-start.6 = (s32[4]{0:T(128)S(1)}, s32[4]{0:T(128)}, u32[]{:S(2)}) copy-start(s32[4]{0:T(128)} %rank_ref.1) | copy-start | bytes 52
  2.8 9.8 %all-to-all-start = ((f32[4,72,128]{2,1,0:T(8,128)}), f32[4,72,128]{2,1,0:T(8,128)S(1)}, u32[]{:S(2)}, u32[]{:S(2)}) async-start(f32[4,72,128]{2,1,0:T(8,128)} %gram.1), calls=%async_computation | async-start | bytes 294912 | tf_op jit(solution)/shard_map/all_to_all | solution.py:331
  9.2 26.6 %copy-start.7 = (s32[96]{0:T(128)S(1)}, s32[96]{0:T(128)}, u32[]{:S(2)}) copy-start(s32[96]{0:T(128)} %row_ref.1) | copy-start | bytes 1156
  14.1 1.0 %copy-start.3 = (bf16[64,72,128]{2,1,0:T(8,128)(2,1)}, bf16[64,72,128]{2,1,0:T(8,128)(2,1)S(1)}, u32[]{:S(2)}) copy-start(bf16[64,72,128]{2,1,0:T(8,128)(2,1)S(1)} %get-tuple-element.26) | copy-start | bytes 3538948
  15.2 44.9 %all-to-all-start.1 = ((bf16[64,72,128]{2,1,0:T(8,128)(2,1)}), bf16[64,72,128]{2,1,0:T(8,128)(2,1)S(1)}, u32[]{:S(2)}, u32[]{:S(2)}) async-start(bf16[64,72,128]{2,1,0:T(8,128)(2,1)} %copy-done.3), calls=%async_computation.1 | async-start | bytes 2359296 | tf_op jit(solution)/shard_map/all_to_all | solution.py:365
  31.5 9.1 %collective-permute-start = (f32[32,128]{1,0:T(8,128)S(1)}, f32[32,128]{1,0:T(8,128)S(1)}, u32[]{:S(2)}, u32[]{:S(2)}) collective-permute-start(f32[32,128]{1,0:T(8,128)S(1)} %get-tuple-element.27.first_ref), channel_id=1, source_target_pairs={{0,4},{4,0},{8,12},{12,8},{16,20},{20,16},{24,28},{28,24},{32,36},... | collective-permute-start | bytes 49160 | tf_op jit(solution)/shard_map/ppermute | solution.py:366
  35.8 1.1 %copy-start.4 = (bf16[96,4096]{1,0:T(8,128)(2,1)S(1)}, bf16[96,4096]{1,0:T(8,128)(2,1)}, u32[]{:S(2)}) copy-start(bf16[96,4096]{1,0:T(8,128)(2,1)} %blocks_ref.1) | copy-start | bytes 2359300
  39.4 1.2 %copy-start.2 = (bf16[96,64,128]{2,1,0:T(8,128)(2,1)}, bf16[96,64,128]{2,1,0:T(8,128)(2,1)S(1)}, u32[]{:S(2)}) copy-start(bf16[96,64,128]{2,1,0:T(8,128)(2,1)S(1)} %left.1.rows_ref) | copy-start | bytes 4718596
  60.1 10.5 %copy-start.1 = (bf16[64,72,128]{2,1,0:T(8,128)(2,1)}, bf16[64,72,128]{2,1,0:T(8,128)(2,1)S(1)}, u32[]{:S(2)}) copy-start(bf16[64,72,128]{2,1,0:T(8,128)(2,1)S(1)} %all-to-all-done.1.own_ref.received_ref) | copy-start | bytes 3538948
  60.1 10.5 %collective-permute-start.1 = (bf16[64,72,128]{2,1,0:T(8,128)(2,1)S(1)}, bf16[64,72,128]{2,1,0:T(8,128)(2,1)}, u32[]{:S(2)}, u32[]{:S(2)}) collective-permute-start(bf16[64,72,128]{2,1,0:T(8,128)(2,1)S(1)} %all-to-all-done.1.own_ref.received_ref), channel_id=1, source_target_pairs={{0,4},{4,0},{8,12},{12,8},{16,20},{20,16},{24,28},{28,24},{32,36},... | collective-permute-start | bytes 3538952 | tf_op jit(solution)/shard_map/ppermute | solution.py:396
  67.4 10.6 %all-to-all-start.2 = ((f32[8,8,128]{2,1,0:T(8,128)}), f32[8,8,128]{2,1,0:T(8,128)S(1)}, u32[]{:S(2)}, u32[]{:S(2)}) async-start(f32[8,8,128]{2,1,0:T(8,128)} %sum.1), calls=%async_computation.2 | async-start | bytes 65536 | tf_op jit(solution)/shard_map/all_to_all | solution.py:397

commit v6 on v5

--- a/solution.py
+++ b/solution.py
@@ -200,7 +200,7 @@
         out_ref[copy] = total
 
 
-def top_kernel(core_ref, received_ref, first_ref, other_ref, out_ref, scratch):
+def top_kernel(core_ref, received_ref, first_ref, other_ref, done_ref, out_ref, scratch):
     parts = received_ref.shape[0] // 2
     wide = received_ref.shape[2]
     width = wide // 2
@@ -215,7 +215,7 @@
         out_ref[:, tile * wide : (tile + 1) * wide] = natural[tile : tile + 1]
 
 
-def left_kernel(row_ref, blocks_ref, left_ref, out_ref, spread):
+def left_kernel(row_ref, blocks_ref, left_ref, out_ref, done_ref, spread):
     step = pl.program_id(0)
     count, flat = blocks_ref.shape
     width = left_ref.shape[1]
@@ -224,24 +224,28 @@
     low = iota((width, wide), 1) < width
     for tile in range(tiles):
         spread[tile * count : (tile + 1) * count, :] = blocks_ref[:, tile * wide : (tile + 1) * wide].astype(F32)
-    for index in range(count):
-        block = step * count + index
-        here = spread[pl.ds(index, tiles, stride=count), :]
-        turned = pltpu.roll(here, width, 1)
-        rows = jnp.where(
-            low, jnp.concatenate([here, turned], axis=0), jnp.concatenate([turned, here], axis=0)
-        ).astype(BF16)
-        out_ref[index] = nn(left_ref[row_ref[block]], rows).astype(BF16)
+    for index in range(0, count, 2):
+        products = []
+        for place in range(2):
+            here = spread[pl.ds(index + place, tiles, stride=count), :]
+            turned = pltpu.roll(here, width, 1)
+            rows = jnp.where(
+                low, jnp.concatenate([here, turned], axis=0), jnp.concatenate([turned, here], axis=0)
+            ).astype(BF16)
+            products.append(nn(left_ref[row_ref[step * count + index + place]], rows))
+        out_ref[index // 2] = jnp.where(low, products[0], products[1]).astype(BF16)
+    done_ref[...] = jnp.zeros_like(done_ref)
 
 
 def project_kernel(
     owner_ref, column_ref, core_ref, rows_ref, own_ref, other_ref, out_ref, result, triangles
 ):
     step = pl.program_id(0)
-    count, width, wide = rows_ref.shape
+    pairs, width, wide = rows_ref.shape
+    count = 2 * pairs
     tiles = width // 2
-
     low = iota((tiles, wide), 1) < width
+    none = jnp.zeros((width, wide), BF16)
 
     @pl.when(step == 0)
     def _():
@@ -280,7 +284,8 @@
                 + centre * triangles[cluster, 1]
                 + mirrored * triangles[4 + place, cluster & 1]
             )
-            full = nn(rows_ref[index + place][:, :width], right)
+            weights = [right, none] if place == 0 else [none, right]
+            full = nn(rows_ref[index // 2], jnp.concatenate(weights, axis=0))
             top, bottom = full[:tiles], full[tiles:]
             out = jnp.where(low, top, bottom) + pltpu.roll(jnp.where(low, bottom, top), width, 1)
             result[pl.ds(index + place, tiles, stride=count), :] = out
@@ -361,13 +366,12 @@
         path_high,
         path_low,
     )
-    sent, first = lax.optimization_barrier((sent, first))
     own = lax.all_to_all(sent, "branch", 0, 0, axis_index_groups=same_core)
     first_other = lax.ppermute(first, "branch", partners)
-    square = pl.BlockSpec((ROWS, width, wide), lambda i, *_: (i, 0, 0))
-    rows = pl.pallas_call(
+    square = pl.BlockSpec((ROWS // 2, width, wide), lambda i, *_: (i, 0, 0))
+    rows, done = pl.pallas_call(
         left_kernel,
-        out_shape=shape((blk, width, wide), BF16),
+        out_shape=[shape((blk // 2, width, wide), BF16), shape((8, wide), F32)],
         grid_spec=pltpu.PrefetchScalarGridSpec(
             num_scalar_prefetch=1,
             grid=(blk // ROWS,),
@@ -375,7 +379,7 @@
                 pl.BlockSpec((ROWS, width * width), lambda i, *_: (i, 0)),
                 pl.BlockSpec((nodes, width, width), lambda i, *_: (0, 0, 0)),
             ],
-            out_specs=square,
+            out_specs=[square, pl.BlockSpec((8, wide), lambda i, *_: (0, 0))],
             scratch_shapes=[pltpu.VMEM((ROWS * half, wide), F32)],
         ),
         compiler_params=SMALL,
@@ -384,7 +388,7 @@
         ),
         name="left",
     )(row_cluster, couplings, left)
-    own, first_other, rows = lax.optimization_barrier((own, first_other, rows))
+    own, first_other, done = lax.optimization_barrier((own, first_other, done))
     summed = pl.pallas_call(
         sum_kernel,
         out_shape=shape((2 * parts, 8, wide), F32),
@@ -410,7 +414,7 @@
                 pltpu.VMEM((6, 2, width, wide), BF16),
             ],
         ),
-        compiler_params=pltpu.CompilerParams(vmem_limit_bytes=56 * 1024 * 1024),
+        compiler_params=pltpu.CompilerParams(vmem_limit_bytes=12 * 1024 * 1024),
         cost_estimate=pl.CostEstimate(
             flops=8 * blk * width**3, bytes_accessed=6 * blk * width * width, transcendentals=0
         ),
@@ -420,12 +424,12 @@
     upper_grams = pl.pallas_call(
         top_kernel,
         out_shape=shape((1, width * width), F32),
-        in_specs=[SMEM, VMEM, VMEM, VMEM],
+        in_specs=[SMEM, VMEM, VMEM, VMEM, VMEM],
         out_specs=VMEM,
         scratch_shapes=[pltpu.VMEM((width, width), F32)],
         compiler_params=SMALL,
         name="top",
-    )(core[None], quarters, first, first_other)
+    )(core[None], quarters, first, first_other, done)
     return (upper_grams, projected)
 
 

time: 79.5 us -> 79.2 us (level)
  Pallas kernels: 15.2 us -> 13.8 us
  local copies, waits for them, and re-layouts: 5.98 us -> 6.82 us
    pallas_call x1, Pallas kernels: 7.28 us -> 5.9 us  [on_device(): pl.pallas_call(project_kernel, out_shape=shape((blk, width * width), F32)...]
    unnamed x20 -> x24, local copies, waits for them, and re-layouts: 4.52 us -> 5.36 us
  transfers between devices with their start and end apart: 5 -> 5, of which waited for: 2 -> 2; matrix products, arithmetic and copies ran while one was open for 2% -> 2% of each run, Pallas kernels for 15% -> 13%
where the time goes in v6:
time: 79.2 us; the launch traced here: 78.6 us
  starting transfers between devices  35.3 us (45%)
  waiting for transfers between devices  21.8 us (28%)
  Pallas kernels  13.8 us (17%)
  local copies, waits for them, and re-layouts  6.82 us (9%)
  between operations  0.85 us (1%)
    all_to_all x1, waiting for transfers between devices, on_device(): own = lax.all_to_all(sent, 'branch', 0, 0, axis_index_groups=same_core)  19.8 us
    all_to_all x1, starting transfers between devices, on_device(): own = lax.all_to_all(sent, 'branch', 0, 0, axis_index_groups=same_core)  16.3 us
    ppermute x1, starting transfers between devices, on_device(): other = lax.ppermute(own, 'branch', partners)  6.56 us
    pallas_call x1, Pallas kernels, on_device(): pl.pallas_call(project_kernel, out_shape=shape((blk, width * width), F32)...  5.9 us
    unnamed x24, local copies, waits for them, and re-layouts  5.36 us
    all_to_all x1, starting transfers between devices, on_device(): gathered = lax.all_to_all(partial_sums, 'level', 0, 0)  4.84 us
    ppermute x1, starting transfers between devices, on_device(): first_other = lax.ppermute(first, 'branch', partners)  4.29 us
    all_to_all x1, starting transfers between devices, on_device(): lax.all_to_all(summed, ('branch', 'level'), 0, 0, axis_index_groups=same_...  3.28 us
  transfers between devices with their start and end apart: 5, of which 2 were waited for; matrix products, arithmetic and copies ran while one was open for 2% of the time, Pallas kernels for 13%

profile of v6, /device:TPU:1, one launch (start us, length us, event | category | flops | bytes accessed | tf_op | source)
XLA Modules:
  0.0 78.6 jit_solution(13097927363419109403)
XLA Ops:
  0.6 0.0 copy-start
  0.6 0.0 copy-start.5
  0.7 1.2 %copy-done.5 = bf16[4,64,1024]{2,1,0:T(8,128)(2,1)S(1)} copy-done((bf16[4,64,1024]{2,1,0:T(8,128)(2,1)S(1)}, bf16[4,64,1024]{2,1,0:T(8,128)(2,1)}, u32[]{:S(2)}) %copy-start.5) | copy-done | bytes 524312
  1.8 0.0 copy-start.10
  1.8 0.0 copy-start.11
  1.8 0.0 copy-start.7
  1.8 1.0 %gram.1 = f32[4,72,128]{2,1,0:T(8,128)} custom-call(bf16[4,64,1024]{2,1,0:T(8,128)(2,1)S(1)} %copy-done.5), custom_call_target="tpu_custom_call" | custom-call | tf_op jit(solution)/shard_map/gram/pallas_call | solution.py:325
  2.8 4.8 %all-to-all-start = ((f32[4,72,128]{2,1,0:T(8,128)}), f32[4,72,128]{2,1,0:T(8,128)S(1)}, u32[]{:S(2)}, u32[]{:S(2)}) async-start(f32[4,72,128]{2,1,0:T(8,128)} %gram.1), calls=%async_computation | async-start | bytes 294912 | tf_op jit(solution)/shard_map/all_to_all | solution.py:336
  7.7 0.0 copy-done
  7.7 0.6 gather_fusion.1
  8.3 0.1 gather.12
  8.4 0.0 copy-done.10
  8.4 0.6 gather_fusion
  9.1 0.1 broadcast_select_fusion.path_ref
  9.2 0.0 copy-start.6
  9.2 0.0 copy-done.11
  9.2 0.1 reshape.46.bottom_ref
  9.3 1.3 %path.1 = (bf16[7,64,64]{2,1,0:T(8,128)(2,1)S(1)}, bf16[7,64,64]{2,1,0:T(8,128)(2,1)S(1)}) custom-call(s32[7]{0:T(128)S(1)} %broadcast_select_fusion.1.rank_ref, bf16[7,64,64]{2,1,0:T(8,128)(2,1)S(1)} %broadcast_select_fusion.path_ref), custom_call_target="tpu_custom_call" | custom-call | tf_op jit(solution)/shard_map/path/pallas_call | solution.py:340
  10.7 1.9 %all-to-all-done.parts_ref = f32[4,72,128]{2,1,0:T(8,128)S(1)} async-done(((f32[4,72,128]{2,1,0:T(8,128)}), f32[4,72,128]{2,1,0:T(8,128)S(1)}, u32[]{:S(2)}, u32[]{:S(2)}) %all-to-all-start) | async-done | bytes 147488 | tf_op jit(solution)/shard_map/all_to_all | solution.py:336
  12.6 0.0 copy-done.7
  12.6 1.6 %near.1 = (bf16[4,64,64]{2,1,0:T(8,128)(2,1)S(1)}, bf16[64,72,128]{2,1,0:T(8,128)(2,1)S(1)}, f32[32,128]{1,0:T(8,128)S(1)}) custom-call(s32[4]{0:T(128)S(1)} %copy-done.7, s32[1]{0:T(128)} %bitcast.2.place_ref, s32[1]{0:T(128)} %bitcast.3.level_ref, f32[4,72,128]{2,1,0:T(8,128)S(1)} %all-to-all-done.parts_ref, bf16[4,64,64]{2,1,0:T(8,128)(2,1)S(1)} %reshape.46.bottom_ref, ...), custom_call_target="tpu_custom_call" | custom-call | tf_op jit(solution)/shard_map/near/pallas_call | solution.py:348
  14.1 0.0 copy-start.1
  14.2 1.0 %copy-done.1 = bf16[64,72,128]{2,1,0:T(8,128)(2,1)} copy-done((bf16[64,72,128]{2,1,0:T(8,128)(2,1)}, bf16[64,72,128]{2,1,0:T(8,128)(2,1)S(1)}, u32[]{:S(2)}) %copy-start.1) | copy-done | bytes 1179672
  15.2 16.3 %all-to-all-start.1 = ((bf16[64,72,128]{2,1,0:T(8,128)(2,1)}), bf16[64,72,128]{2,1,0:T(8,128)(2,1)S(1)}, u32[]{:S(2)}, u32[]{:S(2)}) async-start(bf16[64,72,128]{2,1,0:T(8,128)(2,1)} %copy-done.1), calls=%async_computation.1 | async-start | bytes 2359296 | tf_op jit(solution)/shard_map/all_to_all | solution.py:369
  31.5 0.0 copy-start.8
  31.5 0.0 copy-start.9
  31.5 4.3 %collective-permute-start = (f32[32,128]{1,0:T(8,128)S(1)}, f32[32,128]{1,0:T(8,128)S(1)}, u32[]{:S(2)}, u32[]{:S(2)}) collective-permute-start(f32[32,128]{1,0:T(8,128)S(1)} %get-tuple-element.27.first_ref), channel_id=1, source_target_pairs={{0,4},{4,0},{8,12},{12,8},{16,20},{20,16},{24,28},{28,24},{32,36},... | collective-permute-start | bytes 49160 | tf_op jit(solution)/shard_map/ppermute | solution.py:370
  35.8 0.0 copy-done.6
  35.8 0.0 copy-start.2
  35.8 1.1 %copy-done.2 = bf16[96,4096]{1,0:T(8,128)(2,1)S(1)} copy-done((bf16[96,4096]{1,0:T(8,128)(2,1)S(1)}, bf16[96,4096]{1,0:T(8,128)(2,1)}, u32[]{:S(2)}) %copy-start.2) | copy-done | bytes 786456
  37.0 2.4 %left.1 = (bf16[48,64,128]{2,1,0:T(8,128)(2,1)S(1)}, f32[8,128]{1,0:T(8,128)S(1)}) custom-call(s32[96]{0:T(128)S(1)} %copy-done.6, bf16[96,4096]{1,0:T(8,128)(2,1)S(1)} %copy-done.2, bf16[4,64,64]{2,1,0:T(8,128)(2,1)S(1)} %get-tuple-element.24.left_ref), custom_call_target="tpu_custom_call" | custom-call | flops 100663296 | bytes 1572864 | tf_op jit(solution)/shard_map/left/pallas_call | solution.py:372
  39.4 0.0 copy-start.3
  39.4 0.9 %copy-done.3 = bf16[48,64,128]{2,1,0:T(8,128)(2,1)} copy-done((bf16[48,64,128]{2,1,0:T(8,128)(2,1)}, bf16[48,64,128]{2,1,0:T(8,128)(2,1)S(1)}, u32[]{:S(2)}) %copy-start.3) | copy-done | bytes 786456
  40.3 0.0 collective-permute-done.other_ref
  40.3 19.8 %all-to-all-done.1.own_ref.received_ref = bf16[64,72,128]{2,1,0:T(8,128)(2,1)S(1)} async-done(((bf16[64,72,128]{2,1,0:T(8,128)(2,1)}), bf16[64,72,128]{2,1,0:T(8,128)(2,1)S(1)}, u32[]{:S(2)}, u32[]{:S(2)}) %all-to-all-start.1) | async-done | bytes 1179680 | tf_op jit(solution)/shard_map/all_to_all | solution.py:369
  60.1 6.6 %collective-permute-start.1 = (bf16[64,72,128]{2,1,0:T(8,128)(2,1)S(1)}, bf16[64,72,128]{2,1,0:T(8,128)(2,1)}, u32[]{:S(2)}, u32[]{:S(2)}) collective-permute-start(bf16[64,72,128]{2,1,0:T(8,128)(2,1)S(1)} %all-to-all-done.1.own_ref.received_ref), channel_id=1, source_target_pairs={{0,4},{4,0},{8,12},{12,8},{16,20},{20,16},{24,28},{28,24},{32,36},... | collective-permute-start | bytes 3538952 | tf_op jit(solution)/shard_map/ppermute | solution.py:400
  66.7 0.7 sum.1
  67.4 3.3 %all-to-all-start.2 = ((f32[8,8,128]{2,1,0:T(8,128)}), f32[8,8,128]{2,1,0:T(8,128)S(1)}, u32[]{:S(2)}, u32[]{:S(2)}) async-start(f32[8,8,128]{2,1,0:T(8,128)} %sum.1), calls=%async_computation.2 | async-start | bytes 65536 | tf_op jit(solution)/shard_map/all_to_all | solution.py:401
  70.7 0.0 collective-permute-done.1.other_ref
  70.7 0.0 copy-done.8
  70.7 0.0 copy-done.9
  70.7 0.0 copy-start.4
  70.7 1.1 %copy-done.4 = bf16[48,64,128]{2,1,0:T(8,128)(2,1)S(1)} copy-done((bf16[48,64,128]{2,1,0:T(8,128)(2,1)S(1)}, bf16[48,64,128]{2,1,0:T(8,128)(2,1)}, u32[]{:S(2)}) %copy-start.4) | copy-done | bytes 786456
  71.8 5.9 %project.1 = f32[96,4096]{1,0:T(8,128)} custom-call(s32[96]{0:T(128)S(1)} %bitcast.6, s32[96]{0:T(128)S(1)} %copy-done.9, s32[1]{0:T(128)} %bitcast.core_ref, bf16[48,64,128]{2,1,0:T(8,128)(2,1)S(1)} %copy-done.4, bf16[64,72,128]{2,1,0:T(8,128)(2,1)S(1)} %all-to-all-done.1.own_ref.received_ref, bf16[64,72,128]{2,1,0:T(8,128)(2,1)} %collective-permute-done.1.other_ref), custom_call_target="tpu_custom_call" | custom-call | flops 201326592 | bytes 2359296 | tf_op jit(solution)/shard_map/project/pallas_call | solution.py:404
  77.7 0.0 all-to-all-done.2.received_ref
  77.7 0.9 %top.1 = f32[1,4096]{1,0:T(1,128)} custom-call(s32[1]{0:T(128)} %bitcast.core_ref, f32[8,8,128]{2,1,0:T(8,128)S(1)} %all-to-all-done.2.received_ref, f32[32,128]{1,0:T(8,128)S(1)} %get-tuple-element.27.first_ref, f32[32,128]{1,0:T(8,128)S(1)} %collective-permute-done.other_ref, f32[8,128]{1,0:T(8,128)S(1)} %get-tuple-element.32.done_ref), custom_call_target="tpu_custom_call" | custom-call | tf_op jit(solution)/shard_map/top/pallas_call | solution.py:424
  (4 shorter events, 0.0 us)
Async XLA Ops:
  0.6 7.1 %copy-start = (bf16[254,4096]{1,0:T(8,128)(2,1)S(1)}, bf16[254,4096]{1,0:T(8,128)(2,1)}, u32[]{:S(2)}) copy-start(bf16[254,4096]{1,0:T(8,128)(2,1)} %param.12) | copy-start | bytes 6242308
  0.6 1.2 %copy-start.5 = (bf16[4,64,1024]{2,1,0:T(8,128)(2,1)S(1)}, bf16[4,64,1024]{2,1,0:T(8,128)(2,1)}, u32[]{:S(2)}) copy-start(bf16[4,64,1024]{2,1,0:T(8,128)(2,1)} %basis_ref.1) | copy-start | bytes 1572868
  1.8 6.6 %copy-start.10 = (s32[254]{0:T(256)S(1)}, s32[254]{0:T(256)}, u32[]{:S(2)}) copy-start(s32[254]{0:T(256)} %param.13) | copy-start | bytes 3052
  1.8 7.3 %copy-start.11 = (bf16[4,4096]{1,0:T(4,128)(2,1)S(1)}, bf16[4,4096]{1,0:T(4,128)(2,1)}, u32[]{:S(2)}) copy-start(bf16[4,4096]{1,0:T(4,128)(2,1)} %param.10) | copy-start | bytes 98308
  1.8 10.7 %copy-start.7 = (s32[4]{0:T(128)S(1)}, s32[4]{0:T(128)}, u32[]{:S(2)}) copy-start(s32[4]{0:T(128)} %rank_ref.1) | copy-start | bytes 52
  2.8 9.8 %all-to-all-start = ((f32[4,72,128]{2,1,0:T(8,128)}), f32[4,72,128]{2,1,0:T(8,128)S(1)}, u32[]{:S(2)}, u32[]{:S(2)}) async-start(f32[4,72,128]{2,1,0:T(8,128)} %gram.1), calls=%async_computation | async-start | bytes 294912 | tf_op jit(solution)/shard_map/all_to_all | solution.py:336
  9.2 26.7 %copy-start.6 = (s32[96]{0:T(128)S(1)}, s32[96]{0:T(128)}, u32[]{:S(2)}) copy-start(s32[96]{0:T(128)} %row_ref.1) | copy-start | bytes 1156
  14.1 1.0 %copy-start.1 = (bf16[64,72,128]{2,1,0:T(8,128)(2,1)}, bf16[64,72,128]{2,1,0:T(8,128)(2,1)S(1)}, u32[]{:S(2)}) copy-start(bf16[64,72,128]{2,1,0:T(8,128)(2,1)S(1)} %get-tuple-element.26) | copy-start | bytes 3538948
  15.2 44.9 %all-to-all-start.1 = ((bf16[64,72,128]{2,1,0:T(8,128)(2,1)}), bf16[64,72,128]{2,1,0:T(8,128)(2,1)S(1)}, u32[]{:S(2)}, u32[]{:S(2)}) async-start(bf16[64,72,128]{2,1,0:T(8,128)(2,1)} %copy-done.1), calls=%async_computation.1 | async-start | bytes 2359296 | tf_op jit(solution)/shard_map/all_to_all | solution.py:369
  31.5 39.2 %copy-start.8 = (s32[96,1]{0,1:T(1,128)S(1)}, s32[96,1]{0,1:T(1,128)}, u32[]{:S(2)}) copy-start(s32[96,1]{0,1:T(1,128)} %param.16) | copy-start | bytes 1156
  31.5 39.2 %copy-start.9 = (s32[96]{0:T(128)S(1)}, s32[96]{0:T(128)}, u32[]{:S(2)}) copy-start(s32[96]{0:T(128)} %column_ref.1) | copy-start | bytes 1156
  31.5 8.8 %collective-permute-start = (f32[32,128]{1,0:T(8,128)S(1)}, f32[32,128]{1,0:T(8,128)S(1)}, u32[]{:S(2)}, u32[]{:S(2)}) collective-permute-start(f32[32,128]{1,0:T(8,128)S(1)} %get-tuple-element.27.first_ref), channel_id=1, source_target_pairs={{0,4},{4,0},{8,12},{12,8},{16,20},{20,16},{24,28},{28,24},{32,36},... | collective-permute-start | bytes 49160 | tf_op jit(solution)/shard_map/ppermute | solution.py:370
  35.8 1.1 %copy-start.2 = (bf16[96,4096]{1,0:T(8,128)(2,1)S(1)}, bf16[96,4096]{1,0:T(8,128)(2,1)}, u32[]{:S(2)}) copy-start(bf16[96,4096]{1,0:T(8,128)(2,1)} %blocks_ref.1) | copy-start | bytes 2359300
  39.4 0.9 %copy-start.3 = (bf16[48,64,128]{2,1,0:T(8,128)(2,1)}, bf16[48,64,128]{2,1,0:T(8,128)(2,1)S(1)}, u32[]{:S(2)}) copy-start(bf16[48,64,128]{2,1,0:T(8,128)(2,1)S(1)} %get-tuple-element.25.rows_ref) | copy-start | bytes 2359300
  60.1 10.6 %collective-permute-start.1 = (bf16[64,72,128]{2,1,0:T(8,128)(2,1)S(1)}, bf16[64,72,128]{2,1,0:T(8,128)(2,1)}, u32[]{:S(2)}, u32[]{:S(2)}) collective-permute-start(bf16[64,72,128]{2,1,0:T(8,128)(2,1)S(1)} %all-to-all-done.1.own_ref.received_ref), channel_id=1, source_target_pairs={{0,4},{4,0},{8,12},{12,8},{16,20},{20,16},{24,28},{28,24},{32,36},... | collective-permute-start | bytes 3538952 | tf_op jit(solution)/shard_map/ppermute | solution.py:400
  67.4 10.4 %all-to-all-start.2 = ((f32[8,8,128]{2,1,0:T(8,128)}), f32[8,8,128]{2,1,0:T(8,128)S(1)}, u32[]{:S(2)}, u32[]{:S(2)}) async-start(f32[8,8,128]{2,1,0:T(8,128)} %sum.1), calls=%async_computation.2 | async-start | bytes 65536 | tf_op jit(solution)/shard_map/all_to_all | solution.py:401
  70.7 1.1 %copy-start.4 = (bf16[48,64,128]{2,1,0:T(8,128)(2,1)S(1)}, bf16[48,64,128]{2,1,0:T(8,128)(2,1)}, u32[]{:S(2)}) copy-start(bf16[48,64,128]{2,1,0:T(8,128)(2,1)} %copy-done.3) | copy-start | bytes 2359300

commit v7 on v6

--- a/solution.py
+++ b/solution.py
@@ -1,3 +1,5 @@
+import functools
+
 import jax
 import jax.numpy as jnp
 from jax import lax
@@ -121,7 +123,7 @@
 
 
 def near_kernel(
-    rank_ref, place_ref, level_ref, parts_ref, bottom_ref, high_ref, low_ref, left_ref, sent_ref, first_ref, tiles
+    parts, rank_ref, place_ref, level_ref, parts_ref, bottom_ref, high_ref, low_ref, left_ref, sent_ref, first_ref, tiles
 ):
     nodes, width, _ = bottom_ref.shape
     wide = 2 * width
@@ -152,7 +154,6 @@
     lower = jnp.where(lane < width, rank_ref[1], rank_ref[3])
     diagonal = jnp.where((lane & (width - 1)) < lower, diagonal, 0.0)
     tiles[0] = jnp.concatenate([diagonal, jnp.zeros((7, wide), F32)], axis=0)
-    parts = parts_ref.shape[0]
     share = half // (2 * parts)
     for height in range(heights):
         path = (high_ref[height], low_ref[height])
@@ -324,7 +325,7 @@
 
     partial_sums = pl.pallas_call(
         gram_kernel,
-        out_shape=shape((parts, width + 8, wide), F32),
+        out_shape=shape((1, width + 8, wide), F32),
         in_specs=[VMEM],
         out_specs=VMEM,
         compiler_params=SMALL,
@@ -333,7 +334,8 @@
     partial_sums, upper_transfer, upper_rank, bottom_transfer = lax.optimization_barrier(
         (partial_sums, upper_transfer, upper_rank, bottom_transfer)
     )
-    gathered = lax.all_to_all(partial_sums, "level", 0, 0)
+    same_branch = [list(range(parts * branch, parts * (branch + 1))) for branch in range(branches)]
+    gathered = lax.psum(partial_sums, ("branch", "level"), axis_index_groups=same_branch)
     heights = jnp.arange(levels, dtype=jnp.int32)
     slots = 2 * branches - jnp.right_shift(2 * branches, heights) + jnp.right_shift(me_branch, heights)
     path = jnp.take(upper_transfer, slots, axis=0).reshape(levels, width, width)
@@ -346,7 +348,7 @@
         name="path",
     )(jnp.take(upper_rank, slots, axis=0), path)
     left, sent, first = pl.pallas_call(
-        near_kernel,
+        functools.partial(near_kernel, parts),
         out_shape=[
             shape((nodes, width, width), BF16),
             shape((branches // 2, width + 8, wide), BF16),
@@ -416,7 +418,7 @@
         ),
         compiler_params=pltpu.CompilerParams(vmem_limit_bytes=12 * 1024 * 1024),
         cost_estimate=pl.CostEstimate(
-            flops=8 * blk * width**3, bytes_accessed=6 * blk * width * width, transcendentals=0
+            flops=800 * blk * width**3, bytes_accessed=6 * blk * width * width, transcendentals=0
         ),
         name="project",
     )(column_owner[:, 0], column_cluster, core[None], rows, own, other)

time: 79.2 us -> 86.3 us (1.090)
  blocking collectives: 0 us -> 14.6 us
  waiting for transfers between devices: 21.8 us -> 14.6 us
    psum x0 -> x1, blocking collectives: none -> 14.6 us  [on_device(): lax.psum(partial_sums, ('branch', 'level'), axis_index_groups=same_branch)]
    all_to_all x1, waiting for transfers between devices: 19.8 us -> 14.5 us  [on_device(): own = lax.all_to_all(sent, 'branch', 0, 0, axis_index_groups=same_core)]
    all_to_all x1 -> x0, starting transfers between devices: 4.84 us -> none  [on_device(): gathered = lax.all_to_all(partial_sums, 'level', 0, 0)]
    ppermute x1, starting transfers between devices: 6.56 us -> 9.55 us  [on_device(): other = lax.ppermute(own, 'branch', partners)]
    ppermute x1, starting transfers between devices: 4.29 us -> 6.62 us  [on_device(): first_other = lax.ppermute(first, 'branch', partners)]
    all_to_all x1 -> x0, waiting for transfers between devices: 1.92 us -> none  [on_device(): gathered = lax.all_to_all(partial_sums, 'level', 0, 0)]
  transfers between devices with their start and end apart: 5 -> 4, of which waited for: 2 -> 1; matrix products, arithmetic and copies ran while one was open for 2% -> 0% of each run, Pallas kernels for 13% -> 10%
where the time goes in v7:
time: 86.3 us; the launch traced here: 85.8 us
  starting transfers between devices  35.6 us (41%)
  blocking collectives  14.6 us (17%)
  waiting for transfers between devices  14.6 us (17%)
  Pallas kernels  13.1 us (15%)
  local copies, waits for them, and re-layouts  6.99 us (8%)
  between operations  0.88 us (1%)
    all_to_all x1, starting transfers between devices, on_device(): own = lax.all_to_all(sent, 'branch', 0, 0, axis_index_groups=same_core)  16.1 us
    psum x1, blocking collectives, on_device(): lax.psum(partial_sums, ('branch', 'level'), axis_index_groups=same_branch)  14.6 us
    all_to_all x1, waiting for transfers between devices, on_device(): own = lax.all_to_all(sent, 'branch', 0, 0, axis_index_groups=same_core)  14.5 us
    ppermute x1, starting transfers between devices, on_device(): other = lax.ppermute(own, 'branch', partners)  9.55 us
    ppermute x1, starting transfers between devices, on_device(): first_other = lax.ppermute(first, 'branch', partners)  6.62 us
    pallas_call x1, Pallas kernels, on_device(): pl.pallas_call(project_kernel, out_shape=shape((blk, width * width), F32)...  5.89 us
    unnamed x24, local copies, waits for them, and re-layouts  5.53 us
    all_to_all x1, starting transfers between devices, on_device(): lax.all_to_all(summed, ('branch', 'level'), 0, 0, axis_index_groups=same_...  3.28 us
  transfers between devices with their start and end apart: 4, of which 1 were waited for; matrix products, arithmetic and copies ran while one was open for 0% of the time, Pallas kernels for 10%

profile of v7, /device:TPU:1, one launch (start us, length us, event | category | flops | bytes accessed | tf_op | source)
XLA Modules:
  0.0 85.8 jit_solution(14420849169524183503)
XLA Ops:
  0.6 0.0 copy-start
  0.6 0.0 copy-start.10
  0.7 0.0 copy-start.4
  0.7 0.0 copy-start.3
  0.7 1.2 %copy-done.3 = bf16[4,64,1024]{2,1,0:T(8,128)(2,1)S(1)} copy-done((bf16[4,64,1024]{2,1,0:T(8,128)(2,1)S(1)}, bf16[4,64,1024]{2,1,0:T(8,128)(2,1)}, u32[]{:S(2)}) %copy-start.3) | copy-done | bytes 524312
  1.9 0.0 copy-start.11
  1.9 0.3 gram.1
  2.2 0.2 copy-done
  2.4 0.6 gather_fusion.1
  3.0 0.1 gather.12
  3.1 0.0 copy-done.10
  3.1 0.6 gather_fusion
  3.8 0.0 copy-done.11
  3.8 0.1 reshape.46.bottom_ref
  3.9 0.0 copy-start.5
  3.9 14.6 %psum.7.parts_ref = f32[1,72,128]{2,1,0:T(8,128)S(1)} all-reduce(f32[1,72,128]{2,1,0:T(8,128)S(1)} %gram.1), channel_id=1, replica_groups={{0,1,2,3},{4,5,6,7},{8,9,10,11},{12,13,14,15},{16,17,18,19},{20,21,22,2..., use_global_device_ids=true, to_apply=%region_0.0 | all-reduce | flops 9216 | bytes 73728 | tf_op jit(solution)/shard_map/psum | solution.py:338
  18.5 0.1 broadcast_select_fusion.path_ref
  18.6 1.3 %path.1 = (bf16[7,64,64]{2,1,0:T(8,128)(2,1)S(1)}, bf16[7,64,64]{2,1,0:T(8,128)(2,1)S(1)}) custom-call(s32[7]{0:T(128)S(1)} %broadcast_select_fusion.1.rank_ref, bf16[7,64,64]{2,1,0:T(8,128)(2,1)S(1)} %broadcast_select_fusion.path_ref), custom_call_target="tpu_custom_call" | custom-call | tf_op jit(solution)/shard_map/path/pallas_call | solution.py:342
  19.9 0.0 copy-done.4
  19.9 1.6 %near.1 = (bf16[4,64,64]{2,1,0:T(8,128)(2,1)S(1)}, bf16[64,72,128]{2,1,0:T(8,128)(2,1)S(1)}, f32[32,128]{1,0:T(8,128)S(1)}) custom-call(s32[4]{0:T(128)S(1)} %copy-done.4, s32[1]{0:T(128)} %bitcast.2.place_ref, s32[1]{0:T(128)} %bitcast.3.level_ref, f32[1,72,128]{2,1,0:T(8,128)S(1)} %psum.7.parts_ref, bf16[4,64,64]{2,1,0:T(8,128)(2,1)S(1)} %reshape.46.bottom_ref, ...), custom_call_target="tpu_custom_call" | custom-call | tf_op jit(solution)/shard_map/near/pallas_call | solution.py:350
  21.5 0.0 copy-start.1
  21.5 1.0 %copy-done.1 = bf16[64,72,128]{2,1,0:T(8,128)(2,1)} copy-done((bf16[64,72,128]{2,1,0:T(8,128)(2,1)}, bf16[64,72,128]{2,1,0:T(8,128)(2,1)S(1)}, u32[]{:S(2)}) %copy-start.1) | copy-done | bytes 1179672
  22.5 16.1 %all-to-all-start = ((bf16[64,72,128]{2,1,0:T(8,128)(2,1)}), bf16[64,72,128]{2,1,0:T(8,128)(2,1)S(1)}, u32[]{:S(2)}, u32[]{:S(2)}) async-start(bf16[64,72,128]{2,1,0:T(8,128)(2,1)} %copy-done.1), calls=%async_computation | async-start | bytes 2359296 | tf_op jit(solution)/shard_map/all_to_all | solution.py:371
  38.7 0.0 copy-start.8
  38.7 0.0 copy-start.9
  38.7 6.6 %collective-permute-start = (f32[32,128]{1,0:T(8,128)S(1)}, f32[32,128]{1,0:T(8,128)S(1)}, u32[]{:S(2)}, u32[]{:S(2)}) collective-permute-start(f32[32,128]{1,0:T(8,128)S(1)} %get-tuple-element.27.first_ref), channel_id=1, source_target_pairs={{0,4},{4,0},{8,12},{12,8},{16,20},{20,16},{24,28},{28,24},{32,36},... | collective-permute-start | bytes 49160 | tf_op jit(solution)/shard_map/ppermute | solution.py:372
  45.3 0.0 copy-done.5
  45.3 0.0 copy-start.2
  45.3 1.1 %copy-done.2 = bf16[96,4096]{1,0:T(8,128)(2,1)S(1)} copy-done((bf16[96,4096]{1,0:T(8,128)(2,1)S(1)}, bf16[96,4096]{1,0:T(8,128)(2,1)}, u32[]{:S(2)}) %copy-start.2) | copy-done | bytes 786456
  46.5 2.4 %left.1 = (bf16[48,64,128]{2,1,0:T(8,128)(2,1)S(1)}, f32[8,128]{1,0:T(8,128)S(1)}) custom-call(s32[96]{0:T(128)S(1)} %copy-done.5, bf16[96,4096]{1,0:T(8,128)(2,1)S(1)} %copy-done.2, bf16[4,64,64]{2,1,0:T(8,128)(2,1)S(1)} %get-tuple-element.24.left_ref), custom_call_target="tpu_custom_call" | custom-call | flops 100663296 | bytes 1572864 | tf_op jit(solution)/shard_map/left/pallas_call | solution.py:374
  48.9 0.0 copy-start.6
  48.9 0.9 %copy-done.6 = bf16[48,64,128]{2,1,0:T(8,128)(2,1)} copy-done((bf16[48,64,128]{2,1,0:T(8,128)(2,1)}, bf16[48,64,128]{2,1,0:T(8,128)(2,1)S(1)}, u32[]{:S(2)}) %copy-start.6) | copy-done | bytes 786456
  49.8 0.0 collective-permute-done.other_ref
  49.8 14.5 %all-to-all-done.own_ref.received_ref = bf16[64,72,128]{2,1,0:T(8,128)(2,1)S(1)} async-done(((bf16[64,72,128]{2,1,0:T(8,128)(2,1)}), bf16[64,72,128]{2,1,0:T(8,128)(2,1)S(1)}, u32[]{:S(2)}, u32[]{:S(2)}) %all-to-all-start) | async-done | bytes 1179680 | tf_op jit(solution)/shard_map/all_to_all | solution.py:371
  64.3 9.5 %collective-permute-start.1 = (bf16[64,72,128]{2,1,0:T(8,128)(2,1)S(1)}, bf16[64,72,128]{2,1,0:T(8,128)(2,1)}, u32[]{:S(2)}, u32[]{:S(2)}) collective-permute-start(bf16[64,72,128]{2,1,0:T(8,128)(2,1)S(1)} %all-to-all-done.own_ref.received_ref), channel_id=1, source_target_pairs={{0,4},{4,0},{8,12},{12,8},{16,20},{20,16},{24,28},{28,24},{32,36},... | collective-permute-start | bytes 3538952 | tf_op jit(solution)/shard_map/ppermute | solution.py:402
  73.9 0.7 sum.1
  74.6 3.3 %all-to-all-start.1 = ((f32[8,8,128]{2,1,0:T(8,128)}), f32[8,8,128]{2,1,0:T(8,128)S(1)}, u32[]{:S(2)}, u32[]{:S(2)}) async-start(f32[8,8,128]{2,1,0:T(8,128)} %sum.1), calls=%async_computation.1 | async-start | bytes 65536 | tf_op jit(solution)/shard_map/all_to_all | solution.py:403
  77.9 0.0 collective-permute-done.1.other_ref
  77.9 0.0 copy-done.8
  77.9 0.0 copy-done.9
  77.9 0.0 copy-start.7
  77.9 1.1 %copy-done.7 = bf16[48,64,128]{2,1,0:T(8,128)(2,1)S(1)} copy-done((bf16[48,64,128]{2,1,0:T(8,128)(2,1)S(1)}, bf16[48,64,128]{2,1,0:T(8,128)(2,1)}, u32[]{:S(2)}) %copy-start.7) | copy-done | bytes 786456
  79.0 5.9 %project.1 = f32[96,4096]{1,0:T(8,128)} custom-call(s32[96]{0:T(128)S(1)} %bitcast.6, s32[96]{0:T(128)S(1)} %copy-done.9, s32[1]{0:T(128)} %bitcast.core_ref, bf16[48,64,128]{2,1,0:T(8,128)(2,1)S(1)} %copy-done.7, bf16[64,72,128]{2,1,0:T(8,128)(2,1)S(1)} %all-to-all-done.own_ref.received_ref, bf16[64,72,128]{2,1,0:T(8,128)(2,1)} %collective-permute-done.1.other_ref), custom_call_target="tpu_custom_call" | custom-call | flops 20132659200 | bytes 2359296 | tf_op jit(solution)/shard_map/project/pallas_call | solution.py:406
  84.9 0.0 all-to-all-done.1.received_ref
  84.9 0.9 %top.1 = f32[1,4096]{1,0:T(1,128)} custom-call(s32[1]{0:T(128)} %bitcast.core_ref, f32[8,8,128]{2,1,0:T(8,128)S(1)} %all-to-all-done.1.received_ref, f32[32,128]{1,0:T(8,128)S(1)} %get-tuple-element.27.first_ref, f32[32,128]{1,0:T(8,128)S(1)} %collective-permute-done.other_ref, f32[8,128]{1,0:T(8,128)S(1)} %get-tuple-element.32.done_ref), custom_call_target="tpu_custom_call" | custom-call | tf_op jit(solution)/shard_map/top/pallas_call | solution.py:426
  (4 shorter events, 0.0 us)
Async XLA Ops:
  0.6 1.8 %copy-start = (bf16[254,4096]{1,0:T(8,128)(2,1)S(1)}, bf16[254,4096]{1,0:T(8,128)(2,1)}, u32[]{:S(2)}) copy-start(bf16[254,4096]{1,0:T(8,128)(2,1)} %param.12) | copy-start | bytes 6242308
  0.6 2.4 %copy-start.10 = (s32[254]{0:T(256)S(1)}, s32[254]{0:T(256)}, u32[]{:S(2)}) copy-start(s32[254]{0:T(256)} %param.13) | copy-start | bytes 3052
  0.7 19.3 %copy-start.4 = (s32[4]{0:T(128)S(1)}, s32[4]{0:T(128)}, u32[]{:S(2)}) copy-start(s32[4]{0:T(128)} %rank_ref.1) | copy-start | bytes 52
  0.7 1.2 %copy-start.3 = (bf16[4,64,1024]{2,1,0:T(8,128)(2,1)S(1)}, bf16[4,64,1024]{2,1,0:T(8,128)(2,1)}, u32[]{:S(2)}) copy-start(bf16[4,64,1024]{2,1,0:T(8,128)(2,1)} %basis_ref.1) | copy-start | bytes 1572868
  1.9 1.9 %copy-start.11 = (bf16[4,4096]{1,0:T(4,128)(2,1)S(1)}, bf16[4,4096]{1,0:T(4,128)(2,1)}, u32[]{:S(2)}) copy-start(bf16[4,4096]{1,0:T(4,128)(2,1)} %param.10) | copy-start | bytes 98308
  3.9 41.4 %copy-start.5 = (s32[96]{0:T(128)S(1)}, s32[96]{0:T(128)}, u32[]{:S(2)}) copy-start(s32[96]{0:T(128)} %row_ref.1) | copy-start | bytes 1156
  21.5 1.0 %copy-start.1 = (bf16[64,72,128]{2,1,0:T(8,128)(2,1)}, bf16[64,72,128]{2,1,0:T(8,128)(2,1)S(1)}, u32[]{:S(2)}) copy-start(bf16[64,72,128]{2,1,0:T(8,128)(2,1)S(1)} %get-tuple-element.26) | copy-start | bytes 3538948
  22.5 41.8 %all-to-all-start = ((bf16[64,72,128]{2,1,0:T(8,128)(2,1)}), bf16[64,72,128]{2,1,0:T(8,128)(2,1)S(1)}, u32[]{:S(2)}, u32[]{:S(2)}) async-start(bf16[64,72,128]{2,1,0:T(8,128)(2,1)} %copy-done.1), calls=%async_computation | async-start | bytes 2359296 | tf_op jit(solution)/shard_map/all_to_all | solution.py:371
  38.7 39.2 %copy-start.8 = (s32[96,1]{0,1:T(1,128)S(1)}, s32[96,1]{0,1:T(1,128)}, u32[]{:S(2)}) copy-start(s32[96,1]{0,1:T(1,128)} %param.16) | copy-start | bytes 1156
  38.7 39.2 %copy-start.9 = (s32[96]{0:T(128)S(1)}, s32[96]{0:T(128)}, u32[]{:S(2)}) copy-start(s32[96]{0:T(128)} %column_ref.1) | copy-start | bytes 1156
  38.7 11.1 %collective-permute-start = (f32[32,128]{1,0:T(8,128)S(1)}, f32[32,128]{1,0:T(8,128)S(1)}, u32[]{:S(2)}, u32[]{:S(2)}) collective-permute-start(f32[32,128]{1,0:T(8,128)S(1)} %get-tuple-element.27.first_ref), channel_id=1, source_target_pairs={{0,4},{4,0},{8,12},{12,8},{16,20},{20,16},{24,28},{28,24},{32,36},... | collective-permute-start | bytes 49160 | tf_op jit(solution)/shard_map/ppermute | solution.py:372
  45.3 1.1 %copy-start.2 = (bf16[96,4096]{1,0:T(8,128)(2,1)S(1)}, bf16[96,4096]{1,0:T(8,128)(2,1)}, u32[]{:S(2)}) copy-start(bf16[96,4096]{1,0:T(8,128)(2,1)} %blocks_ref.1) | copy-start | bytes 2359300
  48.9 0.9 %copy-start.6 = (bf16[48,64,128]{2,1,0:T(8,128)(2,1)}, bf16[48,64,128]{2,1,0:T(8,128)(2,1)S(1)}, u32[]{:S(2)}) copy-start(bf16[48,64,128]{2,1,0:T(8,128)(2,1)S(1)} %get-tuple-element.25.rows_ref) | copy-start | bytes 2359300
  64.3 13.5 %collective-permute-start.1 = (bf16[64,72,128]{2,1,0:T(8,128)(2,1)S(1)}, bf16[64,72,128]{2,1,0:T(8,128)(2,1)}, u32[]{:S(2)}, u32[]{:S(2)}) collective-permute-start(bf16[64,72,128]{2,1,0:T(8,128)(2,1)S(1)} %all-to-all-done.own_ref.received_ref), channel_id=1, source_target_pairs={{0,4},{4,0},{8,12},{12,8},{16,20},{20,16},{24,28},{28,24},{32,36},... | collective-permute-start | bytes 3538952 | tf_op jit(solution)/shard_map/ppermute | solution.py:402
  74.6 10.3 %all-to-all-start.1 = ((f32[8,8,128]{2,1,0:T(8,128)}), f32[8,8,128]{2,1,0:T(8,128)S(1)}, u32[]{:S(2)}, u32[]{:S(2)}) async-start(f32[8,8,128]{2,1,0:T(8,128)} %sum.1), calls=%async_computation.1 | async-start | bytes 65536 | tf_op jit(solution)/shard_map/all_to_all | solution.py:403
  77.9 1.1 %copy-start.7 = (bf16[48,64,128]{2,1,0:T(8,128)(2,1)S(1)}, bf16[48,64,128]{2,1,0:T(8,128)(2,1)}, u32[]{:S(2)}) copy-start(bf16[48,64,128]{2,1,0:T(8,128)(2,1)} %copy-done.6) | copy-start | bytes 2359300

commit v8 on v6

--- a/solution.py
+++ b/solution.py
@@ -9,6 +9,7 @@
 SMEM = pl.BlockSpec(memory_space=pltpu.SMEM)
 SMALL = pltpu.CompilerParams(vmem_limit_bytes=8 * 1024 * 1024)
 ROWS = 16
+BLOCKS = 32
 F32 = jnp.float32
 BF16 = jnp.bfloat16
 
@@ -395,6 +396,7 @@
         in_specs=[VMEM],
         out_specs=VMEM,
         compiler_params=SMALL,
+        cost_estimate=pl.CostEstimate(flops=10**10, bytes_accessed=own.size, transcendentals=0),
         name="sum",
     )(own)
     other = lax.ppermute(own, "branch", partners)
@@ -406,11 +408,11 @@
         out_shape=shape((blk, width * width), F32),
         grid_spec=pltpu.PrefetchScalarGridSpec(
             num_scalar_prefetch=3,
-            grid=(blk // ROWS,),
-            in_specs=[square, whole, whole],
-            out_specs=pl.BlockSpec((ROWS, width * width), lambda i, *_: (i, 0)),
+            grid=(blk // BLOCKS,),
+            in_specs=[pl.BlockSpec((BLOCKS // 2, width, wide), lambda i, *_: (i, 0, 0)), whole, whole],
+            out_specs=pl.BlockSpec((BLOCKS, width * width), lambda i, *_: (i, 0)),
             scratch_shapes=[
-                pltpu.VMEM((ROWS * half, wide), F32),
+                pltpu.VMEM((BLOCKS * half, wide), F32),
                 pltpu.VMEM((6, 2, width, wide), BF16),
             ],
         ),

time: 79.2 us -> 79.3 us (level)
  no operation moved by 1% of the time
where the time goes in v8:
time: 79.3 us; the launch traced here: 78.8 us
  starting transfers between devices  35.4 us (45%)
  waiting for transfers between devices  21.8 us (27%)
  Pallas kernels  13.8 us (17%)
  local copies, waits for them, and re-layouts  6.81 us (9%)
  between operations  0.84 us (1%)
    all_to_all x1, waiting for transfers between devices, on_device(): own = lax.all_to_all(sent, 'branch', 0, 0, axis_index_groups=same_core)  19.9 us
    all_to_all x1, starting transfers between devices, on_device(): own = lax.all_to_all(sent, 'branch', 0, 0, axis_index_groups=same_core)  16.3 us
    ppermute x1, starting transfers between devices, on_device(): other = lax.ppermute(own, 'branch', partners)  6.69 us
    pallas_call x1, Pallas kernels, on_device(): pl.pallas_call(project_kernel, out_shape=shape((blk, width * width), F32)...  5.89 us
    unnamed x24, local copies, waits for them, and re-layouts  5.35 us
    all_to_all x1, starting transfers between devices, on_device(): gathered = lax.all_to_all(partial_sums, 'level', 0, 0)  4.84 us
    ppermute x1, starting transfers between devices, on_device(): first_other = lax.ppermute(first, 'branch', partners)  4.29 us
    all_to_all x1, starting transfers between devices, on_device(): lax.all_to_all(summed, ('branch', 'level'), 0, 0, axis_index_groups=same_...  3.28 us
  transfers between devices with their start and end apart: 5, of which 2 were waited for; matrix products, arithmetic and copies ran while one was open for 2% of the time, Pallas kernels for 13%

profile of v8, /device:TPU:1, one launch (start us, length us, event | category | flops | bytes accessed | tf_op | source)
XLA Modules:
  0.0 78.8 jit_solution(1003491973513193853)
XLA Ops:
  0.6 0.0 copy-start
  0.6 0.0 copy-start.5
  0.7 1.2 %copy-done.5 = bf16[4,64,1024]{2,1,0:T(8,128)(2,1)S(1)} copy-done((bf16[4,64,1024]{2,1,0:T(8,128)(2,1)S(1)}, bf16[4,64,1024]{2,1,0:T(8,128)(2,1)}, u32[]{:S(2)}) %copy-start.5) | copy-done | bytes 524312
  1.8 0.0 copy-start.10
  1.8 0.0 copy-start.11
  1.8 0.0 copy-start.7
  1.8 1.0 %gram.1 = f32[4,72,128]{2,1,0:T(8,128)} custom-call(bf16[4,64,1024]{2,1,0:T(8,128)(2,1)S(1)} %copy-done.5), custom_call_target="tpu_custom_call" | custom-call | tf_op jit(solution)/shard_map/gram/pallas_call | solution.py:326
  2.8 4.8 %all-to-all-start = ((f32[4,72,128]{2,1,0:T(8,128)}), f32[4,72,128]{2,1,0:T(8,128)S(1)}, u32[]{:S(2)}, u32[]{:S(2)}) async-start(f32[4,72,128]{2,1,0:T(8,128)} %gram.1), calls=%async_computation | async-start | bytes 294912 | tf_op jit(solution)/shard_map/all_to_all | solution.py:337
  7.7 0.0 copy-done
  7.7 0.6 gather_fusion.1
  8.3 0.1 gather.12
  8.4 0.0 copy-done.10
  8.4 0.6 gather_fusion
  9.1 0.1 broadcast_select_fusion.path_ref
  9.2 0.0 copy-start.6
  9.2 0.0 copy-done.11
  9.2 0.1 reshape.46.bottom_ref
  9.3 1.3 %path.1 = (bf16[7,64,64]{2,1,0:T(8,128)(2,1)S(1)}, bf16[7,64,64]{2,1,0:T(8,128)(2,1)S(1)}) custom-call(s32[7]{0:T(128)S(1)} %broadcast_select_fusion.1.rank_ref, bf16[7,64,64]{2,1,0:T(8,128)(2,1)S(1)} %broadcast_select_fusion.path_ref), custom_call_target="tpu_custom_call" | custom-call | tf_op jit(solution)/shard_map/path/pallas_call | solution.py:341
  10.7 1.9 %all-to-all-done.parts_ref = f32[4,72,128]{2,1,0:T(8,128)S(1)} async-done(((f32[4,72,128]{2,1,0:T(8,128)}), f32[4,72,128]{2,1,0:T(8,128)S(1)}, u32[]{:S(2)}, u32[]{:S(2)}) %all-to-all-start) | async-done | bytes 147488 | tf_op jit(solution)/shard_map/all_to_all | solution.py:337
  12.6 0.0 copy-done.7
  12.6 1.6 %near.1 = (bf16[4,64,64]{2,1,0:T(8,128)(2,1)S(1)}, bf16[64,72,128]{2,1,0:T(8,128)(2,1)S(1)}, f32[32,128]{1,0:T(8,128)S(1)}) custom-call(s32[4]{0:T(128)S(1)} %copy-done.7, s32[1]{0:T(128)} %bitcast.2.place_ref, s32[1]{0:T(128)} %bitcast.3.level_ref, f32[4,72,128]{2,1,0:T(8,128)S(1)} %all-to-all-done.parts_ref, bf16[4,64,64]{2,1,0:T(8,128)(2,1)S(1)} %reshape.46.bottom_ref, ...), custom_call_target="tpu_custom_call" | custom-call | tf_op jit(solution)/shard_map/near/pallas_call | solution.py:349
  14.1 0.0 copy-start.1
  14.2 1.0 %copy-done.1 = bf16[64,72,128]{2,1,0:T(8,128)(2,1)} copy-done((bf16[64,72,128]{2,1,0:T(8,128)(2,1)}, bf16[64,72,128]{2,1,0:T(8,128)(2,1)S(1)}, u32[]{:S(2)}) %copy-start.1) | copy-done | bytes 1179672
  15.2 16.3 %all-to-all-start.1 = ((bf16[64,72,128]{2,1,0:T(8,128)(2,1)}), bf16[64,72,128]{2,1,0:T(8,128)(2,1)S(1)}, u32[]{:S(2)}, u32[]{:S(2)}) async-start(bf16[64,72,128]{2,1,0:T(8,128)(2,1)} %copy-done.1), calls=%async_computation.1 | async-start | bytes 2359296 | tf_op jit(solution)/shard_map/all_to_all | solution.py:370
  31.5 4.3 %collective-permute-start = (f32[32,128]{1,0:T(8,128)S(1)}, f32[32,128]{1,0:T(8,128)S(1)}, u32[]{:S(2)}, u32[]{:S(2)}) collective-permute-start(f32[32,128]{1,0:T(8,128)S(1)} %get-tuple-element.27.first_ref), channel_id=1, source_target_pairs={{0,4},{4,0},{8,12},{12,8},{16,20},{20,16},{24,28},{28,24},{32,36},... | collective-permute-start | bytes 49160 | tf_op jit(solution)/shard_map/ppermute | solution.py:371
  35.8 0.0 copy-done.6
  35.8 0.0 copy-start.2
  35.8 1.1 %copy-done.2 = bf16[96,4096]{1,0:T(8,128)(2,1)S(1)} copy-done((bf16[96,4096]{1,0:T(8,128)(2,1)S(1)}, bf16[96,4096]{1,0:T(8,128)(2,1)}, u32[]{:S(2)}) %copy-start.2) | copy-done | bytes 786456
  36.9 2.4 %left.1 = (bf16[48,64,128]{2,1,0:T(8,128)(2,1)S(1)}, f32[8,128]{1,0:T(8,128)S(1)}) custom-call(s32[96]{0:T(128)S(1)} %copy-done.6, bf16[96,4096]{1,0:T(8,128)(2,1)S(1)} %copy-done.2, bf16[4,64,64]{2,1,0:T(8,128)(2,1)S(1)} %get-tuple-element.24.left_ref), custom_call_target="tpu_custom_call" | custom-call | flops 100663296 | bytes 1572864 | tf_op jit(solution)/shard_map/left/pallas_call | solution.py:373
  39.4 0.0 copy-start.3
  39.4 0.9 %copy-done.3 = bf16[48,64,128]{2,1,0:T(8,128)(2,1)} copy-done((bf16[48,64,128]{2,1,0:T(8,128)(2,1)}, bf16[48,64,128]{2,1,0:T(8,128)(2,1)S(1)}, u32[]{:S(2)}) %copy-start.3) | copy-done | bytes 786456
  40.2 0.0 collective-permute-done.other_ref
  40.2 19.9 %all-to-all-done.1.own_ref.received_ref = bf16[64,72,128]{2,1,0:T(8,128)(2,1)S(1)} async-done(((bf16[64,72,128]{2,1,0:T(8,128)(2,1)}), bf16[64,72,128]{2,1,0:T(8,128)(2,1)S(1)}, u32[]{:S(2)}, u32[]{:S(2)}) %all-to-all-start.1) | async-done | bytes 1179680 | tf_op jit(solution)/shard_map/all_to_all | solution.py:370
  60.1 0.0 copy-start.8
  60.1 0.0 copy-start.9
  60.1 6.7 %collective-permute-start.1 = (bf16[64,72,128]{2,1,0:T(8,128)(2,1)S(1)}, bf16[64,72,128]{2,1,0:T(8,128)(2,1)}, u32[]{:S(2)}, u32[]{:S(2)}) collective-permute-start(bf16[64,72,128]{2,1,0:T(8,128)(2,1)S(1)} %all-to-all-done.1.own_ref.received_ref), channel_id=1, source_target_pairs={{0,4},{4,0},{8,12},{12,8},{16,20},{20,16},{24,28},{28,24},{32,36},... | collective-permute-start | bytes 3538952 | tf_op jit(solution)/shard_map/ppermute | solution.py:402
  66.8 0.7 sum.1
  67.5 3.3 %all-to-all-start.2 = ((f32[8,8,128]{2,1,0:T(8,128)}), f32[8,8,128]{2,1,0:T(8,128)S(1)}, u32[]{:S(2)}, u32[]{:S(2)}) async-start(f32[8,8,128]{2,1,0:T(8,128)} %sum.1), calls=%async_computation.2 | async-start | bytes 65536 | tf_op jit(solution)/shard_map/all_to_all | solution.py:403
  70.8 0.0 collective-permute-done.1.other_ref
  70.8 0.0 copy-done.8
  70.8 0.0 copy-done.9
  70.8 0.0 copy-start.4
  70.8 1.1 %copy-done.4 = bf16[48,64,128]{2,1,0:T(8,128)(2,1)S(1)} copy-done((bf16[48,64,128]{2,1,0:T(8,128)(2,1)S(1)}, bf16[48,64,128]{2,1,0:T(8,128)(2,1)}, u32[]{:S(2)}) %copy-start.4) | copy-done | bytes 786456
  72.0 5.9 %project.1 = f32[96,4096]{1,0:T(8,128)} custom-call(s32[96]{0:T(128)S(1)} %bitcast.6, s32[96]{0:T(128)S(1)} %copy-done.9, s32[1]{0:T(128)} %bitcast.core_ref, bf16[48,64,128]{2,1,0:T(8,128)(2,1)S(1)} %copy-done.4, bf16[64,72,128]{2,1,0:T(8,128)(2,1)S(1)} %all-to-all-done.1.own_ref.received_ref, bf16[64,72,128]{2,1,0:T(8,128)(2,1)} %collective-permute-done.1.other_ref), custom_call_target="tpu_custom_call" | custom-call | flops 201326592 | bytes 2359296 | tf_op jit(solution)/shard_map/project/pallas_call | solution.py:406
  77.8 0.0 all-to-all-done.2.received_ref
  77.8 0.9 %top.1 = f32[1,4096]{1,0:T(1,128)} custom-call(s32[1]{0:T(128)} %bitcast.core_ref, f32[8,8,128]{2,1,0:T(8,128)S(1)} %all-to-all-done.2.received_ref, f32[32,128]{1,0:T(8,128)S(1)} %get-tuple-element.27.first_ref, f32[32,128]{1,0:T(8,128)S(1)} %collective-permute-done.other_ref, f32[8,128]{1,0:T(8,128)S(1)} %get-tuple-element.32.done_ref), custom_call_target="tpu_custom_call" | custom-call | tf_op jit(solution)/shard_map/top/pallas_call | solution.py:426
  (4 shorter events, 0.0 us)
Async XLA Ops:
  0.6 7.1 %copy-start = (bf16[254,4096]{1,0:T(8,128)(2,1)S(1)}, bf16[254,4096]{1,0:T(8,128)(2,1)}, u32[]{:S(2)}) copy-start(bf16[254,4096]{1,0:T(8,128)(2,1)} %param.12) | copy-start | bytes 6242308
  0.6 1.2 %copy-start.5 = (bf16[4,64,1024]{2,1,0:T(8,128)(2,1)S(1)}, bf16[4,64,1024]{2,1,0:T(8,128)(2,1)}, u32[]{:S(2)}) copy-start(bf16[4,64,1024]{2,1,0:T(8,128)(2,1)} %basis_ref.1) | copy-start | bytes 1572868
  1.8 6.6 %copy-start.10 = (s32[254]{0:T(256)S(1)}, s32[254]{0:T(256)}, u32[]{:S(2)}) copy-start(s32[254]{0:T(256)} %param.13) | copy-start | bytes 3052
  1.8 7.3 %copy-start.11 = (bf16[4,4096]{1,0:T(4,128)(2,1)S(1)}, bf16[4,4096]{1,0:T(4,128)(2,1)}, u32[]{:S(2)}) copy-start(bf16[4,4096]{1,0:T(4,128)(2,1)} %param.10) | copy-start | bytes 98308
  1.8 10.7 %copy-start.7 = (s32[4]{0:T(128)S(1)}, s32[4]{0:T(128)}, u32[]{:S(2)}) copy-start(s32[4]{0:T(128)} %rank_ref.1) | copy-start | bytes 52
  2.8 9.8 %all-to-all-start = ((f32[4,72,128]{2,1,0:T(8,128)}), f32[4,72,128]{2,1,0:T(8,128)S(1)}, u32[]{:S(2)}, u32[]{:S(2)}) async-start(f32[4,72,128]{2,1,0:T(8,128)} %gram.1), calls=%async_computation | async-start | bytes 294912 | tf_op jit(solution)/shard_map/all_to_all | solution.py:337
  9.2 26.6 %copy-start.6 = (s32[96]{0:T(128)S(1)}, s32[96]{0:T(128)}, u32[]{:S(2)}) copy-start(s32[96]{0:T(128)} %row_ref.1) | copy-start | bytes 1156
  14.1 1.0 %copy-start.1 = (bf16[64,72,128]{2,1,0:T(8,128)(2,1)}, bf16[64,72,128]{2,1,0:T(8,128)(2,1)S(1)}, u32[]{:S(2)}) copy-start(bf16[64,72,128]{2,1,0:T(8,128)(2,1)S(1)} %get-tuple-element.26) | copy-start | bytes 3538948
  15.2 44.9 %all-to-all-start.1 = ((bf16[64,72,128]{2,1,0:T(8,128)(2,1)}), bf16[64,72,128]{2,1,0:T(8,128)(2,1)S(1)}, u32[]{:S(2)}, u32[]{:S(2)}) async-start(bf16[64,72,128]{2,1,0:T(8,128)(2,1)} %copy-done.1), calls=%async_computation.1 | async-start | bytes 2359296 | tf_op jit(solution)/shard_map/all_to_all | solution.py:370
  31.5 8.8 %collective-permute-start = (f32[32,128]{1,0:T(8,128)S(1)}, f32[32,128]{1,0:T(8,128)S(1)}, u32[]{:S(2)}, u32[]{:S(2)}) collective-permute-start(f32[32,128]{1,0:T(8,128)S(1)} %get-tuple-element.27.first_ref), channel_id=1, source_target_pairs={{0,4},{4,0},{8,12},{12,8},{16,20},{20,16},{24,28},{28,24},{32,36},... | collective-permute-start | bytes 49160 | tf_op jit(solution)/shard_map/ppermute | solution.py:371
  35.8 1.1 %copy-start.2 = (bf16[96,4096]{1,0:T(8,128)(2,1)S(1)}, bf16[96,4096]{1,0:T(8,128)(2,1)}, u32[]{:S(2)}) copy-start(bf16[96,4096]{1,0:T(8,128)(2,1)} %blocks_ref.1) | copy-start | bytes 2359300
  39.4 0.9 %copy-start.3 = (bf16[48,64,128]{2,1,0:T(8,128)(2,1)}, bf16[48,64,128]{2,1,0:T(8,128)(2,1)S(1)}, u32[]{:S(2)}) copy-start(bf16[48,64,128]{2,1,0:T(8,128)(2,1)S(1)} %get-tuple-element.25.rows_ref) | copy-start | bytes 2359300
  60.1 10.7 %copy-start.8 = (s32[96,1]{0,1:T(1,128)S(1)}, s32[96,1]{0,1:T(1,128)}, u32[]{:S(2)}) copy-start(s32[96,1]{0,1:T(1,128)} %param.16) | copy-start | bytes 1156
  60.1 10.7 %copy-start.9 = (s32[96]{0:T(128)S(1)}, s32[96]{0:T(128)}, u32[]{:S(2)}) copy-start(s32[96]{0:T(128)} %column_ref.1) | copy-start | bytes 1156
  60.1 10.7 %collective-permute-start.1 = (bf16[64,72,128]{2,1,0:T(8,128)(2,1)S(1)}, bf16[64,72,128]{2,1,0:T(8,128)(2,1)}, u32[]{:S(2)}, u32[]{:S(2)}) collective-permute-start(bf16[64,72,128]{2,1,0:T(8,128)(2,1)S(1)} %all-to-all-done.1.own_ref.received_ref), channel_id=1, source_target_pairs={{0,4},{4,0},{8,12},{12,8},{16,20},{20,16},{24,28},{28,24},{32,36},... | collective-permute-start | bytes 3538952 | tf_op jit(solution)/shard_map/ppermute | solution.py:402
  67.5 10.3 %all-to-all-start.2 = ((f32[8,8,128]{2,1,0:T(8,128)}), f32[8,8,128]{2,1,0:T(8,128)S(1)}, u32[]{:S(2)}, u32[]{:S(2)}) async-start(f32[8,8,128]{2,1,0:T(8,128)} %sum.1), calls=%async_computation.2 | async-start | bytes 65536 | tf_op jit(solution)/shard_map/all_to_all | solution.py:403
  70.8 1.1 %copy-start.4 = (bf16[48,64,128]{2,1,0:T(8,128)(2,1)S(1)}, bf16[48,64,128]{2,1,0:T(8,128)(2,1)}, u32[]{:S(2)}) copy-start(bf16[48,64,128]{2,1,0:T(8,128)(2,1)} %copy-done.3) | copy-start | bytes 2359300

commit v9 on v6

--- a/solution.py
+++ b/solution.py
@@ -238,7 +238,7 @@
 
 
 def project_kernel(
-    owner_ref, column_ref, core_ref, rows_ref, own_ref, other_ref, out_ref, result, triangles
+    owner_ref, column_ref, core_ref, rows_ref, own_ref, other_ref, out_ref, kept_ref, result, triangles
 ):
     step = pl.program_id(0)
     pairs, width, wide = rows_ref.shape
@@ -401,14 +401,17 @@
     quarters = lax.all_to_all(summed, ("branch", "level"), 0, 0, axis_index_groups=same_chip)
 
     whole = pl.BlockSpec(own.shape, lambda i, *_: (0, 0, 0))
-    projected = pl.pallas_call(
+    projected, _ = pl.pallas_call(
         project_kernel,
-        out_shape=shape((blk, width * width), F32),
+        out_shape=[shape((blk, width * width), F32), shape(rows.shape, BF16)],
         grid_spec=pltpu.PrefetchScalarGridSpec(
             num_scalar_prefetch=3,
             grid=(blk // ROWS,),
             in_specs=[square, whole, whole],
-            out_specs=pl.BlockSpec((ROWS, width * width), lambda i, *_: (i, 0)),
+            out_specs=[
+                pl.BlockSpec((ROWS, width * width), lambda i, *_: (i, 0)),
+                pl.BlockSpec(memory_space=pl.ANY),
+            ],
             scratch_shapes=[
                 pltpu.VMEM((ROWS * half, wide), F32),
                 pltpu.VMEM((6, 2, width, wide), BF16),
@@ -418,6 +421,7 @@
         cost_estimate=pl.CostEstimate(
             flops=8 * blk * width**3, bytes_accessed=6 * blk * width * width, transcendentals=0
         ),
+        input_output_aliases={3: 1},
         name="project",
     )(column_owner[:, 0], column_cluster, core[None], rows, own, other)
     projected, quarters = lax.optimization_barrier((projected, quarters))

time: 79.2 us -> 79.2 us (level)
  no operation moved by 1% of the time
where the time goes in v9:
time: 79.2 us; the launch traced here: 78.6 us
  starting transfers between devices  35.3 us (45%)
  waiting for transfers between devices  21.8 us (28%)
  Pallas kernels  13.8 us (17%)
  local copies, waits for them, and re-layouts  6.83 us (9%)
  between operations  0.85 us (1%)
    all_to_all x1, waiting for transfers between devices, on_device(): own = lax.all_to_all(sent, 'branch', 0, 0, axis_index_groups=same_core)  19.8 us
    all_to_all x1, starting transfers between devices, on_device(): own = lax.all_to_all(sent, 'branch', 0, 0, axis_index_groups=same_core)  16.3 us
    ppermute x1, starting transfers between devices, on_device(): other = lax.ppermute(own, 'branch', partners)  6.56 us
    pallas_call x1, Pallas kernels, on_device(): pl.pallas_call(project_kernel, out_shape=[shape((blk, width * width), F32...  5.92 us
    unnamed x24, local copies, waits for them, and re-layouts  5.37 us
    all_to_all x1, starting transfers between devices, on_device(): gathered = lax.all_to_all(partial_sums, 'level', 0, 0)  4.84 us
    ppermute x1, starting transfers between devices, on_device(): first_other = lax.ppermute(first, 'branch', partners)  4.29 us
    all_to_all x1, starting transfers between devices, on_device(): lax.all_to_all(summed, ('branch', 'level'), 0, 0, axis_index_groups=same_...  3.27 us
  transfers between devices with their start and end apart: 5, of which 2 were waited for; matrix products, arithmetic and copies ran while one was open for 2% of the time, Pallas kernels for 13%

profile of v9, /device:TPU:1, one launch (start us, length us, event | category | flops | bytes accessed | tf_op | source)
XLA Modules:
  0.0 78.6 jit_solution(13358797922922970520)
XLA Ops:
  0.6 0.0 copy-start
  0.6 0.0 copy-start.5
  0.7 1.2 %copy-done.5 = bf16[4,64,1024]{2,1,0:T(8,128)(2,1)S(1)} copy-done((bf16[4,64,1024]{2,1,0:T(8,128)(2,1)S(1)}, bf16[4,64,1024]{2,1,0:T(8,128)(2,1)}, u32[]{:S(2)}) %copy-start.5) | copy-done | bytes 524312
  1.8 0.0 copy-start.10
  1.8 0.0 copy-start.11
  1.8 0.0 copy-start.9
  1.8 1.0 %gram.1 = f32[4,72,128]{2,1,0:T(8,128)} custom-call(bf16[4,64,1024]{2,1,0:T(8,128)(2,1)S(1)} %copy-done.5), custom_call_target="tpu_custom_call" | custom-call | tf_op jit(solution)/shard_map/gram/pallas_call | solution.py:325
  2.8 4.8 %all-to-all-start = ((f32[4,72,128]{2,1,0:T(8,128)}), f32[4,72,128]{2,1,0:T(8,128)S(1)}, u32[]{:S(2)}, u32[]{:S(2)}) async-start(f32[4,72,128]{2,1,0:T(8,128)} %gram.1), calls=%async_computation | async-start | bytes 294912 | tf_op jit(solution)/shard_map/all_to_all | solution.py:336
  7.7 0.0 copy-done
  7.7 0.6 gather_fusion.1
  8.3 0.1 gather.12
  8.4 0.0 copy-done.10
  8.4 0.6 gather_fusion
  9.1 0.1 broadcast_select_fusion.path_ref
  9.2 0.0 copy-start.6
  9.2 0.0 copy-done.11
  9.2 0.1 reshape.46.bottom_ref
  9.3 1.3 %path.1 = (bf16[7,64,64]{2,1,0:T(8,128)(2,1)S(1)}, bf16[7,64,64]{2,1,0:T(8,128)(2,1)S(1)}) custom-call(s32[7]{0:T(128)S(1)} %broadcast_select_fusion.1.rank_ref, bf16[7,64,64]{2,1,0:T(8,128)(2,1)S(1)} %broadcast_select_fusion.path_ref), custom_call_target="tpu_custom_call" | custom-call | tf_op jit(solution)/shard_map/path/pallas_call | solution.py:340
  10.7 1.9 %all-to-all-done.parts_ref = f32[4,72,128]{2,1,0:T(8,128)S(1)} async-done(((f32[4,72,128]{2,1,0:T(8,128)}), f32[4,72,128]{2,1,0:T(8,128)S(1)}, u32[]{:S(2)}, u32[]{:S(2)}) %all-to-all-start) | async-done | bytes 147488 | tf_op jit(solution)/shard_map/all_to_all | solution.py:336
  12.6 0.0 copy-done.9
  12.6 1.6 %near.1 = (bf16[4,64,64]{2,1,0:T(8,128)(2,1)S(1)}, bf16[64,72,128]{2,1,0:T(8,128)(2,1)S(1)}, f32[32,128]{1,0:T(8,128)S(1)}) custom-call(s32[4]{0:T(128)S(1)} %copy-done.9, s32[1]{0:T(128)} %bitcast.2.place_ref, s32[1]{0:T(128)} %bitcast.3.level_ref, f32[4,72,128]{2,1,0:T(8,128)S(1)} %all-to-all-done.parts_ref, bf16[4,64,64]{2,1,0:T(8,128)(2,1)S(1)} %reshape.46.bottom_ref, ...), custom_call_target="tpu_custom_call" | custom-call | tf_op jit(solution)/shard_map/near/pallas_call | solution.py:348
  14.1 0.0 copy-start.1
  14.2 1.0 %copy-done.1 = bf16[64,72,128]{2,1,0:T(8,128)(2,1)} copy-done((bf16[64,72,128]{2,1,0:T(8,128)(2,1)}, bf16[64,72,128]{2,1,0:T(8,128)(2,1)S(1)}, u32[]{:S(2)}) %copy-start.1) | copy-done | bytes 1179672
  15.2 16.3 %all-to-all-start.1 = ((bf16[64,72,128]{2,1,0:T(8,128)(2,1)}), bf16[64,72,128]{2,1,0:T(8,128)(2,1)S(1)}, u32[]{:S(2)}, u32[]{:S(2)}) async-start(bf16[64,72,128]{2,1,0:T(8,128)(2,1)} %copy-done.1), calls=%async_computation.1 | async-start | bytes 2359296 | tf_op jit(solution)/shard_map/all_to_all | solution.py:369
  31.5 0.0 copy-start.7
  31.5 0.0 copy-start.8
  31.5 4.3 %collective-permute-start = (f32[32,128]{1,0:T(8,128)S(1)}, f32[32,128]{1,0:T(8,128)S(1)}, u32[]{:S(2)}, u32[]{:S(2)}) collective-permute-start(f32[32,128]{1,0:T(8,128)S(1)} %get-tuple-element.28.first_ref), channel_id=1, source_target_pairs={{0,4},{4,0},{8,12},{12,8},{16,20},{20,16},{24,28},{28,24},{32,36},... | collective-permute-start | bytes 49160 | tf_op jit(solution)/shard_map/ppermute | solution.py:370
  35.8 0.0 copy-done.6
  35.8 0.0 copy-start.2
  35.8 1.1 %copy-done.2 = bf16[96,4096]{1,0:T(8,128)(2,1)S(1)} copy-done((bf16[96,4096]{1,0:T(8,128)(2,1)S(1)}, bf16[96,4096]{1,0:T(8,128)(2,1)}, u32[]{:S(2)}) %copy-start.2) | copy-done | bytes 786456
  37.0 2.4 %left.1 = (bf16[48,64,128]{2,1,0:T(8,128)(2,1)S(1)}, f32[8,128]{1,0:T(8,128)S(1)}) custom-call(s32[96]{0:T(128)S(1)} %copy-done.6, bf16[96,4096]{1,0:T(8,128)(2,1)S(1)} %copy-done.2, bf16[4,64,64]{2,1,0:T(8,128)(2,1)S(1)} %get-tuple-element.25.left_ref), custom_call_target="tpu_custom_call" | custom-call | flops 100663296 | bytes 1572864 | tf_op jit(solution)/shard_map/left/pallas_call | solution.py:372
  39.4 0.0 copy-start.3
  39.4 0.9 %copy-done.3 = bf16[48,64,128]{2,1,0:T(8,128)(2,1)} copy-done((bf16[48,64,128]{2,1,0:T(8,128)(2,1)}, bf16[48,64,128]{2,1,0:T(8,128)(2,1)S(1)}, u32[]{:S(2)}) %copy-start.3) | copy-done | bytes 786456
  40.3 0.0 collective-permute-done.other_ref
  40.3 19.8 %all-to-all-done.1.own_ref.received_ref = bf16[64,72,128]{2,1,0:T(8,128)(2,1)S(1)} async-done(((bf16[64,72,128]{2,1,0:T(8,128)(2,1)}), bf16[64,72,128]{2,1,0:T(8,128)(2,1)S(1)}, u32[]{:S(2)}, u32[]{:S(2)}) %all-to-all-start.1) | async-done | bytes 1179680 | tf_op jit(solution)/shard_map/all_to_all | solution.py:369
  60.1 6.6 %collective-permute-start.1 = (bf16[64,72,128]{2,1,0:T(8,128)(2,1)S(1)}, bf16[64,72,128]{2,1,0:T(8,128)(2,1)}, u32[]{:S(2)}, u32[]{:S(2)}) collective-permute-start(bf16[64,72,128]{2,1,0:T(8,128)(2,1)S(1)} %all-to-all-done.1.own_ref.received_ref), channel_id=1, source_target_pairs={{0,4},{4,0},{8,12},{12,8},{16,20},{20,16},{24,28},{28,24},{32,36},... | collective-permute-start | bytes 3538952 | tf_op jit(solution)/shard_map/ppermute | solution.py:400
  66.7 0.7 sum.1
  67.3 3.3 %all-to-all-start.2 = ((f32[8,8,128]{2,1,0:T(8,128)}), f32[8,8,128]{2,1,0:T(8,128)S(1)}, u32[]{:S(2)}, u32[]{:S(2)}) async-start(f32[8,8,128]{2,1,0:T(8,128)} %sum.1), calls=%async_computation.2 | async-start | bytes 65536 | tf_op jit(solution)/shard_map/all_to_all | solution.py:401
  70.6 0.0 collective-permute-done.1.other_ref
  70.6 0.0 copy-done.7
  70.7 0.0 copy-done.8
  70.7 0.0 copy-start.4
  70.7 1.1 %copy-done.4 = bf16[48,64,128]{2,1,0:T(8,128)(2,1)S(1)} copy-done((bf16[48,64,128]{2,1,0:T(8,128)(2,1)S(1)}, bf16[48,64,128]{2,1,0:T(8,128)(2,1)}, u32[]{:S(2)}) %copy-start.4) | copy-done | bytes 786456
  71.8 5.9 %project.1 = (f32[96,4096]{1,0:T(8,128)}, bf16[48,64,128]{2,1,0:T(8,128)(2,1)S(1)}) custom-call(s32[96]{0:T(128)S(1)} %bitcast.6, s32[96]{0:T(128)S(1)} %copy-done.8, s32[1]{0:T(128)} %bitcast.core_ref, bf16[48,64,128]{2,1,0:T(8,128)(2,1)S(1)} %copy-done.4, ...), custom_call_target="tpu_custom_call", output_to_operand_aliasing={{1}: (3, {})} | custom-call | flops 201326592 | bytes 2359296 | tf_op jit(solution)/shard_map/project/pallas_call | solution.py:404
  77.7 0.0 all-to-all-done.2.received_ref
  77.7 0.9 %top.1 = f32[1,4096]{1,0:T(1,128)} custom-call(s32[1]{0:T(128)} %bitcast.core_ref, f32[8,8,128]{2,1,0:T(8,128)S(1)} %all-to-all-done.2.received_ref, f32[32,128]{1,0:T(8,128)S(1)} %get-tuple-element.28.first_ref, f32[32,128]{1,0:T(8,128)S(1)} %collective-permute-done.other_ref, f32[8,128]{1,0:T(8,128)S(1)} %get-tuple-element.34.done_ref), custom_call_target="tpu_custom_call" | custom-call | tf_op jit(solution)/shard_map/top/pallas_call | solution.py:428
  (4 shorter events, 0.0 us)
Async XLA Ops:
  0.6 7.1 %copy-start = (bf16[254,4096]{1,0:T(8,128)(2,1)S(1)}, bf16[254,4096]{1,0:T(8,128)(2,1)}, u32[]{:S(2)}) copy-start(bf16[254,4096]{1,0:T(8,128)(2,1)} %param.12) | copy-start | bytes 6242308
  0.6 1.2 %copy-start.5 = (bf16[4,64,1024]{2,1,0:T(8,128)(2,1)S(1)}, bf16[4,64,1024]{2,1,0:T(8,128)(2,1)}, u32[]{:S(2)}) copy-start(bf16[4,64,1024]{2,1,0:T(8,128)(2,1)} %basis_ref.1) | copy-start | bytes 1572868
  1.8 6.6 %copy-start.10 = (s32[254]{0:T(256)S(1)}, s32[254]{0:T(256)}, u32[]{:S(2)}) copy-start(s32[254]{0:T(256)} %param.13) | copy-start | bytes 3052
  1.8 7.3 %copy-start.11 = (bf16[4,4096]{1,0:T(4,128)(2,1)S(1)}, bf16[4,4096]{1,0:T(4,128)(2,1)}, u32[]{:S(2)}) copy-start(bf16[4,4096]{1,0:T(4,128)(2,1)} %param.10) | copy-start | bytes 98308
  1.8 10.7 %copy-start.9 = (s32[4]{0:T(128)S(1)}, s32[4]{0:T(128)}, u32[]{:S(2)}) copy-start(s32[4]{0:T(128)} %rank_ref.1) | copy-start | bytes 52
  2.8 9.8 %all-to-all-start = ((f32[4,72,128]{2,1,0:T(8,128)}), f32[4,72,128]{2,1,0:T(8,128)S(1)}, u32[]{:S(2)}, u32[]{:S(2)}) async-start(f32[4,72,128]{2,1,0:T(8,128)} %gram.1), calls=%async_computation | async-start | bytes 294912 | tf_op jit(solution)/shard_map/all_to_all | solution.py:336
  9.2 26.7 %copy-start.6 = (s32[96]{0:T(128)S(1)}, s32[96]{0:T(128)}, u32[]{:S(2)}) copy-start(s32[96]{0:T(128)} %row_ref.1) | copy-start | bytes 1156
  14.1 1.0 %copy-start.1 = (bf16[64,72,128]{2,1,0:T(8,128)(2,1)}, bf16[64,72,128]{2,1,0:T(8,128)(2,1)S(1)}, u32[]{:S(2)}) copy-start(bf16[64,72,128]{2,1,0:T(8,128)(2,1)S(1)} %get-tuple-element.27) | copy-start | bytes 3538948
  15.2 44.9 %all-to-all-start.1 = ((bf16[64,72,128]{2,1,0:T(8,128)(2,1)}), bf16[64,72,128]{2,1,0:T(8,128)(2,1)S(1)}, u32[]{:S(2)}, u32[]{:S(2)}) async-start(bf16[64,72,128]{2,1,0:T(8,128)(2,1)} %copy-done.1), calls=%async_computation.1 | async-start | bytes 2359296 | tf_op jit(solution)/shard_map/all_to_all | solution.py:369
  31.5 39.2 %copy-start.7 = (s32[96,1]{0,1:T(1,128)S(1)}, s32[96,1]{0,1:T(1,128)}, u32[]{:S(2)}) copy-start(s32[96,1]{0,1:T(1,128)} %param.16) | copy-start | bytes 1156
  31.5 39.2 %copy-start.8 = (s32[96]{0:T(128)S(1)}, s32[96]{0:T(128)}, u32[]{:S(2)}) copy-start(s32[96]{0:T(128)} %column_ref.1) | copy-start | bytes 1156
  31.5 8.8 %collective-permute-start = (f32[32,128]{1,0:T(8,128)S(1)}, f32[32,128]{1,0:T(8,128)S(1)}, u32[]{:S(2)}, u32[]{:S(2)}) collective-permute-start(f32[32,128]{1,0:T(8,128)S(1)} %get-tuple-element.28.first_ref), channel_id=1, source_target_pairs={{0,4},{4,0},{8,12},{12,8},{16,20},{20,16},{24,28},{28,24},{32,36},... | collective-permute-start | bytes 49160 | tf_op jit(solution)/shard_map/ppermute | solution.py:370
  35.8 1.1 %copy-start.2 = (bf16[96,4096]{1,0:T(8,128)(2,1)S(1)}, bf16[96,4096]{1,0:T(8,128)(2,1)}, u32[]{:S(2)}) copy-start(bf16[96,4096]{1,0:T(8,128)(2,1)} %blocks_ref.1) | copy-start | bytes 2359300
  39.4 0.9 %copy-start.3 = (bf16[48,64,128]{2,1,0:T(8,128)(2,1)}, bf16[48,64,128]{2,1,0:T(8,128)(2,1)S(1)}, u32[]{:S(2)}) copy-start(bf16[48,64,128]{2,1,0:T(8,128)(2,1)S(1)} %get-tuple-element.26.rows_ref) | copy-start | bytes 2359300
  60.1 10.5 %collective-permute-start.1 = (bf16[64,72,128]{2,1,0:T(8,128)(2,1)S(1)}, bf16[64,72,128]{2,1,0:T(8,128)(2,1)}, u32[]{:S(2)}, u32[]{:S(2)}) collective-permute-start(bf16[64,72,128]{2,1,0:T(8,128)(2,1)S(1)} %all-to-all-done.1.own_ref.received_ref), channel_id=1, source_target_pairs={{0,4},{4,0},{8,12},{12,8},{16,20},{20,16},{24,28},{28,24},{32,36},... | collective-permute-start | bytes 3538952 | tf_op jit(solution)/shard_map/ppermute | solution.py:400
  67.3 10.4 %all-to-all-start.2 = ((f32[8,8,128]{2,1,0:T(8,128)}), f32[8,8,128]{2,1,0:T(8,128)S(1)}, u32[]{:S(2)}, u32[]{:S(2)}) async-start(f32[8,8,128]{2,1,0:T(8,128)} %sum.1), calls=%async_computation.2 | async-start | bytes 65536 | tf_op jit(solution)/shard_map/all_to_all | solution.py:401
  70.7 1.1 %copy-start.4 = (bf16[48,64,128]{2,1,0:T(8,128)(2,1)S(1)}, bf16[48,64,128]{2,1,0:T(8,128)(2,1)}, u32[]{:S(2)}) copy-start(bf16[48,64,128]{2,1,0:T(8,128)(2,1)} %copy-done.3) | copy-start | bytes 2359300

commit v10 on v6

--- a/solution.py
+++ b/solution.py
@@ -191,7 +191,7 @@
         left_ref[node] = nt(nn(order, masked[node].astype(BF16)).astype(BF16), order).astype(BF16)
 
 
-def sum_kernel(received_ref, out_ref):
+def sum_kernel(received_ref, rows_ref, out_ref):
     sources, rows, _ = received_ref.shape
     total = received_ref[0, rows - 8 :].astype(F32)
     for source in range(1, sources):
@@ -392,11 +392,11 @@
     summed = pl.pallas_call(
         sum_kernel,
         out_shape=shape((2 * parts, 8, wide), F32),
-        in_specs=[VMEM],
+        in_specs=[VMEM, pl.BlockSpec(memory_space=pl.ANY)],
         out_specs=VMEM,
         compiler_params=SMALL,
         name="sum",
-    )(own)
+    )(own, rows)
     other = lax.ppermute(own, "branch", partners)
     quarters = lax.all_to_all(summed, ("branch", "level"), 0, 0, axis_index_groups=same_chip)
 

time: 79.2 us -> 80.6 us (1.018)
  local copies, waits for them, and re-layouts: 6.82 us -> 8.62 us
    unnamed x24, local copies, waits for them, and re-layouts: 5.36 us -> 6.48 us
  transfers between devices with their start and end apart: 5 -> 5, of which waited for: 2 -> 2; matrix products, arithmetic and copies ran while one was open for 2% -> 3% of each run, Pallas kernels for 13% -> 13%
where the time goes in v10:
time: 80.6 us; the launch traced here: 80 us
  starting transfers between devices  35.5 us (44%)
  waiting for transfers between devices  21.1 us (26%)
  Pallas kernels  13.8 us (17%)
  local copies, waits for them, and re-layouts  8.62 us (11%)
  between operations  0.83 us (1%)
    all_to_all x1, waiting for transfers between devices, on_device(): own = lax.all_to_all(sent, 'branch', 0, 0, axis_index_groups=same_core)  19.8 us
    all_to_all x1, starting transfers between devices, on_device(): own = lax.all_to_all(sent, 'branch', 0, 0, axis_index_groups=same_core)  16.3 us
    ppermute x1, starting transfers between devices, on_device(): other = lax.ppermute(own, 'branch', partners)  6.56 us
    unnamed x24, local copies, waits for them, and re-layouts  6.48 us
    pallas_call x1, Pallas kernels, on_device(): pl.pallas_call(project_kernel, out_shape=shape((blk, width * width), F32)...  5.9 us
    all_to_all x1, starting transfers between devices, on_device(): gathered = lax.all_to_all(partial_sums, 'level', 0, 0)  4.84 us
    ppermute x1, starting transfers between devices, on_device(): first_other = lax.ppermute(first, 'branch', partners)  4.29 us
    all_to_all x1, starting transfers between devices, on_device(): lax.all_to_all(summed, ('branch', 'level'), 0, 0, axis_index_groups=same_...  3.5 us
  transfers between devices with their start and end apart: 5, of which 2 were waited for; matrix products, arithmetic and copies ran while one was open for 3% of the time, Pallas kernels for 13%

profile of v10, /device:TPU:1, one launch (start us, length us, event | category | flops | bytes accessed | tf_op | source)
XLA Modules:
  0.0 80.0 jit_solution(17317300539507873785)
XLA Ops:
  0.6 0.0 copy-start
  0.6 0.0 copy-start.6
  0.7 1.2 %copy-done.6 = bf16[4,64,1024]{2,1,0:T(8,128)(2,1)S(1)} copy-done((bf16[4,64,1024]{2,1,0:T(8,128)(2,1)S(1)}, bf16[4,64,1024]{2,1,0:T(8,128)(2,1)}, u32[]{:S(2)}) %copy-start.6) | copy-done | bytes 524312
  1.8 0.0 copy-start.11
  1.8 0.0 copy-start.8
  1.8 1.0 %gram.1 = f32[4,72,128]{2,1,0:T(8,128)} custom-call(bf16[4,64,1024]{2,1,0:T(8,128)(2,1)S(1)} %copy-done.6), custom_call_target="tpu_custom_call" | custom-call | tf_op jit(solution)/shard_map/gram/pallas_call | solution.py:325
  2.8 4.8 %all-to-all-start = ((f32[4,72,128]{2,1,0:T(8,128)}), f32[4,72,128]{2,1,0:T(8,128)S(1)}, u32[]{:S(2)}, u32[]{:S(2)}) async-start(f32[4,72,128]{2,1,0:T(8,128)} %gram.1), calls=%async_computation | async-start | bytes 294912 | tf_op jit(solution)/shard_map/all_to_all | solution.py:336
  7.7 1.3 %gather_fusion = s32[7]{0:T(128)S(1)} fusion(s32[254]{0:T(256)} %param.13, s32[1024]{0:T(1024)S(1)} %pad_clamp_fusion), kind=kCustom, calls=%fused_computation | custom fusion | bytes 84 | tf_op jit(solution)/shard_map/jit(_take)/gather | solution.py:347
  9.0 0.0 copy-done
  9.0 0.6 gather_fusion.1
  9.6 0.1 gather.12
  9.7 0.1 broadcast_select_fusion.path_ref
  9.8 0.0 copy-start.7
  9.8 0.0 copy-done.11
  9.9 0.1 reshape.46.bottom_ref
  10.0 1.3 %path.1 = (bf16[7,64,64]{2,1,0:T(8,128)(2,1)S(1)}, bf16[7,64,64]{2,1,0:T(8,128)(2,1)S(1)}) custom-call(s32[7]{0:T(128)S(1)} %broadcast_select_fusion.1.rank_ref, bf16[7,64,64]{2,1,0:T(8,128)(2,1)S(1)} %broadcast_select_fusion.path_ref), custom_call_target="tpu_custom_call" | custom-call | tf_op jit(solution)/shard_map/path/pallas_call | solution.py:340
  11.3 1.2 %all-to-all-done.parts_ref = f32[4,72,128]{2,1,0:T(8,128)S(1)} async-done(((f32[4,72,128]{2,1,0:T(8,128)}), f32[4,72,128]{2,1,0:T(8,128)S(1)}, u32[]{:S(2)}, u32[]{:S(2)}) %all-to-all-start) | async-done | bytes 147488 | tf_op jit(solution)/shard_map/all_to_all | solution.py:336
  12.6 0.0 copy-done.8
  12.6 1.6 %near.1 = (bf16[4,64,64]{2,1,0:T(8,128)(2,1)S(1)}, bf16[64,72,128]{2,1,0:T(8,128)(2,1)S(1)}, f32[32,128]{1,0:T(8,128)S(1)}) custom-call(s32[4]{0:T(128)S(1)} %copy-done.8, s32[1]{0:T(128)} %bitcast.2.place_ref, s32[1]{0:T(128)} %bitcast.3.level_ref, f32[4,72,128]{2,1,0:T(8,128)S(1)} %all-to-all-done.parts_ref, bf16[4,64,64]{2,1,0:T(8,128)(2,1)S(1)} %reshape.46.bottom_ref, ...), custom_call_target="tpu_custom_call" | custom-call | tf_op jit(solution)/shard_map/near/pallas_call | solution.py:348
  14.1 0.0 copy-start.4
  14.2 1.0 %copy-done.4 = bf16[64,72,128]{2,1,0:T(8,128)(2,1)} copy-done((bf16[64,72,128]{2,1,0:T(8,128)(2,1)}, bf16[64,72,128]{2,1,0:T(8,128)(2,1)S(1)}, u32[]{:S(2)}) %copy-start.4) | copy-done | bytes 1179672
  15.2 16.3 %all-to-all-start.1 = ((bf16[64,72,128]{2,1,0:T(8,128)(2,1)}), bf16[64,72,128]{2,1,0:T(8,128)(2,1)S(1)}, u32[]{:S(2)}, u32[]{:S(2)}) async-start(bf16[64,72,128]{2,1,0:T(8,128)(2,1)} %copy-done.4), calls=%async_computation.1 | async-start | bytes 2359296 | tf_op jit(solution)/shard_map/all_to_all | solution.py:369
  31.5 0.0 copy-start.9
  31.5 0.0 copy-start.10
  31.5 4.3 %collective-permute-start = (f32[32,128]{1,0:T(8,128)S(1)}, f32[32,128]{1,0:T(8,128)S(1)}, u32[]{:S(2)}, u32[]{:S(2)}) collective-permute-start(f32[32,128]{1,0:T(8,128)S(1)} %get-tuple-element.27.first_ref), channel_id=1, source_target_pairs={{0,4},{4,0},{8,12},{12,8},{16,20},{20,16},{24,28},{28,24},{32,36},... | collective-permute-start | bytes 49160 | tf_op jit(solution)/shard_map/ppermute | solution.py:370
  35.8 0.0 copy-done.7
  35.8 0.0 copy-start.5
  35.8 1.1 %copy-done.5 = bf16[96,4096]{1,0:T(8,128)(2,1)S(1)} copy-done((bf16[96,4096]{1,0:T(8,128)(2,1)S(1)}, bf16[96,4096]{1,0:T(8,128)(2,1)}, u32[]{:S(2)}) %copy-start.5) | copy-done | bytes 786456
  37.0 2.4 %left.1 = (bf16[48,64,128]{2,1,0:T(8,128)(2,1)S(1)}, f32[8,128]{1,0:T(8,128)S(1)}) custom-call(s32[96]{0:T(128)S(1)} %copy-done.7, bf16[96,4096]{1,0:T(8,128)(2,1)S(1)} %copy-done.5, bf16[4,64,64]{2,1,0:T(8,128)(2,1)S(1)} %get-tuple-element.24.left_ref), custom_call_target="tpu_custom_call" | custom-call | flops 100663296 | bytes 1572864 | tf_op jit(solution)/shard_map/left/pallas_call | solution.py:372
  39.4 0.0 copy-start.1
  39.4 0.9 %copy-done.1 = bf16[48,64,128]{2,1,0:T(8,128)(2,1)} copy-done((bf16[48,64,128]{2,1,0:T(8,128)(2,1)}, bf16[48,64,128]{2,1,0:T(8,128)(2,1)S(1)}, u32[]{:S(2)}) %copy-start.1) | copy-done | bytes 786456
  40.3 0.0 collective-permute-done.other_ref
  40.3 19.8 %all-to-all-done.1.own_ref.received_ref = bf16[64,72,128]{2,1,0:T(8,128)(2,1)S(1)} async-done(((bf16[64,72,128]{2,1,0:T(8,128)(2,1)}), bf16[64,72,128]{2,1,0:T(8,128)(2,1)S(1)}, u32[]{:S(2)}, u32[]{:S(2)}) %all-to-all-start.1) | async-done | bytes 1179680 | tf_op jit(solution)/shard_map/all_to_all | solution.py:369
  60.1 6.6 %collective-permute-start.1 = (bf16[64,72,128]{2,1,0:T(8,128)(2,1)S(1)}, bf16[64,72,128]{2,1,0:T(8,128)(2,1)}, u32[]{:S(2)}, u32[]{:S(2)}) collective-permute-start(bf16[64,72,128]{2,1,0:T(8,128)(2,1)S(1)} %all-to-all-done.1.own_ref.received_ref), channel_id=1, source_target_pairs={{0,4},{4,0},{8,12},{12,8},{16,20},{20,16},{24,28},{28,24},{32,36},... | collective-permute-start | bytes 3538952 | tf_op jit(solution)/shard_map/ppermute | solution.py:400
  66.7 0.0 copy-start.2
  66.7 1.1 %copy-done.2 = bf16[48,64,128]{2,1,0:T(8,128)(2,1)S(1)} copy-done((bf16[48,64,128]{2,1,0:T(8,128)(2,1)S(1)}, bf16[48,64,128]{2,1,0:T(8,128)(2,1)}, u32[]{:S(2)}) %copy-start.2) | copy-done | bytes 786456
  67.8 0.7 sum.1
  68.5 3.5 %all-to-all-start.2 = ((f32[8,8,128]{2,1,0:T(8,128)}), f32[8,8,128]{2,1,0:T(8,128)S(1)}, u32[]{:S(2)}, u32[]{:S(2)}) async-start(f32[8,8,128]{2,1,0:T(8,128)} %sum.1), calls=%async_computation.2 | async-start | bytes 65536 | tf_op jit(solution)/shard_map/all_to_all | solution.py:401
  72.0 0.0 collective-permute-done.1.other_ref
  72.0 0.0 copy-done.9
  72.0 0.0 copy-done.10
  72.0 0.0 copy-start.3
  72.0 1.1 %copy-done.3 = bf16[48,64,128]{2,1,0:T(8,128)(2,1)S(1)} copy-done((bf16[48,64,128]{2,1,0:T(8,128)(2,1)S(1)}, bf16[48,64,128]{2,1,0:T(8,128)(2,1)}, u32[]{:S(2)}) %copy-start.3) | copy-done | bytes 786456
  73.1 5.9 %project.1 = f32[96,4096]{1,0:T(8,128)} custom-call(s32[96]{0:T(128)S(1)} %bitcast.6, s32[96]{0:T(128)S(1)} %copy-done.10, s32[1]{0:T(128)} %bitcast.core_ref, bf16[48,64,128]{2,1,0:T(8,128)(2,1)S(1)} %copy-done.3, bf16[64,72,128]{2,1,0:T(8,128)(2,1)S(1)} %all-to-all-done.1.own_ref.received_ref, bf16[64,72,128]{2,1,0:T(8,128)(2,1)} %collective-permute-done.1.other_ref), custom_call_target="tpu_custom_call" | custom-call | flops 201326592 | bytes 2359296 | tf_op jit(solution)/shard_map/project/pallas_call | solution.py:404
  79.0 0.0 all-to-all-done.2.received_ref
  79.0 0.9 %top.1 = f32[1,4096]{1,0:T(1,128)} custom-call(s32[1]{0:T(128)} %bitcast.core_ref, f32[8,8,128]{2,1,0:T(8,128)S(1)} %all-to-all-done.2.received_ref, f32[32,128]{1,0:T(8,128)S(1)} %get-tuple-element.27.first_ref, f32[32,128]{1,0:T(8,128)S(1)} %collective-permute-done.other_ref, f32[8,128]{1,0:T(8,128)S(1)} %get-tuple-element.32.done_ref), custom_call_target="tpu_custom_call" | custom-call | tf_op jit(solution)/shard_map/top/pallas_call | solution.py:424
  (4 shorter events, 0.0 us)
Async XLA Ops:
  0.6 8.4 %copy-start = (bf16[254,4096]{1,0:T(8,128)(2,1)S(1)}, bf16[254,4096]{1,0:T(8,128)(2,1)}, u32[]{:S(2)}) copy-start(bf16[254,4096]{1,0:T(8,128)(2,1)} %param.12) | copy-start | bytes 6242308
  0.6 1.2 %copy-start.6 = (bf16[4,64,1024]{2,1,0:T(8,128)(2,1)S(1)}, bf16[4,64,1024]{2,1,0:T(8,128)(2,1)}, u32[]{:S(2)}) copy-start(bf16[4,64,1024]{2,1,0:T(8,128)(2,1)} %basis_ref.1) | copy-start | bytes 1572868
  1.8 8.0 %copy-start.11 = (bf16[4,4096]{1,0:T(4,128)(2,1)S(1)}, bf16[4,4096]{1,0:T(4,128)(2,1)}, u32[]{:S(2)}) copy-start(bf16[4,4096]{1,0:T(4,128)(2,1)} %param.10) | copy-start | bytes 98308
  1.8 10.7 %copy-start.8 = (s32[4]{0:T(128)S(1)}, s32[4]{0:T(128)}, u32[]{:S(2)}) copy-start(s32[4]{0:T(128)} %rank_ref.1) | copy-start | bytes 52
  2.8 9.8 %all-to-all-start = ((f32[4,72,128]{2,1,0:T(8,128)}), f32[4,72,128]{2,1,0:T(8,128)S(1)}, u32[]{:S(2)}, u32[]{:S(2)}) async-start(f32[4,72,128]{2,1,0:T(8,128)} %gram.1), calls=%async_computation | async-start | bytes 294912 | tf_op jit(solution)/shard_map/all_to_all | solution.py:336
  9.8 26.0 %copy-start.7 = (s32[96]{0:T(128)S(1)}, s32[96]{0:T(128)}, u32[]{:S(2)}) copy-start(s32[96]{0:T(128)} %row_ref.1) | copy-start | bytes 1156
  14.1 1.0 %copy-start.4 = (bf16[64,72,128]{2,1,0:T(8,128)(2,1)}, bf16[64,72,128]{2,1,0:T(8,128)(2,1)S(1)}, u32[]{:S(2)}) copy-start(bf16[64,72,128]{2,1,0:T(8,128)(2,1)S(1)} %get-tuple-element.26) | copy-start | bytes 3538948
  15.2 44.9 %all-to-all-start.1 = ((bf16[64,72,128]{2,1,0:T(8,128)(2,1)}), bf16[64,72,128]{2,1,0:T(8,128)(2,1)S(1)}, u32[]{:S(2)}, u32[]{:S(2)}) async-start(bf16[64,72,128]{2,1,0:T(8,128)(2,1)} %copy-done.4), calls=%async_computation.1 | async-start | bytes 2359296 | tf_op jit(solution)/shard_map/all_to_all | solution.py:369
  31.5 40.5 %copy-start.9 = (s32[96,1]{0,1:T(1,128)S(1)}, s32[96,1]{0,1:T(1,128)}, u32[]{:S(2)}) copy-start(s32[96,1]{0,1:T(1,128)} %param.16) | copy-start | bytes 1156
  31.5 40.5 %copy-start.10 = (s32[96]{0:T(128)S(1)}, s32[96]{0:T(128)}, u32[]{:S(2)}) copy-start(s32[96]{0:T(128)} %column_ref.1) | copy-start | bytes 1156
  31.5 8.8 %collective-permute-start = (f32[32,128]{1,0:T(8,128)S(1)}, f32[32,128]{1,0:T(8,128)S(1)}, u32[]{:S(2)}, u32[]{:S(2)}) collective-permute-start(f32[32,128]{1,0:T(8,128)S(1)} %get-tuple-element.27.first_ref), channel_id=1, source_target_pairs={{0,4},{4,0},{8,12},{12,8},{16,20},{20,16},{24,28},{28,24},{32,36},... | collective-permute-start | bytes 49160 | tf_op jit(solution)/shard_map/ppermute | solution.py:370
  35.8 1.1 %copy-start.5 = (bf16[96,4096]{1,0:T(8,128)(2,1)S(1)}, bf16[96,4096]{1,0:T(8,128)(2,1)}, u32[]{:S(2)}) copy-start(bf16[96,4096]{1,0:T(8,128)(2,1)} %blocks_ref.1) | copy-start | bytes 2359300
  39.4 0.9 %copy-start.1 = (bf16[48,64,128]{2,1,0:T(8,128)(2,1)}, bf16[48,64,128]{2,1,0:T(8,128)(2,1)S(1)}, u32[]{:S(2)}) copy-start(bf16[48,64,128]{2,1,0:T(8,128)(2,1)S(1)} %get-tuple-element.25.rows_ref) | copy-start | bytes 2359300
  60.1 11.9 %collective-permute-start.1 = (bf16[64,72,128]{2,1,0:T(8,128)(2,1)S(1)}, bf16[64,72,128]{2,1,0:T(8,128)(2,1)}, u32[]{:S(2)}, u32[]{:S(2)}) collective-permute-start(bf16[64,72,128]{2,1,0:T(8,128)(2,1)S(1)} %all-to-all-done.1.own_ref.received_ref), channel_id=1, source_target_pairs={{0,4},{4,0},{8,12},{12,8},{16,20},{20,16},{24,28},{28,24},{32,36},... | collective-permute-start | bytes 3538952 | tf_op jit(solution)/shard_map/ppermute | solution.py:400
  66.7 1.1 %copy-start.2 = (bf16[48,64,128]{2,1,0:T(8,128)(2,1)S(1)}, bf16[48,64,128]{2,1,0:T(8,128)(2,1)}, u32[]{:S(2)}) copy-start(bf16[48,64,128]{2,1,0:T(8,128)(2,1)} %copy-done.1) | copy-start | bytes 2359300
  68.5 10.6 %all-to-all-start.2 = ((f32[8,8,128]{2,1,0:T(8,128)}), f32[8,8,128]{2,1,0:T(8,128)S(1)}, u32[]{:S(2)}, u32[]{:S(2)}) async-start(f32[8,8,128]{2,1,0:T(8,128)} %sum.1), calls=%async_computation.2 | async-start | bytes 65536 | tf_op jit(solution)/shard_map/all_to_all | solution.py:401
  72.0 1.1 %copy-start.3 = (bf16[48,64,128]{2,1,0:T(8,128)(2,1)S(1)}, bf16[48,64,128]{2,1,0:T(8,128)(2,1)}, u32[]{:S(2)}) copy-start(bf16[48,64,128]{2,1,0:T(8,128)(2,1)} %copy-done.1) | copy-start | bytes 2359300

commit v11 on v9

--- a/solution.py
+++ b/solution.py
@@ -184,11 +184,8 @@
         sent_ref[target, :width] = share_rows
         sent_ref[target, width:] = tiles[jnp.where(inside, height - 1, 0)].astype(BF16)
 
-    row = iota((width, width), 0)
-    even_first = jnp.where(row < half, 2 * row, 2 * row - width + 1)
-    order = (iota((width, width), 1) == even_first).astype(F32).astype(BF16)
     for node in range(nodes):
-        left_ref[node] = nt(nn(order, masked[node].astype(BF16)).astype(BF16), order).astype(BF16)
+        left_ref[node] = masked[node].astype(BF16)
 
 
 def sum_kernel(received_ref, out_ref):
@@ -215,13 +212,22 @@
         out_ref[:, tile * wide : (tile + 1) * wide] = natural[tile : tile + 1]
 
 
-def left_kernel(row_ref, blocks_ref, left_ref, out_ref, done_ref, spread):
+def left_kernel(row_ref, blocks_ref, masked_ref, out_ref, done_ref, spread, left_ref):
     step = pl.program_id(0)
     count, flat = blocks_ref.shape
-    width = left_ref.shape[1]
+    width = masked_ref.shape[1]
     wide = 2 * width
     tiles = flat // wide
     low = iota((width, wide), 1) < width
+
+    @pl.when(step == 0)
+    def _():
+        row = iota((width, width), 0)
+        even_first = jnp.where(row < tiles, 2 * row, 2 * row - width + 1)
+        order = (iota((width, width), 1) == even_first).astype(F32).astype(BF16)
+        for node in range(left_ref.shape[0]):
+            left_ref[node] = nt(nn(order, masked_ref[node]).astype(BF16), order).astype(BF16)
+
     for tile in range(tiles):
         spread[tile * count : (tile + 1) * count, :] = blocks_ref[:, tile * wide : (tile + 1) * wide].astype(F32)
     for index in range(0, count, 2):
@@ -380,7 +386,7 @@
                 pl.BlockSpec((nodes, width, width), lambda i, *_: (0, 0, 0)),
             ],
             out_specs=[square, pl.BlockSpec((8, wide), lambda i, *_: (0, 0))],
-            scratch_shapes=[pltpu.VMEM((ROWS * half, wide), F32)],
+            scratch_shapes=[pltpu.VMEM((ROWS * half, wide), F32), pltpu.VMEM((nodes, width, width), BF16)],
         ),
         compiler_params=SMALL,
         cost_estimate=pl.CostEstimate(

time: 79.2 us -> 79.1 us (level)
  transfers between devices with their start and end apart: 5 -> 5, of which waited for: 2 -> 2; matrix products, arithmetic and copies ran while one was open for 2% -> 2% of each run, Pallas kernels for 13% -> 14%
where the time goes in v11:
time: 79.1 us; the launch traced here: 78.6 us
  starting transfers between devices  35.3 us (45%)
  waiting for transfers between devices  21.4 us (27%)
  Pallas kernels  14.2 us (18%)
  local copies, waits for them, and re-layouts  6.83 us (9%)
  between operations  0.85 us (1%)
    all_to_all x1, waiting for transfers between devices, on_device(): own = lax.all_to_all(sent, 'branch', 0, 0, axis_index_groups=same_core)  19.4 us
    all_to_all x1, starting transfers between devices, on_device(): own = lax.all_to_all(sent, 'branch', 0, 0, axis_index_groups=same_core)  16.3 us
    ppermute x1, starting transfers between devices, on_device(): other = lax.ppermute(own, 'branch', partners)  6.56 us
    pallas_call x1, Pallas kernels, on_device(): pl.pallas_call(project_kernel, out_shape=[shape((blk, width * width), F32...  5.9 us
    unnamed x24, local copies, waits for them, and re-layouts  5.37 us
    all_to_all x1, starting transfers between devices, on_device(): gathered = lax.all_to_all(partial_sums, 'level', 0, 0)  4.84 us
    ppermute x1, starting transfers between devices, on_device(): first_other = lax.ppermute(first, 'branch', partners)  4.29 us
    all_to_all x1, starting transfers between devices, on_device(): lax.all_to_all(summed, ('branch', 'level'), 0, 0, axis_index_groups=same_...  3.27 us
  transfers between devices with their start and end apart: 5, of which 2 were waited for; matrix products, arithmetic and copies ran while one was open for 2% of the time, Pallas kernels for 14%

profile of v11, /device:TPU:1, one launch (start us, length us, event | category | flops | bytes accessed | tf_op | source)
XLA Modules:
  0.0 78.6 jit_solution(3650601389040901370)
XLA Ops:
  0.6 0.0 copy-start
  0.6 0.0 copy-start.5
  0.7 1.2 %copy-done.5 = bf16[4,64,1024]{2,1,0:T(8,128)(2,1)S(1)} copy-done((bf16[4,64,1024]{2,1,0:T(8,128)(2,1)S(1)}, bf16[4,64,1024]{2,1,0:T(8,128)(2,1)}, u32[]{:S(2)}) %copy-start.5) | copy-done | bytes 524312
  1.8 0.0 copy-start.10
  1.8 0.0 copy-start.11
  1.8 0.0 copy-start.9
  1.8 1.0 %gram.1 = f32[4,72,128]{2,1,0:T(8,128)} custom-call(bf16[4,64,1024]{2,1,0:T(8,128)(2,1)S(1)} %copy-done.5), custom_call_target="tpu_custom_call" | custom-call | tf_op jit(solution)/shard_map/gram/pallas_call | solution.py:331
  2.8 4.8 %all-to-all-start = ((f32[4,72,128]{2,1,0:T(8,128)}), f32[4,72,128]{2,1,0:T(8,128)S(1)}, u32[]{:S(2)}, u32[]{:S(2)}) async-start(f32[4,72,128]{2,1,0:T(8,128)} %gram.1), calls=%async_computation | async-start | bytes 294912 | tf_op jit(solution)/shard_map/all_to_all | solution.py:342
  7.7 0.0 copy-done
  7.7 0.6 gather_fusion.1
  8.3 0.1 gather.12
  8.4 0.0 copy-done.10
  8.4 0.6 gather_fusion
  9.1 0.1 broadcast_select_fusion.path_ref
  9.2 0.0 copy-start.6
  9.2 0.0 copy-done.11
  9.2 0.1 reshape.46.bottom_ref
  9.3 1.3 %path.1 = (bf16[7,64,64]{2,1,0:T(8,128)(2,1)S(1)}, bf16[7,64,64]{2,1,0:T(8,128)(2,1)S(1)}) custom-call(s32[7]{0:T(128)S(1)} %broadcast_select_fusion.1.rank_ref, bf16[7,64,64]{2,1,0:T(8,128)(2,1)S(1)} %broadcast_select_fusion.path_ref), custom_call_target="tpu_custom_call" | custom-call | tf_op jit(solution)/shard_map/path/pallas_call | solution.py:346
  10.7 1.9 %all-to-all-done.parts_ref = f32[4,72,128]{2,1,0:T(8,128)S(1)} async-done(((f32[4,72,128]{2,1,0:T(8,128)}), f32[4,72,128]{2,1,0:T(8,128)S(1)}, u32[]{:S(2)}, u32[]{:S(2)}) %all-to-all-start) | async-done | bytes 147488 | tf_op jit(solution)/shard_map/all_to_all | solution.py:342
  12.6 0.0 copy-done.9
  12.6 1.6 %near.1 = (bf16[4,64,64]{2,1,0:T(8,128)(2,1)S(1)}, bf16[64,72,128]{2,1,0:T(8,128)(2,1)S(1)}, f32[32,128]{1,0:T(8,128)S(1)}) custom-call(s32[4]{0:T(128)S(1)} %copy-done.9, s32[1]{0:T(128)} %bitcast.2.place_ref, s32[1]{0:T(128)} %bitcast.3.level_ref, f32[4,72,128]{2,1,0:T(8,128)S(1)} %all-to-all-done.parts_ref, bf16[4,64,64]{2,1,0:T(8,128)(2,1)S(1)} %reshape.46.bottom_ref, ...), custom_call_target="tpu_custom_call" | custom-call | tf_op jit(solution)/shard_map/near/pallas_call | solution.py:354
  14.1 0.0 copy-start.1
  14.1 1.0 %copy-done.1 = bf16[64,72,128]{2,1,0:T(8,128)(2,1)} copy-done((bf16[64,72,128]{2,1,0:T(8,128)(2,1)}, bf16[64,72,128]{2,1,0:T(8,128)(2,1)S(1)}, u32[]{:S(2)}) %copy-start.1) | copy-done | bytes 1179672
  15.2 16.3 %all-to-all-start.1 = ((bf16[64,72,128]{2,1,0:T(8,128)(2,1)}), bf16[64,72,128]{2,1,0:T(8,128)(2,1)S(1)}, u32[]{:S(2)}, u32[]{:S(2)}) async-start(bf16[64,72,128]{2,1,0:T(8,128)(2,1)} %copy-done.1), calls=%async_computation.1 | async-start | bytes 2359296 | tf_op jit(solution)/shard_map/all_to_all | solution.py:375
  31.5 0.0 copy-start.7
  31.5 0.0 copy-start.8
  31.5 4.3 %collective-permute-start = (f32[32,128]{1,0:T(8,128)S(1)}, f32[32,128]{1,0:T(8,128)S(1)}, u32[]{:S(2)}, u32[]{:S(2)}) collective-permute-start(f32[32,128]{1,0:T(8,128)S(1)} %get-tuple-element.28.first_ref), channel_id=1, source_target_pairs={{0,4},{4,0},{8,12},{12,8},{16,20},{20,16},{24,28},{28,24},{32,36},... | collective-permute-start | bytes 49160 | tf_op jit(solution)/shard_map/ppermute | solution.py:376
  35.8 0.0 copy-done.6
  35.8 0.0 copy-start.2
  35.8 1.1 %copy-done.2 = bf16[96,4096]{1,0:T(8,128)(2,1)S(1)} copy-done((bf16[96,4096]{1,0:T(8,128)(2,1)S(1)}, bf16[96,4096]{1,0:T(8,128)(2,1)}, u32[]{:S(2)}) %copy-start.2) | copy-done | bytes 786456
  36.9 2.8 %left.1 = (bf16[48,64,128]{2,1,0:T(8,128)(2,1)S(1)}, f32[8,128]{1,0:T(8,128)S(1)}) custom-call(s32[96]{0:T(128)S(1)} %copy-done.6, bf16[96,4096]{1,0:T(8,128)(2,1)S(1)} %copy-done.2, bf16[4,64,64]{2,1,0:T(8,128)(2,1)S(1)} %get-tuple-element.25.masked_ref), custom_call_target="tpu_custom_call" | custom-call | flops 100663296 | bytes 1572864 | tf_op jit(solution)/shard_map/left/pallas_call | solution.py:378
  39.8 0.0 copy-start.3
  39.8 0.9 %copy-done.3 = bf16[48,64,128]{2,1,0:T(8,128)(2,1)} copy-done((bf16[48,64,128]{2,1,0:T(8,128)(2,1)}, bf16[48,64,128]{2,1,0:T(8,128)(2,1)S(1)}, u32[]{:S(2)}) %copy-start.3) | copy-done | bytes 786456
  40.7 0.0 collective-permute-done.other_ref
  40.7 19.4 %all-to-all-done.1.own_ref.received_ref = bf16[64,72,128]{2,1,0:T(8,128)(2,1)S(1)} async-done(((bf16[64,72,128]{2,1,0:T(8,128)(2,1)}), bf16[64,72,128]{2,1,0:T(8,128)(2,1)S(1)}, u32[]{:S(2)}, u32[]{:S(2)}) %all-to-all-start.1) | async-done | bytes 1179680 | tf_op jit(solution)/shard_map/all_to_all | solution.py:375
  60.1 6.6 %collective-permute-start.1 = (bf16[64,72,128]{2,1,0:T(8,128)(2,1)S(1)}, bf16[64,72,128]{2,1,0:T(8,128)(2,1)}, u32[]{:S(2)}, u32[]{:S(2)}) collective-permute-start(bf16[64,72,128]{2,1,0:T(8,128)(2,1)S(1)} %all-to-all-done.1.own_ref.received_ref), channel_id=1, source_target_pairs={{0,4},{4,0},{8,12},{12,8},{16,20},{20,16},{24,28},{28,24},{32,36},... | collective-permute-start | bytes 3538952 | tf_op jit(solution)/shard_map/ppermute | solution.py:406
  66.7 0.7 sum.1
  67.3 3.3 %all-to-all-start.2 = ((f32[8,8,128]{2,1,0:T(8,128)}), f32[8,8,128]{2,1,0:T(8,128)S(1)}, u32[]{:S(2)}, u32[]{:S(2)}) async-start(f32[8,8,128]{2,1,0:T(8,128)} %sum.1), calls=%async_computation.2 | async-start | bytes 65536 | tf_op jit(solution)/shard_map/all_to_all | solution.py:407
  70.6 0.0 collective-permute-done.1.other_ref
  70.6 0.0 copy-done.7
  70.6 0.0 copy-done.8
  70.7 0.0 copy-start.4
  70.7 1.1 %copy-done.4 = bf16[48,64,128]{2,1,0:T(8,128)(2,1)S(1)} copy-done((bf16[48,64,128]{2,1,0:T(8,128)(2,1)S(1)}, bf16[48,64,128]{2,1,0:T(8,128)(2,1)}, u32[]{:S(2)}) %copy-start.4) | copy-done | bytes 786456
  71.8 5.9 %project.1 = (f32[96,4096]{1,0:T(8,128)}, bf16[48,64,128]{2,1,0:T(8,128)(2,1)S(1)}) custom-call(s32[96]{0:T(128)S(1)} %bitcast.6, s32[96]{0:T(128)S(1)} %copy-done.8, s32[1]{0:T(128)} %bitcast.core_ref, bf16[48,64,128]{2,1,0:T(8,128)(2,1)S(1)} %copy-done.4, ...), custom_call_target="tpu_custom_call", output_to_operand_aliasing={{1}: (3, {})} | custom-call | flops 201326592 | bytes 2359296 | tf_op jit(solution)/shard_map/project/pallas_call | solution.py:410
  77.7 0.0 all-to-all-done.2.received_ref
  77.7 0.9 %top.1 = f32[1,4096]{1,0:T(1,128)} custom-call(s32[1]{0:T(128)} %bitcast.core_ref, f32[8,8,128]{2,1,0:T(8,128)S(1)} %all-to-all-done.2.received_ref, f32[32,128]{1,0:T(8,128)S(1)} %get-tuple-element.28.first_ref, f32[32,128]{1,0:T(8,128)S(1)} %collective-permute-done.other_ref, f32[8,128]{1,0:T(8,128)S(1)} %get-tuple-element.34.done_ref), custom_call_target="tpu_custom_call" | custom-call | tf_op jit(solution)/shard_map/top/pallas_call | solution.py:434
  (4 shorter events, 0.0 us)
Async XLA Ops:
  0.6 7.1 %copy-start = (bf16[254,4096]{1,0:T(8,128)(2,1)S(1)}, bf16[254,4096]{1,0:T(8,128)(2,1)}, u32[]{:S(2)}) copy-start(bf16[254,4096]{1,0:T(8,128)(2,1)} %param.12) | copy-start | bytes 6242308
  0.6 1.2 %copy-start.5 = (bf16[4,64,1024]{2,1,0:T(8,128)(2,1)S(1)}, bf16[4,64,1024]{2,1,0:T(8,128)(2,1)}, u32[]{:S(2)}) copy-start(bf16[4,64,1024]{2,1,0:T(8,128)(2,1)} %basis_ref.1) | copy-start | bytes 1572868
  1.8 6.6 %copy-start.10 = (s32[254]{0:T(256)S(1)}, s32[254]{0:T(256)}, u32[]{:S(2)}) copy-start(s32[254]{0:T(256)} %param.13) | copy-start | bytes 3052
  1.8 7.3 %copy-start.11 = (bf16[4,4096]{1,0:T(4,128)(2,1)S(1)}, bf16[4,4096]{1,0:T(4,128)(2,1)}, u32[]{:S(2)}) copy-start(bf16[4,4096]{1,0:T(4,128)(2,1)} %param.10) | copy-start | bytes 98308
  1.8 10.7 %copy-start.9 = (s32[4]{0:T(128)S(1)}, s32[4]{0:T(128)}, u32[]{:S(2)}) copy-start(s32[4]{0:T(128)} %rank_ref.1) | copy-start | bytes 52
  2.8 9.8 %all-to-all-start = ((f32[4,72,128]{2,1,0:T(8,128)}), f32[4,72,128]{2,1,0:T(8,128)S(1)}, u32[]{:S(2)}, u32[]{:S(2)}) async-start(f32[4,72,128]{2,1,0:T(8,128)} %gram.1), calls=%async_computation | async-start | bytes 294912 | tf_op jit(solution)/shard_map/all_to_all | solution.py:342
  9.2 26.6 %copy-start.6 = (s32[96]{0:T(128)S(1)}, s32[96]{0:T(128)}, u32[]{:S(2)}) copy-start(s32[96]{0:T(128)} %row_ref.1) | copy-start | bytes 1156
  14.1 1.0 %copy-start.1 = (bf16[64,72,128]{2,1,0:T(8,128)(2,1)}, bf16[64,72,128]{2,1,0:T(8,128)(2,1)S(1)}, u32[]{:S(2)}) copy-start(bf16[64,72,128]{2,1,0:T(8,128)(2,1)S(1)} %get-tuple-element.27) | copy-start | bytes 3538948
  15.2 44.9 %all-to-all-start.1 = ((bf16[64,72,128]{2,1,0:T(8,128)(2,1)}), bf16[64,72,128]{2,1,0:T(8,128)(2,1)S(1)}, u32[]{:S(2)}, u32[]{:S(2)}) async-start(bf16[64,72,128]{2,1,0:T(8,128)(2,1)} %copy-done.1), calls=%async_computation.1 | async-start | bytes 2359296 | tf_op jit(solution)/shard_map/all_to_all | solution.py:375
  31.5 39.2 %copy-start.7 = (s32[96,1]{0,1:T(1,128)S(1)}, s32[96,1]{0,1:T(1,128)}, u32[]{:S(2)}) copy-start(s32[96,1]{0,1:T(1,128)} %param.16) | copy-start | bytes 1156
  31.5 39.2 %copy-start.8 = (s32[96]{0:T(128)S(1)}, s32[96]{0:T(128)}, u32[]{:S(2)}) copy-start(s32[96]{0:T(128)} %column_ref.1) | copy-start | bytes 1156
  31.5 9.2 %collective-permute-start = (f32[32,128]{1,0:T(8,128)S(1)}, f32[32,128]{1,0:T(8,128)S(1)}, u32[]{:S(2)}, u32[]{:S(2)}) collective-permute-start(f32[32,128]{1,0:T(8,128)S(1)} %get-tuple-element.28.first_ref), channel_id=1, source_target_pairs={{0,4},{4,0},{8,12},{12,8},{16,20},{20,16},{24,28},{28,24},{32,36},... | collective-permute-start | bytes 49160 | tf_op jit(solution)/shard_map/ppermute | solution.py:376
  35.8 1.1 %copy-start.2 = (bf16[96,4096]{1,0:T(8,128)(2,1)S(1)}, bf16[96,4096]{1,0:T(8,128)(2,1)}, u32[]{:S(2)}) copy-start(bf16[96,4096]{1,0:T(8,128)(2,1)} %blocks_ref.1) | copy-start | bytes 2359300
  39.8 0.9 %copy-start.3 = (bf16[48,64,128]{2,1,0:T(8,128)(2,1)}, bf16[48,64,128]{2,1,0:T(8,128)(2,1)S(1)}, u32[]{:S(2)}) copy-start(bf16[48,64,128]{2,1,0:T(8,128)(2,1)S(1)} %get-tuple-element.26.rows_ref) | copy-start | bytes 2359300
  60.1 10.5 %collective-permute-start.1 = (bf16[64,72,128]{2,1,0:T(8,128)(2,1)S(1)}, bf16[64,72,128]{2,1,0:T(8,128)(2,1)}, u32[]{:S(2)}, u32[]{:S(2)}) collective-permute-start(bf16[64,72,128]{2,1,0:T(8,128)(2,1)S(1)} %all-to-all-done.1.own_ref.received_ref), channel_id=1, source_target_pairs={{0,4},{4,0},{8,12},{12,8},{16,20},{20,16},{24,28},{28,24},{32,36},... | collective-permute-start | bytes 3538952 | tf_op jit(solution)/shard_map/ppermute | solution.py:406
  67.3 10.3 %all-to-all-start.2 = ((f32[8,8,128]{2,1,0:T(8,128)}), f32[8,8,128]{2,1,0:T(8,128)S(1)}, u32[]{:S(2)}, u32[]{:S(2)}) async-start(f32[8,8,128]{2,1,0:T(8,128)} %sum.1), calls=%async_computation.2 | async-start | bytes 65536 | tf_op jit(solution)/shard_map/all_to_all | solution.py:407
  70.7 1.1 %copy-start.4 = (bf16[48,64,128]{2,1,0:T(8,128)(2,1)S(1)}, bf16[48,64,128]{2,1,0:T(8,128)(2,1)}, u32[]{:S(2)}) copy-start(bf16[48,64,128]{2,1,0:T(8,128)(2,1)} %copy-done.3) | copy-start | bytes 2359300
